TPU v7x, 256 devices: a whole 4x4x8 slice. The times are simulated.
256 devices in a mesh: row: 8 (over z_lo, y), col: 32 (over z_hi, x, core).
Axes of the slice: x: 4, y: 4, z: 8 (z_hi: 4, z_lo: 2; z = z_hi * 2 + z_lo), core: 2. Of those that a mesh axis runs over, the one named last changes fastest.
Arguments:
- eigvecs: float32 [32768, 4096], P(('row', 'col')), may hold values from -6 to 6
- householder: float32 [5, 32768, 256], P(None, 'row', 'col'), may hold values from -0.375 to 0.375
- tfactor: float32 [5, 256, 256], replicated, may hold values from -0.02 to 0.03, as said below
Outputs:
- transformed: float32 [32768, 4096], P('row', 'col')
Inputs may be any that keep to these rules, and one draw needn't show every extreme that they name: tfactor[b] is upper triangular with a positive diagonal.
All inputs are finite; a program needn't handle non-finite values.
Results may differ from a plain program's by a relative error of at most 0.0001.
Values sent between devices are 32-bit elements; how exact they have to be, the bound alone decides.
No kernel may reach another device: no remote copies, remote signals or barrier semaphores. Data moves between devices by JAX's collectives and lax.ppermute only.
A program may use at most 128 MiB of HBM per device.

v0:
```python
import functools

import jax
import jax.numpy as jnp
from jax import lax
from jax.experimental import pallas as pl
from jax.experimental.pallas import tpu as pltpu
from jax.sharding import Mesh
from jax.sharding import PartitionSpec as P

AXES = ("zl", "y", "zh", "x", "core")
SIZES = (2, 4, 4, 4, 2)
ROW, COL = ("zl", "y"), ("zh", "x", "core")
RING = 4
ROWS = 4096
NB = 256
K = 128
STEP = 512
HIGHEST = lax.Precision.HIGHEST


def tie(a, *events):
    return lax.optimization_barrier((a, *events))[0] if events else a


def shift(a, axis, by):
    n = SIZES[AXES.index(axis)]
    return lax.ppermute(a, axis, [(i, (i + by) % n) for i in range(n)])


def both_ways(a, axis):
    pairs = []
    for i in range(RING):
        pairs.append((i * 2, ((i + 1) % RING) * 2))
        pairs.append((i * 2 + 1, ((i - 1) % RING) * 2 + 1))
    return lax.ppermute(a, (axis, "core"), pairs)


def swap(a):
    return shift(a, "core", 1)


def gather_x(full, before=(), between=()):
    half = full.shape[0] // 2
    near = both_ways(tie(full, *before), "x")
    far = both_ways(tie(near[:half], *between), "x")
    return (full, near, far, swap(near), swap(far))


def chunks(n, i):
    return (i, n + i, 2 * n + i, 3 * n + i, 4 * n + i, 5 * n + i, 6 * n + i, 7 * n + i)


def column_order():
    x, c = lax.axis_index("x"), lax.axis_index("core")
    s = 1 - 2 * c
    order = [(x, c), (x, 1 - c), (x - s, c), (x - s, 1 - c), (x + 2, c)]
    order += [(x + s, 1 - c), (x + s, c), (x + 2, 1 - c)]
    unit = jnp.stack([(z * 4 + xx % 4) * 2 + cc for xx, cc in order for z in range(4)])
    return (unit[:, None] * 8 + jnp.arange(8)[None, :]).reshape(NB)


def exchange(eigvecs):
    return lax.all_to_all(eigvecs.T.reshape(32, K, 128), COL, split_axis=0, concat_axis=0, tiled=True)


def row_sum(a):
    n, width = a.shape
    a = lax.all_to_all(a.reshape(8, n // 8, width), ROW, split_axis=0, concat_axis=0, tiled=True)
    a = jnp.broadcast_to(jnp.sum(a, 0), a.shape)
    return lax.all_to_all(a, ROW, split_axis=0, concat_axis=0, tiled=True).reshape(n, width)


def split(a):
    hi = a.astype(jnp.bfloat16)
    return hi, (a - hi.astype(jnp.float32)).astype(jnp.bfloat16)


def dot(a, b, dims):
    return lax.dot_general(a, b, (dims, ((), ())), preferred_element_type=jnp.float32)


def product(a, b, dims):
    (ah, al), (bh, bl) = a, b
    return dot(ah, bh, dims) + (dot(ah, bl, dims) + dot(al, bh, dims))


NT = ((1,), (1,))
NN = ((1,), (0,))


def stacked(refs):
    return jnp.concatenate([r[...] for r in refs], 0)


def work_kernel(has_old, has_new, *refs):
    cur_ref, refs = refs[0], refs[1:]
    cur = cur_ref[...] if len(cur_ref.shape) == 2 else jnp.concatenate([cur_ref[i] for i in range(STEP // 128)], 1)
    if has_old:
        applied, old, refs = split(refs[0][...]), split(stacked(refs[1:6])), refs[6:]
        cur = cur - product(applied, old, NN)
    if not has_new:
        refs[0][...] = cur.T
        return
    new, refs = split(stacked(refs[:5])), refs[5:]
    if has_old:
        refs[0][...] = cur
        refs = refs[1:]
    w_ref = refs[0]
    part = product(new, split(cur), NT)

    @pl.when(pl.program_id(0) == 0)
    def _():
        w_ref[...] = part

    @pl.when(pl.program_id(0) != 0)
    def _():
        w_ref[...] += part


def piece_specs(pieces):
    return [pl.BlockSpec((p.shape[0], STEP), lambda i: (0, i)) for p in pieces]


def rows_of(pieces):
    return sum(p.shape[0] for p in pieces)


def work(cur, applied, old, new):
    args, specs = [cur], [pl.BlockSpec((K, STEP), lambda i: (0, i))]
    if cur.ndim == 3:
        specs = [pl.BlockSpec((STEP // 128, K, 128), lambda i: (i, 0, 0))]
    if old:
        args += [applied, *old]
        specs += [pl.BlockSpec(applied.shape, lambda i: (0, 0))] + piece_specs(old)
    args += new
    specs += piece_specs(new)
    shapes, outs = [], []
    if not new:
        shapes.append(jax.ShapeDtypeStruct((ROWS, K), jnp.float32))
        outs.append(pl.BlockSpec((STEP, K), lambda i: (i, 0)))
    elif old:
        shapes.append(jax.ShapeDtypeStruct((K, ROWS), jnp.float32))
        outs.append(pl.BlockSpec((K, STEP), lambda i: (0, i)))
    if new:
        shapes.append(jax.ShapeDtypeStruct((rows_of(new), K), jnp.float32))
        outs.append(pl.BlockSpec((rows_of(new), K), lambda i: (0, 0)))
    n = rows_of(old) + rows_of(new)
    return pl.pallas_call(
        functools.partial(work_kernel, bool(old), bool(new)),
        grid=(ROWS // STEP,),
        in_specs=specs,
        out_specs=outs,
        out_shape=shapes,
        compiler_params=pltpu.CompilerParams(vmem_limit_bytes=40 << 20),
        cost_estimate=pl.CostEstimate(
            flops=6 * n * K * ROWS, bytes_accessed=4 * ROWS * (n + 2 * K), transcendentals=0
        ),
        name="work",
    )(*args)


def block_of(a, i, n):
    return jnp.concatenate([a[32 * k : 32 * k + 32] for k in chunks(n, i)], 0)


def overlap_kernel(*refs):
    g_ref = refs[-1]
    both = stacked(refs[:5])
    part = product(split(block_of(both, 1, 2)), split(block_of(both, 0, 2)), NT)

    @pl.when(pl.program_id(0) == 0)
    def _():
        g_ref[...] = part

    @pl.when(pl.program_id(0) != 0)
    def _():
        g_ref[...] += part


def overlap(pieces):
    return pl.pallas_call(
        overlap_kernel,
        grid=(ROWS // STEP,),
        in_specs=piece_specs(pieces),
        out_specs=pl.BlockSpec((NB, NB), lambda i: (0, 0)),
        out_shape=jax.ShapeDtypeStruct((NB, NB), jnp.float32),
        compiler_params=pltpu.CompilerParams(vmem_limit_bytes=40 << 20),
        cost_estimate=pl.CostEstimate(
            flops=6 * NB * NB * ROWS, bytes_accessed=8 * ROWS * NB, transcendentals=0
        ),
        name="overlap",
    )(*pieces)


def exact(a, b):
    return lax.dot_general(a, b, (NN, ((), ())), precision=HIGHEST, preferred_element_type=jnp.float32)


def solve_kernel(n, *refs):
    t_ref, w_ref, out = refs[0], refs[1], refs[-1]
    w = w_ref[...]
    done = [exact(t_ref[0], block_of(w, 0, n))]
    if n == 2:
        done.append(exact(t_ref[1], block_of(w, 1, n) - exact(refs[2][...], done[0])))
    laid = sorted((k, i, j) for i in range(n) for j, k in enumerate(chunks(n, i)))
    out[...] = jnp.concatenate([done[i][32 * j : 32 * j + 32] for _, i, j in laid], 0).T


def solve(t, w, *g):
    n = t.shape[0]
    return pl.pallas_call(
        functools.partial(solve_kernel, n),
        out_shape=jax.ShapeDtypeStruct((K, NB * n), jnp.float32),
        cost_estimate=pl.CostEstimate(flops=12 * n * NB * NB * K, bytes_accessed=1 << 20, transcendentals=0),
        compiler_params=pltpu.CompilerParams(vmem_limit_bytes=24 << 20),
        name="solve",
    )(t, w, *g)


def on_device(eigvecs, householder, tfactor):
    v = jnp.swapaxes(householder, 1, 2)

    def gather_z(blocks):
        mine = jnp.stack([v[b] for b in blocks])
        return lax.all_gather(mine, "zh", axis=1).reshape(32 * len(blocks), ROWS)

    def full(half):
        return jnp.concatenate([half, swap(half)], 0)

    first, rest = gather_z((4, 3)), gather_z((2, 1, 0))
    pick = (column_order()[:, None] == jnp.arange(NB)[None, :]).astype(jnp.float32)
    t = jnp.einsum("ij,bjk,lk->bil", pick, tfactor, pick, precision=HIGHEST)
    ts = [jnp.stack([t[b] for b in group]) for group in ((4, 3), (2, 1), (0,))]

    cur = exchange(eigvecs)
    pieces = [gather_x(full(first), (cur,))]
    pieces.append(gather_x(full(rest[:64]), (pieces[0][1],), (pieces[0][2],)))
    pieces.append(gather_x(full(rest[64:]), (pieces[1][1],), (pieces[1][2],)))

    applied, old, g = None, (), [row_sum(overlap(pieces[0]))]
    for group, new in enumerate(pieces):
        res = work(cur, applied, old, new)
        if old:
            cur, w = res
        else:
            (w,) = res
        w = row_sum(w)
        after = [overlap(pieces[1])] if group == 0 else []
        applied = solve(ts[group], tie(w, *after), *g)
        old, g = new, [row_sum(a) for a in after]
    return work(cur, applied, old, ())[0]


def solution(mesh):
    fine = Mesh(mesh.devices.reshape(SIZES), AXES)
    placed = (P(ROW + COL, None), P(None, ROW, COL), P())
    return jax.shard_map(on_device, mesh=fine, in_specs=placed, out_specs=P(ROW, COL), check_vma=False)
```

profile of v0, /device:TPU:32, one launch (start us, length us, event | category | flops | bytes accessed | tf_op | source)
XLA Modules:
  0.0 340.0 jit_solution(2458928892431974471)
XLA Ops:
  6.5 3.0 copy.5
  9.5 10.7 %all-to-all-start = ((f32[32,128,128]{2,1,0:T(8,128)}), f32[32,128,128]{2,1,0:T(8,128)}, u32[]{:S(2)}, u32[]{:S(2)}) async-start(f32[32,128,128]{2,1,0:T(8,128)} %bitcast.1), calls=%async_computation | async-start | bytes 4194304 | tf_op jit(solution)/shard_map/all_to_all | solution.py:64
  21.1 66.2 %all-gather.5.cloned.1.call-done = f32[2,32,4096]{2,1,0:T(8,128)} async-done(((f32[2,8,4096]{2,1,0:T(8,128)}), f32[2,32,4096]{2,1,0:T(8,128)}) %all-gather.5.cloned.1.call-update) | async-done | bytes 1048592 | tf_op jit(solution)/shard_map/all_gather | solution.py:226
  88.2 2.1 collective-permute-done
  90.3 1.7 pad_maximum_fusion.refs_1_.refs_0_.refs_2_
  92.1 1.6 collective-permute-start.1
  93.6 34.4 %all-gather.7.cloned.1.call-done = f32[3,32,4096]{2,1,0:T(8,128)} async-done(((f32[3,8,4096]{2,1,0:T(8,128)}), f32[3,32,4096]{2,1,0:T(8,128)}) %all-gather.7.cloned.1.call-update) | async-done | bytes 1572880 | tf_op jit(solution)/shard_map/all_gather | solution.py:226
  128.0 1.3 slice.78
  129.4 1.3 slice.74
  130.7 2.4 collective-permute-start.2
  133.1 1.4 collective-permute-start.3
  134.8 12.4 %collective-permute-done.2.refs_3_.refs_2_.refs_4_ = f32[64,4096]{1,0:T(8,128)} collective-permute-done((f32[64,4096]{1,0:T(8,128)S(1)}, f32[64,4096]{1,0:T(8,128)}, u32[]{:S(2)}, u32[]{:S(2)}) %collective-permute-start.2) | collective-permute-done | bytes 1048608 | tf_op jit(solution)/shard_map/ppermute | solution.py:36
  147.3 2.9 collective-permute-done.4.refs_5_.refs_4_.refs_6_
  150.2 1.6 copy-done.4
  151.7 8.1 %work.4 = f32[512,128]{1,0:T(8,128)S(1)} custom-call(f32[32,128,128]{2,1,0:T(8,128)} %all-to-all-done.refs_0_, f32[128,4096]{1,0:T(8,128)S(1)} %copy-done.4, f32[128,4096]{1,0:T(8,128)} %collective-permute-done.1.refs_2_.refs_1_.refs_3_, f32[64,4096]{1,0:T(8,128)} %collective-permute-done.2.refs_3_.refs_2_.refs_4_, ...), custom_call_target="tpu_custom_call" | custom-call | flops 1610612736 | bytes 12582912 | tf_op jit(solution)/shard_map/work/pallas_call | solution.py:149
  160.6 7.8 %all-to-all-start.1 = ((f32[8,64,128]{2,1,0:T(8,128)}), f32[8,64,128]{2,1,0:T(8,128)}, u32[]{:S(2)}, u32[]{:S(2)}) async-start(f32[8,64,128]{2,1,0:T(8,128)} %bitcast.58), calls=%async_computation.1 | async-start | bytes 524288 | tf_op jit(solution)/shard_map/all_to_all | solution.py:69
  168.5 2.0 convolution_bitcast_fusion
  170.5 2.3 slice.79
  174.2 7.0 %overlap.3 = f32[256,256]{1,0:T(8,128)S(1)} custom-call(f32[128,4096]{1,0:T(8,128)S(1)} %copy-done.5, f32[128,4096]{1,0:T(8,128)} %collective-permute-done.1.refs_2_.refs_1_.refs_3_, f32[64,4096]{1,0:T(8,128)} %collective-permute-done.2.refs_3_.refs_2_.refs_4_, f32[128,4096]{1,0:T(8,128)} %collective-permute-done.3.refs_4_.refs_3_.refs_5_, ...), custom_call_target="tpu_custom_call" | custom-call | flops 1610612736 | bytes 8388608 | tf_op jit(solution)/shard_map/overlap/pallas_call | solution.py:182
  181.9 7.4 %all-to-all-start.3 = ((f32[8,32,256]{2,1,0:T(8,128)}), f32[8,32,256]{2,1,0:T(8,128)}, u32[]{:S(2)}, u32[]{:S(2)}) async-start(f32[8,32,256]{2,1,0:T(8,128)} %bitcast.57), calls=%async_computation.3 | async-start | bytes 524288 | tf_op jit(solution)/shard_map/all_to_all | solution.py:69
  189.3 1.9 slice_bitcast_fusion
  192.8 2.7 all-to-all-done.3
  196.2 5.3 %all-to-all-start.2 = ((f32[8,64,128]{2,1,0:T(8,128)}), f32[8,64,128]{2,1,0:T(8,128)}, u32[]{:S(2)}, u32[]{:S(2)}) async-start(f32[8,64,128]{2,1,0:T(8,128)} %broadcast_in_dim.18), calls=%async_computation.2 | async-start | bytes 524288 | tf_op jit(solution)/shard_map/all_to_all | solution.py:71
  201.6 2.1 fusion.1
  208.2 5.3 %all-to-all-start.4 = ((f32[8,32,256]{2,1,0:T(8,128)}), f32[8,32,256]{2,1,0:T(8,128)}, u32[]{:S(2)}, u32[]{:S(2)}) async-start(f32[8,32,256]{2,1,0:T(8,128)} %broadcast_in_dim.19), calls=%async_computation.4 | async-start | bytes 524288 | tf_op jit(solution)/shard_map/all_to_all | solution.py:71
  213.6 2.2 pad_maximum_fusion.2.refs_7_.refs_2_
  215.9 7.7 %overlap.2 = f32[256,256]{1,0:T(8,128)} custom-call(f32[128,4096]{1,0:T(8,128)S(1)} %pad_maximum_fusion.1.refs_0_.refs_7_.refs_2_, f32[128,4096]{1,0:T(8,128)} %collective-permute-done.6.refs_1_.refs_8_.refs_3_, f32[64,4096]{1,0:T(8,128)} %collective-permute-done.7.refs_2_.refs_9_.refs_4_, f32[128,4096]{1,0:T(8,128)} %collective-permute-done.8.refs_3_.refs_10_.refs_5_, ...), custom_call_target="tpu_custom_call" | custom-call | flops 1610612736 | bytes 8388608 | tf_op jit(solution)/shard_map/overlap/pallas_call | solution.py:182
  224.7 2.5 solve.3.refs_1_
  227.2 1.6 copy-done.6
  228.8 11.4 %work.5 = (f32[128,4096]{1,0:T(8,128)S(1)}, f32[512,128]{1,0:T(8,128)S(1)}) custom-call(f32[32,128,128]{2,1,0:T(8,128)} %all-to-all-done.refs_0_, f32[128,512]{1,0:T(8,128)S(1)} %solve.3.refs_1_, f32[128,4096]{1,0:T(8,128)S(1)} %copy-done.6, f32[128,4096]{1,0:T(8,128)} %collective-permute-done.1.refs_2_.refs_1_.refs_3_, ...), custom_call_target="tpu_custom_call" | custom-call | flops 3221225472 | bytes 20971520 | tf_op jit(solution)/shard_map/work/pallas_call | solution.py:149
  240.3 1.3 copy-done.7
  241.6 11.3 %all_to_all.55 = f32[8,64,128]{2,1,0:T(8,128)S(1)} all-to-all(f32[8,64,128]{2,1,0:T(8,128)S(1)} %bitcast.60), channel_id=1, replica_groups=mesh['zl'=2,'y'=4,'zh'=4,'x'=4,'core'=2] {'zl','y'}, dimensions={0} | all-to-all | bytes 524288 | tf_op jit(solution)/shard_map/all_to_all | solution.py:69
  252.9 5.3 %all-to-all-start.7 = ((f32[8,32,256]{2,1,0:T(8,128)}), f32[8,32,256]{2,1,0:T(8,128)}, u32[]{:S(2)}, u32[]{:S(2)}) async-start(f32[8,32,256]{2,1,0:T(8,128)} %bitcast.45), calls=%async_computation.7 | async-start | bytes 524288 | tf_op jit(solution)/shard_map/all_to_all | solution.py:69
  258.3 1.9 slice.83
  261.4 2.9 all-to-all-done.7
  264.9 5.3 %all-to-all-start.6 = ((f32[8,64,128]{2,1,0:T(8,128)}), f32[8,64,128]{2,1,0:T(8,128)}, u32[]{:S(2)}, u32[]{:S(2)}) async-start(f32[8,64,128]{2,1,0:T(8,128)} %broadcast_in_dim.20), calls=%async_computation.6 | async-start | bytes 524288 | tf_op jit(solution)/shard_map/all_to_all | solution.py:71
  271.8 4.4 %all-to-all-done.6 = f32[8,64,128]{2,1,0:T(8,128)} async-done(((f32[8,64,128]{2,1,0:T(8,128)}), f32[8,64,128]{2,1,0:T(8,128)}, u32[]{:S(2)}, u32[]{:S(2)}) %all-to-all-start.6) | async-done | bytes 262176 | tf_op jit(solution)/shard_map/all_to_all | solution.py:71
  276.9 5.3 %all-to-all-start.8 = ((f32[8,32,256]{2,1,0:T(8,128)}), f32[8,32,256]{2,1,0:T(8,128)}, u32[]{:S(2)}, u32[]{:S(2)}) async-start(f32[8,32,256]{2,1,0:T(8,128)} %broadcast_in_dim.21), calls=%async_computation.8 | async-start | bytes 524288 | tf_op jit(solution)/shard_map/all_to_all | solution.py:71
  282.3 1.8 pad_maximum_fusion.4.refs_0_
  284.1 4.1 %all-to-all-done.8 = f32[8,32,256]{2,1,0:T(8,128)} async-done(((f32[8,32,256]{2,1,0:T(8,128)}), f32[8,32,256]{2,1,0:T(8,128)}, u32[]{:S(2)}, u32[]{:S(2)}) %all-to-all-start.8) | async-done | bytes 262176 | tf_op jit(solution)/shard_map/all_to_all | solution.py:71
  289.3 2.5 solve.4.refs_1_
  291.8 1.6 copy-done.8
  293.4 9.6 %work.6 = (f32[128,4096]{1,0:T(8,128)S(1)}, f32[256,128]{1,0:T(8,128)S(1)}) custom-call(f32[128,4096]{1,0:T(8,128)S(1)} %copy-done.8, f32[128,512]{1,0:T(8,128)S(1)} %solve.4.refs_1_, f32[128,4096]{1,0:T(8,128)S(1)} %copy-done.2, f32[128,4096]{1,0:T(8,128)} %collective-permute-done.6.refs_1_.refs_8_.refs_3_, ...), custom_call_target="tpu_custom_call" | custom-call | flops 2415919104 | bytes 16777216 | tf_op jit(solution)/shard_map/work/pallas_call | solution.py:149
  303.0 1.3 copy-done.11
  304.4 9.2 %all_to_all.56 = f32[8,32,128]{2,1,0:T(8,128)S(1)} all-to-all(f32[8,32,128]{2,1,0:T(8,128)S(1)} %bitcast.61), channel_id=1, replica_groups=mesh['zl'=2,'y'=4,'zh'=4,'x'=4,'core'=2] {'zl','y'}, dimensions={0} | all-to-all | bytes 262144 | tf_op jit(solution)/shard_map/all_to_all | solution.py:69
  313.6 9.1 %all_to_all.57 = f32[8,32,128]{2,1,0:T(8,128)S(1)} all-to-all(f32[8,32,128]{2,1,0:T(8,128)S(1)} %broadcast_in_dim.22), channel_id=1, replica_groups=mesh['zl'=2,'y'=4,'zh'=4,'x'=4,'core'=2] {'zl','y'}, dimensions={0} | all-to-all | bytes 262144 | tf_op jit(solution)/shard_map/all_to_all | solution.py:71
  324.1 1.6 copy-done.12
  325.7 7.5 %work.7 = f32[4096,128]{1,0:T(8,128)} custom-call(f32[128,4096]{1,0:T(8,128)S(1)} %copy-done.12, f32[128,256]{1,0:T(8,128)S(1)} %solve.5.refs_1_, f32[64,4096]{1,0:T(8,128)} %pad_maximum_fusion.2.refs_7_.refs_2_, f32[64,4096]{1,0:T(8,128)} %collective-permute-done.11.refs_8_.refs_3_, f32[32,4096]{1,0:T(8,128)} %collective-permute-done.12.refs_9_.refs_4_, ...), custom_call_target="tpu_custom_call" | custom-call | flops 805306368 | bytes 8388608 | tf_op jit(solution)/shard_map/work/pallas_call | solution.py:149
  (81 shorter events, 19.9 us)
Async XLA Ops:
  6.5 162.0 %copy-start = (f32[5,256,256]{2,1,0:T(8,128)S(1)}, f32[5,256,256]{2,1,0:T(8,128)}, u32[]{:S(2)}) copy-start(f32[5,256,256]{2,1,0:T(8,128)} %param.5) | copy-start | bytes 3932164
  9.5 10.7 %copy-start.16 = (f32[5,4096,8]{1,2,0:T(8,128)S(1)}, f32[5,4096,8]{1,2,0:T(8,128)}, u32[]{:S(2)}) copy-start(f32[5,4096,8]{1,2,0:T(8,128)} %param.4) | copy-start | bytes 1966084
  9.5 82.5 %all-to-all-start = ((f32[32,128,128]{2,1,0:T(8,128)}), f32[32,128,128]{2,1,0:T(8,128)}, u32[]{:S(2)}, u32[]{:S(2)}) async-start(f32[32,128,128]{2,1,0:T(8,128)} %bitcast.1), calls=%async_computation | async-start | bytes 4194304 | tf_op jit(solution)/shard_map/all_to_all | solution.py:64
  20.2 67.1 %all-gather.5.cloned.1.call-start = ((), (), s32[]{:S(2)}) async-start(), calls=%async_computation.11 | async-start | bytes 1310720 | tf_op jit(solution)/shard_map/all_gather | solution.py:226
  21.1 106.9 %all-gather.7.cloned.1.call-start = ((), (), s32[]{:S(2)}) async-start(), calls=%async_computation.12 | async-start | bytes 1966080 | tf_op jit(solution)/shard_map/all_gather | solution.py:226
  87.3 3.0 collective-permute-start
  92.0 38.7 %copy-start.3 = (f32[128,4096]{1,0:T(8,128)}, f32[128,4096]{1,0:T(8,128)S(1)}, u32[]{:S(2)}) copy-start(f32[128,4096]{1,0:T(8,128)S(1)} %pad_maximum_fusion.refs_1_.refs_0_.refs_2_) | copy-start | bytes 6291460
  92.1 37.3 %collective-permute-start.1 = (f32[128,4096]{1,0:T(8,128)S(1)}, f32[128,4096]{1,0:T(8,128)}, u32[]{:S(2)}, u32[]{:S(2)}) collective-permute-start(f32[128,4096]{1,0:T(8,128)S(1)} %pad_maximum_fusion.refs_1_.refs_0_.refs_2_), channel_id=1, source_target_pairs={{0,2},{1,7},{2,4},{3,1},{4,6},{5,3},{6,0},{7,5},{8,10},{9,15},{10,... | collective-permute-start | bytes 6291464 | tf_op jit(solution)/shard_map/ppermute | solution.py:36
  129.3 5.2 %collective-permute-start.5 = (f32[64,4096]{1,0:T(8,128)S(1)}, f32[64,4096]{1,0:T(8,128)S(1)}, u32[]{:S(2)}, u32[]{:S(2)}) collective-permute-start(f32[64,4096]{1,0:T(8,128)S(1)} %bitcast.62), channel_id=1, source_target_pairs={{0,1},{1,0},{2,3},{3,2},{4,5},{5,4},{6,7},{7,6},{8,9},{9,8},{10,11... | collective-permute-start | bytes 3145736 | tf_op jit(solution)/shard_map/ppermute | solution.py:28
  130.7 16.4 %collective-permute-start.2 = (f32[64,4096]{1,0:T(8,128)S(1)}, f32[64,4096]{1,0:T(8,128)}, u32[]{:S(2)}, u32[]{:S(2)}) collective-permute-start(f32[64,4096]{1,0:T(8,128)S(1)} %slice.74), channel_id=1, source_target_pairs={{0,2},{1,7},{2,4},{3,1},{4,6},{5,3},{6,0},{7,5},{8,10},{9,15},{10,... | collective-permute-start | bytes 3145736 | tf_op jit(solution)/shard_map/ppermute | solution.py:36
  133.1 17.1 %collective-permute-start.3 = (f32[128,4096]{1,0:T(8,128)}, f32[128,4096]{1,0:T(8,128)}, u32[]{:S(2)}, u32[]{:S(2)}) collective-permute-start(f32[128,4096]{1,0:T(8,128)} %collective-permute-done.1.refs_2_.refs_1_.refs_3_), channel_id=1, source_target_pairs={{0,1},{1,0},{2,3},{3,2},{4,5},{5,4},{6,7},{7,6},{8,9},{9,8},{10,11... | collective-permute-start | bytes 6291464 | tf_op jit(solution)/shard_map/ppermute | solution.py:28
  134.6 81.3 %copy-start.1 = (f32[128,4096]{1,0:T(8,128)}, f32[128,4096]{1,0:T(8,128)S(1)}, u32[]{:S(2)}) copy-start(f32[128,4096]{1,0:T(8,128)S(1)} %pad_maximum_fusion.1.refs_0_.refs_7_.refs_2_) | copy-start | bytes 6291460
  134.6 35.9 %collective-permute-start.6 = (f32[128,4096]{1,0:T(8,128)S(1)}, f32[128,4096]{1,0:T(8,128)}, u32[]{:S(2)}, u32[]{:S(2)}) collective-permute-start(f32[128,4096]{1,0:T(8,128)S(1)} %pad_maximum_fusion.1.refs_0_.refs_7_.refs_2_), channel_id=1, source_target_pairs={{0,2},{1,7},{2,4},{3,1},{4,6},{5,3},{6,0},{7,5},{8,10},{9,15},{10,... | collective-permute-start | bytes 6291464 | tf_op jit(solution)/shard_map/ppermute | solution.py:36
  147.2 3.0 collective-permute-start.4
  150.2 1.6 copy-start.4
  159.9 0.7 copy-start.15
  160.6 21.3 %all-to-all-start.1 = ((f32[8,64,128]{2,1,0:T(8,128)}), f32[8,64,128]{2,1,0:T(8,128)}, u32[]{:S(2)}, u32[]{:S(2)}) async-start(f32[8,64,128]{2,1,0:T(8,128)} %bitcast.58), calls=%async_computation.1 | async-start | bytes 524288 | tf_op jit(solution)/shard_map/all_to_all | solution.py:69
  168.5 5.7 %copy-start.5 = (f32[128,4096]{1,0:T(8,128)S(1)}, f32[128,4096]{1,0:T(8,128)}, u32[]{:S(2)}) copy-start(f32[128,4096]{1,0:T(8,128)} %copy-done.3) | copy-start | bytes 6291460
  172.8 19.3 %collective-permute-start.7 = (f32[64,4096]{1,0:T(8,128)}, f32[64,4096]{1,0:T(8,128)}, u32[]{:S(2)}, u32[]{:S(2)}) collective-permute-start(f32[64,4096]{1,0:T(8,128)} %slice.79), channel_id=1, source_target_pairs={{0,2},{1,7},{2,4},{3,1},{4,6},{5,3},{6,0},{7,5},{8,10},{9,15},{10,... | collective-permute-start | bytes 3145736 | tf_op jit(solution)/shard_map/ppermute | solution.py:36
  173.1 42.8 %collective-permute-start.8 = (f32[128,4096]{1,0:T(8,128)}, f32[128,4096]{1,0:T(8,128)}, u32[]{:S(2)}, u32[]{:S(2)}) collective-permute-start(f32[128,4096]{1,0:T(8,128)} %collective-permute-done.6.refs_1_.refs_8_.refs_3_), channel_id=1, source_target_pairs={{0,1},{1,0},{2,3},{3,2},{4,5},{5,4},{6,7},{7,6},{8,9},{9,8},{10,11... | collective-permute-start | bytes 6291464 | tf_op jit(solution)/shard_map/ppermute | solution.py:28
  181.2 0.7 copy-start.14
  181.9 13.6 %all-to-all-start.3 = ((f32[8,32,256]{2,1,0:T(8,128)}), f32[8,32,256]{2,1,0:T(8,128)}, u32[]{:S(2)}, u32[]{:S(2)}) async-start(f32[8,32,256]{2,1,0:T(8,128)} %bitcast.57), calls=%async_computation.3 | async-start | bytes 524288 | tf_op jit(solution)/shard_map/all_to_all | solution.py:69
  191.2 22.4 %collective-permute-start.10 = (f32[32,4096]{1,0:T(8,128)}, f32[32,4096]{1,0:T(8,128)}, u32[]{:S(2)}, u32[]{:S(2)}) collective-permute-start(f32[32,4096]{1,0:T(8,128)} %slice_bitcast_fusion), channel_id=1, source_target_pairs={{0,1},{1,0},{2,3},{3,2},{4,5},{5,4},{6,7},{7,6},{8,9},{9,8},{10,11... | collective-permute-start | bytes 1572872 | tf_op jit(solution)/shard_map/ppermute | solution.py:28
  192.2 23.8 %collective-permute-start.9 = (f32[64,4096]{1,0:T(8,128)}, f32[64,4096]{1,0:T(8,128)}, u32[]{:S(2)}, u32[]{:S(2)}) collective-permute-start(f32[64,4096]{1,0:T(8,128)} %collective-permute-done.7.refs_2_.refs_9_.refs_4_), channel_id=1, source_target_pairs={{0,1},{1,0},{2,3},{3,2},{4,5},{5,4},{6,7},{7,6},{8,9},{9,8},{10,11... | collective-permute-start | bytes 3145736 | tf_op jit(solution)/shard_map/ppermute | solution.py:28
  196.2 11.3 %all-to-all-start.2 = ((f32[8,64,128]{2,1,0:T(8,128)}), f32[8,64,128]{2,1,0:T(8,128)}, u32[]{:S(2)}, u32[]{:S(2)}) async-start(f32[8,64,128]{2,1,0:T(8,128)} %broadcast_in_dim.18), calls=%async_computation.2 | async-start | bytes 524288 | tf_op jit(solution)/shard_map/all_to_all | solution.py:71
  208.2 15.4 %all-to-all-start.4 = ((f32[8,32,256]{2,1,0:T(8,128)}), f32[8,32,256]{2,1,0:T(8,128)}, u32[]{:S(2)}, u32[]{:S(2)}) async-start(f32[8,32,256]{2,1,0:T(8,128)} %broadcast_in_dim.19), calls=%async_computation.4 | async-start | bytes 524288 | tf_op jit(solution)/shard_map/all_to_all | solution.py:71
  215.8 42.4 %collective-permute-start.11 = (f32[64,4096]{1,0:T(8,128)}, f32[64,4096]{1,0:T(8,128)}, u32[]{:S(2)}, u32[]{:S(2)}) collective-permute-start(f32[64,4096]{1,0:T(8,128)} %pad_maximum_fusion.2.refs_7_.refs_2_), channel_id=1, source_target_pairs={{0,2},{1,7},{2,4},{3,1},{4,6},{5,3},{6,0},{7,5},{8,10},{9,15},{10,... | collective-permute-start | bytes 3145736 | tf_op jit(solution)/shard_map/ppermute | solution.py:36
  223.7 1.0 copy-start.9
  227.2 1.6 copy-start.6
  240.3 1.3 copy-start.7
  252.9 11.3 %all-to-all-start.7 = ((f32[8,32,256]{2,1,0:T(8,128)}), f32[8,32,256]{2,1,0:T(8,128)}, u32[]{:S(2)}, u32[]{:S(2)}) async-start(f32[8,32,256]{2,1,0:T(8,128)} %bitcast.45), calls=%async_computation.7 | async-start | bytes 524288 | tf_op jit(solution)/shard_map/all_to_all | solution.py:69
  260.1 10.7 %collective-permute-start.12 = (f32[32,4096]{1,0:T(8,128)}, f32[32,4096]{1,0:T(8,128)}, u32[]{:S(2)}, u32[]{:S(2)}) collective-permute-start(f32[32,4096]{1,0:T(8,128)} %slice.83), channel_id=1, source_target_pairs={{0,2},{1,7},{2,4},{3,1},{4,6},{5,3},{6,0},{7,5},{8,10},{9,15},{10,... | collective-permute-start | bytes 1572872 | tf_op jit(solution)/shard_map/ppermute | solution.py:36
  261.3 30.5 %collective-permute-start.13 = (f32[64,4096]{1,0:T(8,128)}, f32[64,4096]{1,0:T(8,128)}, u32[]{:S(2)}, u32[]{:S(2)}) collective-permute-start(f32[64,4096]{1,0:T(8,128)} %collective-permute-done.11.refs_8_.refs_3_), channel_id=1, source_target_pairs={{0,1},{1,0},{2,3},{3,2},{4,5},{5,4},{6,7},{7,6},{8,9},{9,8},{10,11... | collective-permute-start | bytes 3145736 | tf_op jit(solution)/shard_map/ppermute | solution.py:28
  261.3 30.5 %copy-start.2 = (f32[128,4096]{1,0:T(8,128)S(1)}, f32[128,4096]{1,0:T(8,128)}, u32[]{:S(2)}) copy-start(f32[128,4096]{1,0:T(8,128)} %copy-done.1) | copy-start | bytes 6291460
  264.9 11.3 %all-to-all-start.6 = ((f32[8,64,128]{2,1,0:T(8,128)}), f32[8,64,128]{2,1,0:T(8,128)}, u32[]{:S(2)}, u32[]{:S(2)}) async-start(f32[8,64,128]{2,1,0:T(8,128)} %broadcast_in_dim.20), calls=%async_computation.6 | async-start | bytes 524288 | tf_op jit(solution)/shard_map/all_to_all | solution.py:71
  270.8 21.0 %collective-permute-start.14 = (f32[32,4096]{1,0:T(8,128)}, f32[32,4096]{1,0:T(8,128)}, u32[]{:S(2)}, u32[]{:S(2)}) collective-permute-start(f32[32,4096]{1,0:T(8,128)} %collective-permute-done.12.refs_9_.refs_4_), channel_id=1, source_target_pairs={{0,1},{1,0},{2,3},{3,2},{4,5},{5,4},{6,7},{7,6},{8,9},{9,8},{10,11... | collective-permute-start | bytes 1572872 | tf_op jit(solution)/shard_map/ppermute | solution.py:28
  276.9 11.3 %all-to-all-start.8 = ((f32[8,32,256]{2,1,0:T(8,128)}), f32[8,32,256]{2,1,0:T(8,128)}, u32[]{:S(2)}, u32[]{:S(2)}) async-start(f32[8,32,256]{2,1,0:T(8,128)} %broadcast_in_dim.21), calls=%async_computation.8 | async-start | bytes 524288 | tf_op jit(solution)/shard_map/all_to_all | solution.py:71
  288.2 1.0 copy-start.10
  291.8 1.6 copy-start.8
  303.0 1.3 copy-start.11
  322.7 1.0 copy-start.13
  324.1 1.6 copy-start.12
Sparse Core Ops, SparseCore 0:
  22.9 64.4 all-gather.4
  89.1 38.8 all-gather.6
where the time goes:
time: 344 us; the launch traced here: 340 us
  waiting for transfers between devices  134 us (39%)
  starting transfers between devices  61.4 us (18%)
  Pallas kernels  56.8 us (17%)
  blocking collectives  29.6 us (9%)
  local copies, waits for them, and re-layouts  29.1 us (8%)
  between operations  13.7 us (4%)
  other arithmetic  11.3 us (3%)
  matrix products  4.11 us (1%)
    all_gather x2, waiting for transfers between devices, gather_z(): return lax.all_gather(mine, 'zh', axis=1).reshape(32 * len(blocks), ROWS)  101 us
    pallas_call x4, Pallas kernels, work(): pl.pallas_call(functools.partial(work_kernel, bool(old), bool(new)), grid...  36.7 us
    all_to_all x4, starting transfers between devices, row_sum(): lax.all_to_all(a, ROW, split_axis=0, concat_axis=0, tiled=True)  21.3 us
    all_to_all x3, starting transfers between devices, row_sum(): lax.all_to_all(a.reshape(8, n // 8, width), ROW, split_axis=0, concat_axi...  20.5 us
    all_to_all x2, blocking collectives, row_sum(): lax.all_to_all(a.reshape(8, n // 8, width), ROW, split_axis=0, concat_axi...  20.5 us
    pallas_call x2, Pallas kernels, overlap(): pl.pallas_call(overlap_kernel, grid=(ROWS // STEP,), in_specs=piece_specs...  14.7 us
    unnamed x34, local copies, waits for them, and re-layouts  13.5 us
    ppermute x6, waiting for transfers between devices, both_ways(): return lax.ppermute(a, (axis, 'core'), pairs)  13 us
  transfers between devices with their start and end apart: 25, of which 11 were waited for; matrix products, arithmetic and copies ran while one was open for 8% of the time, Pallas kernels for 12%

commit v1 on v0

v1 whole, which is shorter than its diff:
```python
import functools

import jax
import jax.numpy as jnp
from jax import lax
from jax.experimental import pallas as pl
from jax.experimental.pallas import tpu as pltpu
from jax.sharding import Mesh
from jax.sharding import PartitionSpec as P

AXES = ("zl", "y", "zh", "x", "core")
SIZES = (2, 4, 4, 4, 2)
ROW, COL = ("zl", "y"), ("zh", "x", "core")
RING = 4
ROWS = 4096
NB = 256
K = 128
STEP = 1024
HIGHEST = lax.Precision.HIGHEST


def tie(a, *events):
    return lax.optimization_barrier((a, *events))[0] if events else a


def shift(a, axis, by):
    n = SIZES[AXES.index(axis)]
    return lax.ppermute(a, axis, [(i, (i + by) % n) for i in range(n)])


def both_ways(a, axis):
    pairs = []
    for i in range(RING):
        pairs.append((i * 2, ((i + 1) % RING) * 2))
        pairs.append((i * 2 + 1, ((i - 1) % RING) * 2 + 1))
    return lax.ppermute(a, (axis, "core"), pairs)


def swap(a):
    return shift(a, "core", 1)


def gather_z(v, other, *events):
    n = v.shape[0]
    near = both_ways(tie(jnp.concatenate([v, other], 0), *events), "zh")
    far = both_ways(near[:n], "zh")
    got = swap(jnp.concatenate([near, far], 0))
    mine = by_block((v, near[:n], near[n:], far))
    theirs = by_block((other, got[:n], got[n : 2 * n], got[2 * n :]))
    return jnp.concatenate([mine, theirs], 0), near


def by_block(parts):
    n = parts[0].shape[0] // 8
    return jnp.stack([p.reshape(n, 8, ROWS) for p in parts], 1).reshape(32 * n, ROWS)


def gather_x(full, before=(), between=()):
    half = full.shape[0] // 2
    near = both_ways(tie(full, *before), "x")
    far = both_ways(tie(near[:half], *between), "x")
    return (full, near, far, swap(near), swap(far))


def chunks(n, i):
    return (i, n + i, 2 * n + i, 3 * n + i, 4 * n + i, 5 * n + i, 6 * n + i, 7 * n + i)


def column_order(ring):
    z, x, c = (lax.axis_index(a) for a in COL)
    s = 1 - 2 * c

    def half(core, sign):
        if ring:
            return [(z, core), (z - sign, core), (z - sign, 1 - core), (z + 2, core)]
        return [(i, core) for i in range(4)]

    mine, theirs = half(c, s), half(1 - c, -s)
    order = [(x, mine), (x, theirs), (x - s, mine), (x - s, theirs), (x + 2, mine)]
    order += [(x + s, theirs), (x + s, mine), (x + 2, theirs)]
    unit = jnp.stack([((zz % 4) * 4 + xx % 4) * 2 + cc for xx, units in order for zz, cc in units])
    return (unit[:, None] * 8 + jnp.arange(8)[None, :]).reshape(NB)


def exchange(eigvecs):
    return lax.all_to_all(eigvecs.T.reshape(32, K, 128), COL, split_axis=0, concat_axis=0, tiled=True)


def row_sum(a):
    n, width = a.shape
    a = lax.all_to_all(a.reshape(8, n // 8, width), ROW, split_axis=0, concat_axis=0, tiled=True)
    a = jnp.broadcast_to(jnp.sum(a, 0), a.shape)
    return lax.all_to_all(a, ROW, split_axis=0, concat_axis=0, tiled=True).reshape(n, width)


def row_sum_small(w):
    w = w + shift(w, "zl", 1)
    return w + shift(w, "y", 1) + shift(w, "y", 2) + shift(w, "y", 3)


def split(a):
    hi = a.astype(jnp.bfloat16)
    return hi, (a - hi.astype(jnp.float32)).astype(jnp.bfloat16)


def dot(a, b, dims):
    return lax.dot_general(a, b, (dims, ((), ())), preferred_element_type=jnp.float32)


NT = ((1,), (1,))
NN = ((1,), (0,))


def project(v, cur):
    (vh, vl), (ch, cl) = v, cur
    n = ch.shape[0]
    both = dot(vh, jnp.concatenate([ch, cl], 0), NT)
    return both[:, :n] + both[:, n:] + dot(vl, ch, NT)


def spread_out(applied, v):
    (ah, al), (vh, vl) = applied, v
    both = dot(jnp.concatenate([ah, al], 0), vh, NN)
    return both[:K] + both[K:] + dot(ah, vl, NN)


def stacked(refs):
    return jnp.concatenate([r[...] for r in refs], 0)


def block_of(a, i, n):
    return jnp.concatenate([a[32 * k : 32 * k + 32] for k in chunks(n, i)], 0)


def work_kernel(has_old, has_new, *refs):
    cur_ref, refs = refs[0], refs[1:]
    cur = cur_ref[...] if len(cur_ref.shape) == 2 else jnp.concatenate([cur_ref[i] for i in range(STEP // 128)], 1)
    if has_old:
        applied, old, refs = split(refs[0][...]), split(stacked(refs[1:6])), refs[6:]
        cur = cur - spread_out(applied, old)
    if not has_new:
        refs[0][...] = cur.T
        return
    new, refs = stacked(refs[:5]), refs[5:]
    if has_old:
        refs[0][...] = cur
        refs = refs[1:]
    w_ref = refs[0]
    if new.shape[0] == NB:
        part = project(split(new), split(cur))
    else:
        high, low = split(new)
        first, second = ((block_of(high, i, 2), block_of(low, i, 2)) for i in range(2))
        now = split(cur)
        g = project(second, first)
        part = jnp.concatenate([project(first, now), project(second, now), g[:, :K], g[:, K:]], 0)

    @pl.when(pl.program_id(0) == 0)
    def _():
        w_ref[...] = part

    @pl.when(pl.program_id(0) != 0)
    def _():
        w_ref[...] += part


def piece_specs(pieces):
    return [pl.BlockSpec((p.shape[0], STEP), lambda i: (0, i)) for p in pieces]


def rows_of(pieces):
    return sum(p.shape[0] for p in pieces)


def work(cur, applied, old, new):
    args, specs = [cur], [pl.BlockSpec((K, STEP), lambda i: (0, i))]
    if cur.ndim == 3:
        specs = [pl.BlockSpec((STEP // 128, K, 128), lambda i: (i, 0, 0))]
    if old:
        args += [applied, *old]
        specs += [pl.BlockSpec(applied.shape, lambda i: (0, 0))] + piece_specs(old)
    args += new
    specs += piece_specs(new)
    shapes, outs = [], []
    if not new:
        shapes.append(jax.ShapeDtypeStruct((ROWS, K), jnp.float32))
        outs.append(pl.BlockSpec((STEP, K), lambda i: (i, 0)))
    elif old:
        shapes.append(jax.ShapeDtypeStruct((K, ROWS), jnp.float32))
        outs.append(pl.BlockSpec((K, STEP), lambda i: (0, i)))
    if new:
        n = 1024 if rows_of(new) > NB else NB
        shapes.append(jax.ShapeDtypeStruct((n, K), jnp.float32))
        outs.append(pl.BlockSpec((n, K), lambda i: (0, 0)))
    n = rows_of(old) + rows_of(new)
    return pl.pallas_call(
        functools.partial(work_kernel, bool(old), bool(new)),
        grid=(ROWS // STEP,),
        in_specs=specs,
        out_specs=outs,
        out_shape=shapes,
        compiler_params=pltpu.CompilerParams(vmem_limit_bytes=50 << 20),
        cost_estimate=pl.CostEstimate(
            flops=6 * n * K * ROWS, bytes_accessed=4 * ROWS * (n + 2 * K), transcendentals=0
        ),
        name="work",
    )(*args)


def exact(a, b):
    return lax.dot_general(a, b, (NN, ((), ())), precision=HIGHEST, preferred_element_type=jnp.float32)


def solve_kernel(n, t_ref, w_ref, out):
    done = [exact(t_ref[0], w_ref[:NB])]
    if n == 2:
        g = exact(w_ref[2 * NB : 3 * NB], done[0][:K]) + exact(w_ref[3 * NB :], done[0][K:])
        done.append(exact(t_ref[1], w_ref[NB : 2 * NB] - g))
    laid = sorted((k, i, j) for i in range(n) for j, k in enumerate(chunks(n, i)))
    out[...] = jnp.concatenate([done[i][32 * j : 32 * j + 32] for _, i, j in laid], 0).T


def solve(t, w):
    n = t.shape[0]
    return pl.pallas_call(
        functools.partial(solve_kernel, n),
        out_shape=jax.ShapeDtypeStruct((K, NB * n), jnp.float32),
        cost_estimate=pl.CostEstimate(flops=12 * n * NB * NB * K, bytes_accessed=1 << 20, transcendentals=0),
        compiler_params=pltpu.CompilerParams(vmem_limit_bytes=24 << 20),
        name="solve",
    )(t, w)


def on_device(eigvecs, householder, tfactor):
    v = jnp.swapaxes(householder, 1, 2)

    v43 = jnp.concatenate([v[4], v[3]], 0)
    rest = jnp.stack([v[2], v[1], v[0]])
    full43, _ = gather_z(v43, swap(v43), rest)
    rest = lax.all_gather(rest, "zh", axis=1).reshape(96, ROWS)

    def full(half):
        return jnp.concatenate([half, swap(half)], 0)

    cur = exchange(eigvecs)
    pieces = [gather_x(full43)]
    pieces.append(gather_x(full(rest[:64]), (pieces[0][1], cur), (pieces[0][2],)))
    pieces.append(gather_x(full(rest[64:]), (pieces[1][1],), (pieces[1][2],)))

    def ordered(ring, *blocks):
        pick = (column_order(ring)[:, None] == jnp.arange(NB)[None, :]).astype(jnp.float32)
        part = jnp.stack([tfactor[b] for b in blocks])
        return jnp.einsum("ij,bjk,lk->bil", pick, part, pick, precision=HIGHEST)

    ts = [ordered(True, 4, 3), ordered(False, 2, 1), ordered(False, 0)]

    applied, old = None, ()
    for t, new in zip(ts, pieces):
        res = work(cur, applied, old, new)
        if old:
            cur, w = res
        else:
            (w,) = res
        applied = solve(t, row_sum(w) if len(t) == 2 else row_sum_small(w))
        old = new
    return work(cur, applied, old, ())[0]


def solution(mesh):
    fine = Mesh(mesh.devices.reshape(SIZES), AXES)
    placed = (P(ROW + COL, None), P(None, ROW, COL), P())
    return jax.shard_map(on_device, mesh=fine, in_specs=placed, out_specs=P(ROW, COL), check_vma=False)
```

time: 344 us -> 285 us (0.83)
  blocking collectives: 29.6 us -> 0 us
  Pallas kernels: 56.8 us -> 36.8 us
  starting transfers between devices: 61.4 us -> 77.3 us
  waiting for transfers between devices: 134 us -> 121 us
  local copies, waits for them, and re-layouts: 29.1 us -> 21.1 us
  other arithmetic: 11.3 us -> 7.11 us
    all_gather x2 -> x1, waiting for transfers between devices: 101 us -> 37.7 us  [on_device(): rest = lax.all_gather(rest, 'zh', axis=1).reshape(96, ROWS)]
    ppermute x6 -> x8, waiting for transfers between devices: 13 us -> 51.4 us  [both_ways(): return lax.ppermute(a, (axis, 'core'), pairs)]
    all_to_all x3 -> x0, blocking collectives: 29.6 us -> none  [the longest x2 20.5 us: row_sum(): lax.all_to_all(a.reshape(8, n // 8, width), ROW, split_axis=0, concat_axi...]
    all_to_all x3 -> x2, starting transfers between devices: 20.5 us -> 39 us  [row_sum(): lax.all_to_all(a.reshape(8, n // 8, width), ROW, split_axis=0, concat_axi...]
    pallas_call x2 -> x0, Pallas kernels: 14.7 us -> none  [overlap(): pl.pallas_call(overlap_kernel, grid=(ROWS // STEP,), in_specs=piece_specs...]
    unnamed x34 -> x42, local copies, waits for them, and re-layouts: 13.5 us -> 5.38 us
    pallas_call x4, Pallas kernels: 36.7 us -> 31.3 us  [work(): pl.pallas_call(functools.partial(work_kernel, bool(old), bool(new)), grid...]
    ppermute x9 -> x14, waiting for transfers between devices: 5.04 us -> 9.78 us  [shift(): return lax.ppermute(a, axis, [(i, (i + by) % n) for i in range(n)])]
  transfers between devices with their start and end apart: 25 -> 28, of which waited for: 11 -> 16; matrix products, arithmetic and copies ran while one was open for 8% -> 9% of each run, Pallas kernels for 12% -> 8%
where the time goes in v1:
time: 285 us; the launch traced here: 284 us
  waiting for transfers between devices  121 us (42%)
  starting transfers between devices  77.3 us (27%)
  Pallas kernels  36.8 us (13%)
  local copies, waits for them, and re-layouts  21.1 us (7%)
  between operations  13.9 us (5%)
  other arithmetic  7.11 us (2%)
  matrix products  6.14 us (2%)
    ppermute x8, waiting for transfers between devices, both_ways(): return lax.ppermute(a, (axis, 'core'), pairs)  51.4 us
    all_to_all x2, starting transfers between devices, row_sum(): lax.all_to_all(a.reshape(8, n // 8, width), ROW, split_axis=0, concat_axi...  39 us
    all_gather x1, waiting for transfers between devices, on_device(): rest = lax.all_gather(rest, 'zh', axis=1).reshape(96, ROWS)  37.7 us
    pallas_call x4, Pallas kernels, work(): pl.pallas_call(functools.partial(work_kernel, bool(old), bool(new)), grid...  31.3 us
    all_to_all x2, starting transfers between devices, row_sum(): lax.all_to_all(a, ROW, split_axis=0, concat_axis=0, tiled=True)  17 us
    all_to_all x2, waiting for transfers between devices, row_sum(): lax.all_to_all(a, ROW, split_axis=0, concat_axis=0, tiled=True)  12 us
    ppermute x14, waiting for transfers between devices, shift(): return lax.ppermute(a, axis, [(i, (i + by) % n) for i in range(n)])  9.78 us
    ppermute x8, starting transfers between devices, both_ways(): return lax.ppermute(a, (axis, 'core'), pairs)  8.48 us
  transfers between devices with their start and end apart: 28, of which 16 were waited for; matrix products, arithmetic and copies ran while one was open for 9% of the time, Pallas kernels for 8%

profile of v1, /device:TPU:32, one launch (start us, length us, event | category | flops | bytes accessed | tf_op | source)
XLA Modules:
  0.0 283.6 jit_solution(5260370230343584013)
XLA Ops:
  6.5 1.2 fusion.29
  10.3 3.3 %collective-permute-start.1 = (f32[32,4096]{1,0:T(8,128)S(1)}, f32[32,4096]{1,0:T(8,128)S(1)}, u32[]{:S(2)}, u32[]{:S(2)}) collective-permute-start(f32[32,4096]{1,0:T(8,128)S(1)} %pad_maximum_fusion.6), channel_id=1, source_target_pairs={{0,8},{1,25},{8,16},{9,1},{16,24},{17,9},{24,0},{25,17},{2,10},{3,... | collective-permute-start | bytes 1572872 | tf_op jit(solution)/shard_map/ppermute | solution.py:36
  13.6 14.9 %collective-permute-done.1 = f32[32,4096]{1,0:T(8,128)S(1)} collective-permute-done((f32[32,4096]{1,0:T(8,128)S(1)}, f32[32,4096]{1,0:T(8,128)S(1)}, u32[]{:S(2)}, u32[]{:S(2)}) %collective-permute-start.1) | collective-permute-done | bytes 524320 | tf_op jit(solution)/shard_map/ppermute | solution.py:36
  29.8 9.9 %collective-permute-done.2 = f32[16,4096]{1,0:T(8,128)S(1)} collective-permute-done((f32[16,4096]{1,0:T(8,128)S(1)}, f32[16,4096]{1,0:T(8,128)S(1)}, u32[]{:S(2)}, u32[]{:S(2)}) %collective-permute-start.2) | collective-permute-done | bytes 262176 | tf_op jit(solution)/shard_map/ppermute | solution.py:36
  40.8 1.8 copy.7
  42.6 6.5 %all-to-all-start = ((f32[32,128,128]{2,1,0:T(8,128)}), f32[32,128,128]{2,1,0:T(8,128)S(1)}, u32[]{:S(2)}, u32[]{:S(2)}) async-start(f32[32,128,128]{2,1,0:T(8,128)} %bitcast.111), calls=%async_computation | async-start | bytes 4194304 | tf_op jit(solution)/shard_map/all_to_all | solution.py:86
  49.3 1.2 slice_bitcast_fusion.3
  50.7 1.5 pad_maximum_fusion.refs_1_.refs_2_
  52.2 1.8 collective-permute-start.4
  54.0 37.7 %all-gather.3.cloned.1.call-done = f32[3,32,4096]{2,1,0:T(8,128)} async-done(((f32[3,8,4096]{2,1,0:T(8,128)}), f32[3,32,4096]{2,1,0:T(8,128)}) %all-gather.3.cloned.1.call-update) | async-done | bytes 1572880 | tf_op jit(solution)/shard_map/all_gather | solution.py:240
  91.7 1.3 slice.102
  93.2 3.7 %collective-permute-done.4.refs_2_.refs_3_ = f32[128,4096]{1,0:T(8,128)} collective-permute-done((f32[128,4096]{1,0:T(8,128)}, f32[128,4096]{1,0:T(8,128)}, u32[]{:S(2)}, u32[]{:S(2)}) %collective-permute-start.4) | collective-permute-done | bytes 2097184 | tf_op jit(solution)/shard_map/ppermute | solution.py:36
  96.9 2.3 slice.101
  99.3 1.5 pad_maximum_fusion.1.refs_7_.refs_2_
  100.8 2.4 all-to-all-done.refs_0_
  103.3 2.3 collective-permute-start.9
  105.5 9.9 %collective-permute-done.5.refs_3_.refs_4_ = f32[64,4096]{1,0:T(8,128)S(1)} collective-permute-done((f32[64,4096]{1,0:T(8,128)}, f32[64,4096]{1,0:T(8,128)S(1)}, u32[]{:S(2)}, u32[]{:S(2)}) %collective-permute-start.5) | collective-permute-done | bytes 1048608 | tf_op jit(solution)/shard_map/ppermute | solution.py:36
  115.6 2.4 fusion.28
  118.1 8.0 %work.4 = f32[1024,128]{1,0:T(8,128)} custom-call(f32[32,128,128]{2,1,0:T(8,128)} %copy-done.11, f32[128,4096]{1,0:T(8,128)} %pad_maximum_fusion.refs_1_.refs_2_, f32[128,4096]{1,0:T(8,128)} %collective-permute-done.4.refs_2_.refs_3_, f32[64,4096]{1,0:T(8,128)S(1)} %collective-permute-done.5.refs_3_.refs_4_, ...), custom_call_target="tpu_custom_call" | custom-call | flops 1610612736 | bytes 12582912 | tf_op jit(solution)/shard_map/work/pallas_call | solution.py:196
  126.1 34.1 %all-to-all-start.1 = ((f32[8,128,128]{2,1,0:T(8,128)}), f32[8,128,128]{2,1,0:T(8,128)S(1)}, u32[]{:S(2)}, u32[]{:S(2)}) async-start(f32[8,128,128]{2,1,0:T(8,128)} %bitcast.48), calls=%async_computation.1 | async-start | bytes 1048576 | tf_op jit(solution)/shard_map/all_to_all | solution.py:91
  160.3 1.3 slice.103
  162.1 1.3 collective-permute-start.11
  163.4 1.1 slice_bitcast_fusion
  164.8 12.9 %collective-permute-done.10.refs_9_.refs_4_ = f32[64,4096]{1,0:T(8,128)S(1)} collective-permute-done((f32[64,4096]{1,0:T(8,128)S(1)}, f32[64,4096]{1,0:T(8,128)S(1)}, u32[]{:S(2)}, u32[]{:S(2)}) %collective-permute-start.10) | collective-permute-done | bytes 1048608 | tf_op jit(solution)/shard_map/ppermute | solution.py:36
  178.7 11.9 %all-to-all-start.2 = ((f32[8,128,128]{2,1,0:T(8,128)}), f32[8,128,128]{2,1,0:T(8,128)}, u32[]{:S(2)}, u32[]{:S(2)}) async-start(f32[8,128,128]{2,1,0:T(8,128)} %broadcast_in_dim.4), calls=%async_computation.2 | async-start | bytes 1048576 | tf_op jit(solution)/shard_map/all_to_all | solution.py:93
  191.3 1.3 fusion.16.t_ref
  192.6 7.5 %all-to-all-done.2 = f32[8,128,128]{2,1,0:T(8,128)} async-done(((f32[8,128,128]{2,1,0:T(8,128)}), f32[8,128,128]{2,1,0:T(8,128)}, u32[]{:S(2)}, u32[]{:S(2)}) %all-to-all-start.2) | async-done | bytes 524320 | tf_op jit(solution)/shard_map/all_to_all | solution.py:93
  201.1 2.5 solve.3.refs_1_
  203.6 1.2 copy-done.5
  204.8 1.2 copy-done.7
  206.1 10.4 %work.5 = (f32[128,4096]{1,0:T(8,128)}, f32[1024,128]{1,0:T(8,128)S(1)}) custom-call(f32[32,128,128]{2,1,0:T(8,128)} %copy-done.11, f32[128,512]{1,0:T(8,128)S(1)} %solve.3.refs_1_, f32[128,4096]{1,0:T(8,128)} %pad_maximum_fusion.refs_1_.refs_2_, f32[128,4096]{1,0:T(8,128)} %collective-permute-done.4.refs_2_.refs_3_, f32[64,4096]{1,0:T(8,128)S(1)} %copy-done.5, ...), custom_call_target="tpu_custom_call" | custom-call | flops 3221225472 | bytes 20971520 | tf_op jit(solution)/shard_map/work/pallas_call | solution.py:196
  217.3 4.8 %all-to-all-start.3 = ((f32[8,128,128]{2,1,0:T(8,128)}), f32[8,128,128]{2,1,0:T(8,128)}, u32[]{:S(2)}, u32[]{:S(2)}) async-start(f32[8,128,128]{2,1,0:T(8,128)} %bitcast.110), calls=%async_computation.3 | async-start | bytes 1048576 | tf_op jit(solution)/shard_map/all_to_all | solution.py:91
  222.5 7.9 %all-to-all-done.3 = f32[8,128,128]{2,1,0:T(8,128)} async-done(((f32[8,128,128]{2,1,0:T(8,128)}), f32[8,128,128]{2,1,0:T(8,128)}, u32[]{:S(2)}, u32[]{:S(2)}) %all-to-all-start.3) | async-done | bytes 524320 | tf_op jit(solution)/shard_map/all_to_all | solution.py:91
  230.4 1.1 reduce_sum.19
  232.3 5.1 %all-to-all-start.4 = ((f32[8,128,128]{2,1,0:T(8,128)}), f32[8,128,128]{2,1,0:T(8,128)}, u32[]{:S(2)}, u32[]{:S(2)}) async-start(f32[8,128,128]{2,1,0:T(8,128)} %broadcast_in_dim.5), calls=%async_computation.4 | async-start | bytes 1048576 | tf_op jit(solution)/shard_map/all_to_all | solution.py:93
  237.7 1.4 fusion.4
  239.1 1.3 fusion.12.t_ref
  240.4 4.6 %all-to-all-done.4 = f32[8,128,128]{2,1,0:T(8,128)} async-done(((f32[8,128,128]{2,1,0:T(8,128)}), f32[8,128,128]{2,1,0:T(8,128)}, u32[]{:S(2)}, u32[]{:S(2)}) %all-to-all-start.4) | async-done | bytes 524320 | tf_op jit(solution)/shard_map/all_to_all | solution.py:93
  246.0 2.5 solve.4.refs_1_
  248.6 8.0 %work.6 = (f32[128,4096]{1,0:T(8,128)}, f32[256,128]{1,0:T(8,128)S(1)}) custom-call(f32[128,4096]{1,0:T(8,128)} %get-tuple-element.17.refs_0_, f32[128,512]{1,0:T(8,128)S(1)} %solve.4.refs_1_, f32[128,4096]{1,0:T(8,128)} %pad_maximum_fusion.1.refs_7_.refs_2_, f32[128,4096]{1,0:T(8,128)} %collective-permute-done.9.refs_8_.refs_3_, ...), custom_call_target="tpu_custom_call" | custom-call | flops 2415919104 | bytes 16777216 | tf_op jit(solution)/shard_map/work/pallas_call | solution.py:196
  256.6 1.1 collective-permute-start.18
  257.7 3.9 %collective-permute-done.18 = f32[256,128]{1,0:T(8,128)S(1)} collective-permute-done((f32[256,128]{1,0:T(8,128)S(1)}, f32[256,128]{1,0:T(8,128)S(1)}, u32[]{:S(2)}, u32[]{:S(2)}) %collective-permute-start.18) | collective-permute-done | bytes 131104 | tf_op jit(solution)/shard_map/ppermute | solution.py:28
  261.6 1.8 collective-permute-start.21
  263.4 1.5 collective-permute-start.20
  264.9 1.3 fusion.8
  266.9 3.0 %collective-permute-done.20 = f32[256,128]{1,0:T(8,128)S(1)} collective-permute-done((f32[256,128]{1,0:T(8,128)S(1)}, f32[256,128]{1,0:T(8,128)S(1)}, u32[]{:S(2)}, u32[]{:S(2)}) %collective-permute-start.20) | collective-permute-done | bytes 131104 | tf_op jit(solution)/shard_map/ppermute | solution.py:28
  269.9 1.4 collective-permute-done.19
  271.8 4.9 %work.7 = f32[4096,128]{1,0:T(8,128)} custom-call(f32[128,4096]{1,0:T(8,128)} %get-tuple-element.21.refs_0_, f32[128,256]{1,0:T(8,128)S(1)} %solve.5.refs_1_, f32[64,4096]{1,0:T(8,128)S(1)} %copy-done.1, f32[64,4096]{1,0:T(8,128)S(1)} %copy-done.3, f32[32,4096]{1,0:T(8,128)S(1)} %collective-permute-done.15.refs_9_.refs_4_, ...), custom_call_target="tpu_custom_call" | custom-call | flops 805306368 | bytes 8388608 | tf_op jit(solution)/shard_map/work/pallas_call | solution.py:196
  (99 shorter events, 13.6 us)
Async XLA Ops:
  6.5 85.2 %all-gather.3.cloned.1.call-start = ((), (), s32[]{:S(2)}) async-start(), calls=%async_computation.5 | async-start | bytes 1966080 | tf_op jit(solution)/shard_map/all_gather | solution.py:240
  8.5 1.7 collective-permute-start
  9.3 31.5 %copy-start.12 = (f32[128,4096]{1,0:T(8,128)S(1)}, f32[128,4096]{1,0:T(8,128)}, u32[]{:S(2)}) copy-start(f32[128,4096]{1,0:T(8,128)} %param.3) | copy-start | bytes 6291460
  10.2 30.5 %copy-start.17 = (f32[16,4096]{1,0:T(8,128)}, f32[16,4096]{1,0:T(8,128)S(1)}, u32[]{:S(2)}) copy-start(f32[16,4096]{1,0:T(8,128)S(1)} %collective-permute-done) | copy-start | bytes 786436
  10.3 18.3 %collective-permute-start.1 = (f32[32,4096]{1,0:T(8,128)S(1)}, f32[32,4096]{1,0:T(8,128)S(1)}, u32[]{:S(2)}, u32[]{:S(2)}) collective-permute-start(f32[32,4096]{1,0:T(8,128)S(1)} %pad_maximum_fusion.6), channel_id=1, source_target_pairs={{0,8},{1,25},{8,16},{9,1},{16,24},{17,9},{24,0},{25,17},{2,10},{3,... | collective-permute-start | bytes 1572872 | tf_op jit(solution)/shard_map/ppermute | solution.py:36
  29.4 10.3 %collective-permute-start.2 = (f32[16,4096]{1,0:T(8,128)S(1)}, f32[16,4096]{1,0:T(8,128)S(1)}, u32[]{:S(2)}, u32[]{:S(2)}) collective-permute-start(f32[16,4096]{1,0:T(8,128)S(1)} %get-tuple-element.37), channel_id=1, source_target_pairs={{0,8},{1,25},{8,16},{9,1},{16,24},{17,9},{24,0},{25,17},{2,10},{3,... | collective-permute-start | bytes 786440 | tf_op jit(solution)/shard_map/ppermute | solution.py:36
  39.7 2.9 %copy-start.19 = (f32[16,4096]{1,0:T(8,128)}, f32[16,4096]{1,0:T(8,128)S(1)}, u32[]{:S(2)}) copy-start(f32[16,4096]{1,0:T(8,128)S(1)} %collective-permute-done.2) | copy-start | bytes 786436
  40.7 8.6 %collective-permute-start.3 = (f32[48,4096]{1,0:T(8,128)}, f32[48,4096]{1,0:T(8,128)}, u32[]{:S(2)}, u32[]{:S(2)}) collective-permute-start(f32[48,4096]{1,0:T(8,128)} %pad_maximum_fusion.5), channel_id=1, source_target_pairs={{0,1},{1,0},{2,3},{3,2},{4,5},{5,4},{6,7},{7,6},{8,9},{9,8},{10,11... | collective-permute-start | bytes 2359304 | tf_op jit(solution)/shard_map/ppermute | solution.py:28
  42.6 6.5 %copy-start.15 = (f32[2,1,8,4096]{3,2,0,1:T(8,128)S(1)}, f32[2,1,8,4096]{3,2,0,1:T(8,128)}, u32[]{:S(2)}) copy-start(f32[2,1,8,4096]{3,2,0,1:T(8,128)} %get-tuple-element.35) | copy-start | bytes 786436
  42.6 6.6 %copy-start.16 = (f32[2,1,8,4096]{3,2,0,1:T(8,128)S(1)}, f32[2,1,8,4096]{3,2,0,1:T(8,128)}, u32[]{:S(2)}) copy-start(f32[2,1,8,4096]{3,2,0,1:T(8,128)} %get-tuple-element.36) | copy-start | bytes 786436
  42.6 6.6 %copy-start.20 = (f32[16,4096]{1,0:T(8,128)S(1)}, f32[16,4096]{1,0:T(8,128)}, u32[]{:S(2)}) copy-start(f32[16,4096]{1,0:T(8,128)} %copy-done.19) | copy-start | bytes 786436
  42.6 60.6 %all-to-all-start = ((f32[32,128,128]{2,1,0:T(8,128)}), f32[32,128,128]{2,1,0:T(8,128)S(1)}, u32[]{:S(2)}, u32[]{:S(2)}) async-start(f32[32,128,128]{2,1,0:T(8,128)} %bitcast.111), calls=%async_computation | async-start | bytes 4194304 | tf_op jit(solution)/shard_map/all_to_all | solution.py:86
  49.2 1.3 copy-start.18
  52.2 44.7 %collective-permute-start.4 = (f32[128,4096]{1,0:T(8,128)}, f32[128,4096]{1,0:T(8,128)}, u32[]{:S(2)}, u32[]{:S(2)}) collective-permute-start(f32[128,4096]{1,0:T(8,128)} %pad_maximum_fusion.refs_1_.refs_2_), channel_id=1, source_target_pairs={{0,2},{1,7},{2,4},{3,1},{4,6},{5,3},{6,0},{7,5},{8,10},{9,15},{10,... | collective-permute-start | bytes 6291464 | tf_op jit(solution)/shard_map/ppermute | solution.py:36
  93.0 6.3 %collective-permute-start.8 = (f32[64,4096]{1,0:T(8,128)S(1)}, f32[64,4096]{1,0:T(8,128)S(1)}, u32[]{:S(2)}, u32[]{:S(2)}) collective-permute-start(f32[64,4096]{1,0:T(8,128)S(1)} %bitcast.112), channel_id=1, source_target_pairs={{0,1},{1,0},{2,3},{3,2},{4,5},{5,4},{6,7},{7,6},{8,9},{9,8},{10,11... | collective-permute-start | bytes 3145736 | tf_op jit(solution)/shard_map/ppermute | solution.py:28
  99.2 16.2 %collective-permute-start.5 = (f32[64,4096]{1,0:T(8,128)}, f32[64,4096]{1,0:T(8,128)S(1)}, u32[]{:S(2)}, u32[]{:S(2)}) collective-permute-start(f32[64,4096]{1,0:T(8,128)} %slice.101), channel_id=1, source_target_pairs={{0,2},{1,7},{2,4},{3,1},{4,6},{5,3},{6,0},{7,5},{8,10},{9,15},{10,... | collective-permute-start | bytes 3145736 | tf_op jit(solution)/shard_map/ppermute | solution.py:36
  99.2 18.7 %collective-permute-start.6 = (f32[128,4096]{1,0:T(8,128)}, f32[128,4096]{1,0:T(8,128)}, u32[]{:S(2)}, u32[]{:S(2)}) collective-permute-start(f32[128,4096]{1,0:T(8,128)} %collective-permute-done.4.refs_2_.refs_3_), channel_id=1, source_target_pairs={{0,1},{1,0},{2,3},{3,2},{4,5},{5,4},{6,7},{7,6},{8,9},{9,8},{10,11... | collective-permute-start | bytes 6291464 | tf_op jit(solution)/shard_map/ppermute | solution.py:28
  103.2 2.3 copy-start.11
  103.3 57.0 %collective-permute-start.9 = (f32[128,4096]{1,0:T(8,128)}, f32[128,4096]{1,0:T(8,128)}, u32[]{:S(2)}, u32[]{:S(2)}) collective-permute-start(f32[128,4096]{1,0:T(8,128)} %pad_maximum_fusion.1.refs_7_.refs_2_), channel_id=1, source_target_pairs={{0,2},{1,7},{2,4},{3,1},{4,6},{5,3},{6,0},{7,5},{8,10},{9,15},{10,... | collective-permute-start | bytes 6291464 | tf_op jit(solution)/shard_map/ppermute | solution.py:36
  115.4 10.7 %copy-start.4 = (f32[64,4096]{1,0:T(8,128)}, f32[64,4096]{1,0:T(8,128)S(1)}, u32[]{:S(2)}) copy-start(f32[64,4096]{1,0:T(8,128)S(1)} %collective-permute-done.5.refs_3_.refs_4_) | copy-start | bytes 3145732
  115.5 2.7 collective-permute-start.7
  118.1 8.0 %copy-start.6 = (f32[64,4096]{1,0:T(8,128)}, f32[64,4096]{1,0:T(8,128)S(1)}, u32[]{:S(2)}) copy-start(f32[64,4096]{1,0:T(8,128)S(1)} %collective-permute-done.7.refs_5_.refs_6_) | copy-start | bytes 3145732
  126.1 51.7 %all-to-all-start.1 = ((f32[8,128,128]{2,1,0:T(8,128)}), f32[8,128,128]{2,1,0:T(8,128)S(1)}, u32[]{:S(2)}, u32[]{:S(2)}) async-start(f32[8,128,128]{2,1,0:T(8,128)} %bitcast.48), calls=%async_computation.1 | async-start | bytes 1048576 | tf_op jit(solution)/shard_map/all_to_all | solution.py:91
  161.6 29.0 %copy-start.13 = (f32[1,256,256]{2,1,0:T(8,128)S(1)}, f32[1,256,256]{2,1,0:T(8,128)}, u32[]{:S(2)}) copy-start(f32[1,256,256]{2,1,0:T(8,128)} %get-tuple-element.24) | copy-start | bytes 786436
  161.6 29.0 %copy-start.14 = (f32[1,256,256]{2,1,0:T(8,128)S(1)}, f32[1,256,256]{2,1,0:T(8,128)}, u32[]{:S(2)}) copy-start(f32[1,256,256]{2,1,0:T(8,128)} %get-tuple-element.25) | copy-start | bytes 786436
  161.6 16.1 %collective-permute-start.10 = (f32[64,4096]{1,0:T(8,128)S(1)}, f32[64,4096]{1,0:T(8,128)S(1)}, u32[]{:S(2)}, u32[]{:S(2)}) collective-permute-start(f32[64,4096]{1,0:T(8,128)S(1)} %slice.103), channel_id=1, source_target_pairs={{0,2},{1,7},{2,4},{3,1},{4,6},{5,3},{6,0},{7,5},{8,10},{9,15},{10,... | collective-permute-start | bytes 3145736 | tf_op jit(solution)/shard_map/ppermute | solution.py:36
  162.1 41.5 %collective-permute-start.11 = (f32[128,4096]{1,0:T(8,128)}, f32[128,4096]{1,0:T(8,128)}, u32[]{:S(2)}, u32[]{:S(2)}) collective-permute-start(f32[128,4096]{1,0:T(8,128)} %collective-permute-done.9.refs_8_.refs_3_), channel_id=1, source_target_pairs={{0,1},{1,0},{2,3},{3,2},{4,5},{5,4},{6,7},{7,6},{8,9},{9,8},{10,11... | collective-permute-start | bytes 6291464 | tf_op jit(solution)/shard_map/ppermute | solution.py:28
  164.5 26.6 %collective-permute-start.13 = (f32[32,4096]{1,0:T(8,128)S(1)}, f32[32,4096]{1,0:T(8,128)S(1)}, u32[]{:S(2)}, u32[]{:S(2)}) collective-permute-start(f32[32,4096]{1,0:T(8,128)S(1)} %slice_bitcast_fusion), channel_id=1, source_target_pairs={{0,1},{1,0},{2,3},{3,2},{4,5},{5,4},{6,7},{7,6},{8,9},{9,8},{10,11... | collective-permute-start | bytes 1572872 | tf_op jit(solution)/shard_map/ppermute | solution.py:28
  177.7 25.9 %collective-permute-start.12 = (f32[64,4096]{1,0:T(8,128)S(1)}, f32[64,4096]{1,0:T(8,128)}, u32[]{:S(2)}, u32[]{:S(2)}) collective-permute-start(f32[64,4096]{1,0:T(8,128)S(1)} %collective-permute-done.10.refs_9_.refs_4_), channel_id=1, source_target_pairs={{0,1},{1,0},{2,3},{3,2},{4,5},{5,4},{6,7},{7,6},{8,9},{9,8},{10,11... | collective-permute-start | bytes 3145736 | tf_op jit(solution)/shard_map/ppermute | solution.py:28
  178.7 21.3 %all-to-all-start.2 = ((f32[8,128,128]{2,1,0:T(8,128)}), f32[8,128,128]{2,1,0:T(8,128)}, u32[]{:S(2)}, u32[]{:S(2)}) async-start(f32[8,128,128]{2,1,0:T(8,128)} %broadcast_in_dim.4), calls=%async_computation.2 | async-start | bytes 1048576 | tf_op jit(solution)/shard_map/all_to_all | solution.py:93
  191.2 25.3 %copy-start = (f32[64,4096]{1,0:T(8,128)}, f32[64,4096]{1,0:T(8,128)S(1)}, u32[]{:S(2)}) copy-start(f32[64,4096]{1,0:T(8,128)S(1)} %pad_maximum_fusion.4.refs_7_.refs_2_) | copy-start | bytes 3145732
  191.2 30.9 %collective-permute-start.14 = (f32[64,4096]{1,0:T(8,128)S(1)}, f32[64,4096]{1,0:T(8,128)S(1)}, u32[]{:S(2)}, u32[]{:S(2)}) collective-permute-start(f32[64,4096]{1,0:T(8,128)S(1)} %pad_maximum_fusion.4.refs_7_.refs_2_), channel_id=1, source_target_pairs={{0,2},{1,7},{2,4},{3,1},{4,6},{5,3},{6,0},{7,5},{8,10},{9,15},{10,... | collective-permute-start | bytes 3145736 | tf_op jit(solution)/shard_map/ppermute | solution.py:36
  200.0 1.0 copy-start.8
  203.6 1.2 copy-start.5
  204.8 1.2 copy-start.7
  217.3 13.1 %all-to-all-start.3 = ((f32[8,128,128]{2,1,0:T(8,128)}), f32[8,128,128]{2,1,0:T(8,128)}, u32[]{:S(2)}, u32[]{:S(2)}) async-start(f32[8,128,128]{2,1,0:T(8,128)} %bitcast.110), calls=%async_computation.3 | async-start | bytes 1048576 | tf_op jit(solution)/shard_map/all_to_all | solution.py:91
  222.1 17.0 %copy-start.2 = (f32[64,4096]{1,0:T(8,128)}, f32[64,4096]{1,0:T(8,128)S(1)}, u32[]{:S(2)}) copy-start(f32[64,4096]{1,0:T(8,128)S(1)} %collective-permute-done.14.refs_8_.refs_3_) | copy-start | bytes 3145732
  222.2 15.2 %collective-permute-start.15 = (f32[32,4096]{1,0:T(8,128)S(1)}, f32[32,4096]{1,0:T(8,128)S(1)}, u32[]{:S(2)}, u32[]{:S(2)}) collective-permute-start(f32[32,4096]{1,0:T(8,128)S(1)} %slice.105), channel_id=1, source_target_pairs={{0,2},{1,7},{2,4},{3,1},{4,6},{5,3},{6,0},{7,5},{8,10},{9,15},{10,... | collective-permute-start | bytes 1572872 | tf_op jit(solution)/shard_map/ppermute | solution.py:36
  222.3 26.3 %collective-permute-start.16 = (f32[64,4096]{1,0:T(8,128)S(1)}, f32[64,4096]{1,0:T(8,128)}, u32[]{:S(2)}, u32[]{:S(2)}) collective-permute-start(f32[64,4096]{1,0:T(8,128)S(1)} %collective-permute-done.14.refs_8_.refs_3_), channel_id=1, source_target_pairs={{0,1},{1,0},{2,3},{3,2},{4,5},{5,4},{6,7},{7,6},{8,9},{9,8},{10,11... | collective-permute-start | bytes 3145736 | tf_op jit(solution)/shard_map/ppermute | solution.py:28
  232.3 12.7 %all-to-all-start.4 = ((f32[8,128,128]{2,1,0:T(8,128)}), f32[8,128,128]{2,1,0:T(8,128)}, u32[]{:S(2)}, u32[]{:S(2)}) async-start(f32[8,128,128]{2,1,0:T(8,128)} %broadcast_in_dim.5), calls=%async_computation.4 | async-start | bytes 1048576 | tf_op jit(solution)/shard_map/all_to_all | solution.py:93
  237.4 11.2 %collective-permute-start.17 = (f32[32,4096]{1,0:T(8,128)S(1)}, f32[32,4096]{1,0:T(8,128)S(1)}, u32[]{:S(2)}, u32[]{:S(2)}) collective-permute-start(f32[32,4096]{1,0:T(8,128)S(1)} %collective-permute-done.15.refs_9_.refs_4_), channel_id=1, source_target_pairs={{0,1},{1,0},{2,3},{3,2},{4,5},{5,4},{6,7},{7,6},{8,9},{9,8},{10,11... | collective-permute-start | bytes 1572872 | tf_op jit(solution)/shard_map/ppermute | solution.py:28
  245.0 1.0 copy-start.9
  256.6 15.2 %copy-start.1 = (f32[64,4096]{1,0:T(8,128)S(1)}, f32[64,4096]{1,0:T(8,128)}, u32[]{:S(2)}) copy-start(f32[64,4096]{1,0:T(8,128)} %copy-done) | copy-start | bytes 3145732
  256.6 15.2 %copy-start.3 = (f32[64,4096]{1,0:T(8,128)S(1)}, f32[64,4096]{1,0:T(8,128)}, u32[]{:S(2)}) copy-start(f32[64,4096]{1,0:T(8,128)} %copy-done.2) | copy-start | bytes 3145732
  256.6 5.1 %collective-permute-start.18 = (f32[256,128]{1,0:T(8,128)S(1)}, f32[256,128]{1,0:T(8,128)S(1)}, u32[]{:S(2)}, u32[]{:S(2)}) collective-permute-start(f32[256,128]{1,0:T(8,128)S(1)} %get-tuple-element.22), channel_id=1, source_target_pairs={{0,128},{128,0},{1,129},{129,1},{2,130},{130,2},{3,131},{131,3},{4... | collective-permute-start | bytes 393224 | tf_op jit(solution)/shard_map/ppermute | solution.py:28
  261.6 5.3 %collective-permute-start.21 = (f32[256,128]{1,0:T(8,128)S(1)}, f32[256,128]{1,0:T(8,128)S(1)}, u32[]{:S(2)}, u32[]{:S(2)}) collective-permute-start(f32[256,128]{1,0:T(8,128)S(1)} %add.695), channel_id=1, source_target_pairs={{0,96},{32,0},{64,32},{96,64},{1,97},{33,1},{65,33},{97,65},{2,98}... | collective-permute-start | bytes 393224 | tf_op jit(solution)/shard_map/ppermute | solution.py:28
  263.4 6.5 %collective-permute-start.20 = (f32[256,128]{1,0:T(8,128)S(1)}, f32[256,128]{1,0:T(8,128)S(1)}, u32[]{:S(2)}, u32[]{:S(2)}) collective-permute-start(f32[256,128]{1,0:T(8,128)S(1)} %add.695), channel_id=1, source_target_pairs={{0,64},{32,96},{64,0},{96,32},{1,65},{33,97},{65,1},{97,33},{2,66}... | collective-permute-start | bytes 393224 | tf_op jit(solution)/shard_map/ppermute | solution.py:28
  264.9 6.4 %collective-permute-start.19 = (f32[256,128]{1,0:T(8,128)S(1)}, f32[256,128]{1,0:T(8,128)S(1)}, u32[]{:S(2)}, u32[]{:S(2)}) collective-permute-start(f32[256,128]{1,0:T(8,128)S(1)} %add.695), channel_id=1, source_target_pairs={{0,32},{32,64},{64,96},{96,0},{1,33},{33,65},{65,97},{97,1},{2,34}... | collective-permute-start | bytes 393224 | tf_op jit(solution)/shard_map/ppermute | solution.py:28
  (1 other events, 0.8 us)
Sparse Core Ops, SparseCore 0:
  40.9 50.8 all-gather.2

commit v2 on v1

--- a/solution.py
+++ b/solution.py
@@ -40,11 +40,11 @@
     return shift(a, "core", 1)
 
 
-def gather_z(v, other, *events):
+def gather_z(v, other, before=(), between=(), after=()):
     n = v.shape[0]
-    near = both_ways(tie(jnp.concatenate([v, other], 0), *events), "zh")
-    far = both_ways(near[:n], "zh")
-    got = swap(jnp.concatenate([near, far], 0))
+    near = both_ways(tie(jnp.concatenate([v, other], 0), *before), "zh")
+    far = both_ways(tie(near[:n], *between), "zh")
+    got = swap(tie(jnp.concatenate([near, far], 0), *after))
     mine = by_block((v, near[:n], near[n:], far))
     theirs = by_block((other, got[:n], got[n : 2 * n], got[2 * n :]))
     return jnp.concatenate([mine, theirs], 0), near
@@ -86,11 +86,16 @@
     return lax.all_to_all(eigvecs.T.reshape(32, K, 128), COL, split_axis=0, concat_axis=0, tiled=True)
 
 
-def row_sum(a):
+def row_share(a):
     n, width = a.shape
     a = lax.all_to_all(a.reshape(8, n // 8, width), ROW, split_axis=0, concat_axis=0, tiled=True)
-    a = jnp.broadcast_to(jnp.sum(a, 0), a.shape)
-    return lax.all_to_all(a, ROW, split_axis=0, concat_axis=0, tiled=True).reshape(n, width)
+    return jnp.sum(a, 0)
+
+
+def hand_on(share):
+    n, width = share.shape
+    a = jnp.broadcast_to(share, (8, n, width))
+    return lax.all_to_all(a, ROW, split_axis=0, concat_axis=0, tiled=True).reshape(8 * n, width)
 
 
 def row_sum_small(w):
@@ -234,36 +239,30 @@
 def on_device(eigvecs, householder, tfactor):
     v = jnp.swapaxes(householder, 1, 2)
 
-    v43 = jnp.concatenate([v[4], v[3]], 0)
-    rest = jnp.stack([v[2], v[1], v[0]])
-    full43, _ = gather_z(v43, swap(v43), rest)
-    rest = lax.all_gather(rest, "zh", axis=1).reshape(96, ROWS)
-
-    def full(half):
-        return jnp.concatenate([half, swap(half)], 0)
-
+    v43, v21 = jnp.concatenate([v[4], v[3]], 0), jnp.concatenate([v[2], v[1]], 0)
+    full43, _ = gather_z(v43, swap(v43))
     cur = exchange(eigvecs)
-    pieces = [gather_x(full43)]
-    pieces.append(gather_x(full(rest[:64]), (pieces[0][1], cur), (pieces[0][2],)))
-    pieces.append(gather_x(full(rest[64:]), (pieces[1][1],), (pieces[1][2],)))
+    pieces43 = gather_x(full43, (), (cur,))
+    near43, far43 = pieces43[1:3]
+    full21, _ = gather_z(v21, swap(v21), (full43,), (near43, cur), (far43,))
+    (w,) = work(cur, None, (), pieces43)
+    share = row_share(w)
+    pieces21 = gather_x(full21, (far43,), (share,))
+    near21, far21 = pieces21[1:3]
+    full0, _ = gather_z(v[0], swap(v[0]), (far43,), (share,))
+    pieces0 = gather_x(full0, (near21,), (far21,))
 
     def ordered(ring, *blocks):
         pick = (column_order(ring)[:, None] == jnp.arange(NB)[None, :]).astype(jnp.float32)
         part = jnp.stack([tfactor[b] for b in blocks])
         return jnp.einsum("ij,bjk,lk->bil", pick, part, pick, precision=HIGHEST)
 
-    ts = [ordered(True, 4, 3), ordered(False, 2, 1), ordered(False, 0)]
-
-    applied, old = None, ()
-    for t, new in zip(ts, pieces):
-        res = work(cur, applied, old, new)
-        if old:
-            cur, w = res
-        else:
-            (w,) = res
-        applied = solve(t, row_sum(w) if len(t) == 2 else row_sum_small(w))
-        old = new
-    return work(cur, applied, old, ())[0]
+    applied = solve(ordered(True, 4, 3), hand_on(share))
+    cur, w = work(cur, applied, pieces43, pieces21)
+    applied = solve(ordered(True, 2, 1), hand_on(row_share(w)))
+    cur, w = work(cur, applied, pieces21, pieces0)
+    applied = solve(ordered(True, 0), row_sum_small(w))
+    return work(cur, applied, pieces0, ())[0]
 
 
 def solution(mesh):

time: 285 us -> 252 us (0.88)
  starting transfers between devices: 77.3 us -> 54.4 us
  between operations: 13.9 us -> 0.51 us
  waiting for transfers between devices: 121 us -> 125 us
    all_gather x1 -> x0, waiting for transfers between devices: 37.7 us -> none  [on_device(): rest = lax.all_gather(rest, 'zh', axis=1).reshape(96, ROWS)]
    ppermute x8 -> x12, waiting for transfers between devices: 51.4 us -> 87.7 us  [both_ways(): return lax.ppermute(a, (axis, 'core'), pairs)]
    all_to_all x4, starting transfers between devices: 55.9 us -> 24.5 us  [the longest x2 14.9 us: row_share(): lax.all_to_all(a.reshape(8, n // 8, width), ROW, split_axis=0, concat_axi...]
    ppermute x8 -> x12, starting transfers between devices: 8.48 us -> 15.5 us  [both_ways(): return lax.ppermute(a, (axis, 'core'), pairs)]
    all_to_all x4, waiting for transfers between devices: 19.9 us -> 24.5 us  [the longest x2 18 us: row_share(): lax.all_to_all(a.reshape(8, n // 8, width), ROW, split_axis=0, concat_axi...]
    slice x3 -> x0, local copies, waits for them, and re-layouts: 3.58 us -> none  [the longest x1 1.29 us: on_device(): rest[:64]]
    ppermute x14 -> x16, waiting for transfers between devices: 9.78 us -> 12.9 us  [shift(): return lax.ppermute(a, axis, [(i, (i + by) % n) for i in range(n)])]
    unnamed x42 -> x48, local copies, waits for them, and re-layouts: 5.38 us -> 6.98 us
  transfers between devices with their start and end apart: 28 -> 33, of which waited for: 16 -> 15; matrix products, arithmetic and copies ran while one was open for 9% -> 10% of each run, Pallas kernels for 8% -> 9%
where the time goes in v2:
time: 252 us; the launch traced here: 251 us
  waiting for transfers between devices  125 us (50%)
  starting transfers between devices  54.4 us (22%)
  Pallas kernels  36.8 us (15%)
  local copies, waits for them, and re-layouts  20.2 us (8%)
  other arithmetic  8.18 us (3%)
  matrix products  6.1 us (2%)
    ppermute x12, waiting for transfers between devices, both_ways(): return lax.ppermute(a, (axis, 'core'), pairs)  87.7 us
    pallas_call x4, Pallas kernels, work(): pl.pallas_call(functools.partial(work_kernel, bool(old), bool(new)), grid...  31.3 us
    all_to_all x2, waiting for transfers between devices, row_share(): lax.all_to_all(a.reshape(8, n // 8, width), ROW, split_axis=0, concat_axi...  18 us
    ppermute x12, starting transfers between devices, both_ways(): return lax.ppermute(a, (axis, 'core'), pairs)  15.5 us
    all_to_all x2, starting transfers between devices, row_share(): lax.all_to_all(a.reshape(8, n // 8, width), ROW, split_axis=0, concat_axi...  14.9 us
    ppermute x16, waiting for transfers between devices, shift(): return lax.ppermute(a, axis, [(i, (i + by) % n) for i in range(n)])  12.9 us
    all_to_all x2, starting transfers between devices, hand_on(): lax.all_to_all(a, ROW, split_axis=0, concat_axis=0, tiled=True)  9.66 us
    ppermute x16, starting transfers between devices, shift(): return lax.ppermute(a, axis, [(i, (i + by) % n) for i in range(n)])  7.72 us
  transfers between devices with their start and end apart: 33, of which 15 were waited for; matrix products, arithmetic and copies ran while one was open for 10% of the time, Pallas kernels for 9%

profile of v2, /device:TPU:32, one launch (start us, length us, event | category | flops | bytes accessed | tf_op | source)
XLA Modules:
  0.0 251.2 jit_solution(706537685657232120)
XLA Ops:
  0.0 1.9 slice_bitcast_fusion.17
  2.0 1.5 collective-permute-done
  3.6 3.3 %collective-permute-start.1 = (f32[32,4096]{1,0:T(8,128)S(1)}, f32[32,4096]{1,0:T(8,128)S(1)}, u32[]{:S(2)}, u32[]{:S(2)}) collective-permute-start(f32[32,4096]{1,0:T(8,128)S(1)} %pad_maximum_fusion.9), channel_id=1, source_target_pairs={{0,8},{1,25},{8,16},{9,1},{16,24},{17,9},{24,0},{25,17},{2,10},{3,... | collective-permute-start | bytes 1572872 | tf_op jit(solution)/shard_map/ppermute | solution.py:36
  6.9 14.9 %collective-permute-done.1 = f32[32,4096]{1,0:T(8,128)S(1)} collective-permute-done((f32[32,4096]{1,0:T(8,128)S(1)}, f32[32,4096]{1,0:T(8,128)S(1)}, u32[]{:S(2)}, u32[]{:S(2)}) %collective-permute-start.1) | collective-permute-done | bytes 524320 | tf_op jit(solution)/shard_map/ppermute | solution.py:36
  22.3 9.9 %collective-permute-done.2 = f32[16,4096]{1,0:T(8,128)S(1)} collective-permute-done((f32[16,4096]{1,0:T(8,128)S(1)}, f32[16,4096]{1,0:T(8,128)S(1)}, u32[]{:S(2)}, u32[]{:S(2)}) %collective-permute-start.2) | collective-permute-done | bytes 262176 | tf_op jit(solution)/shard_map/ppermute | solution.py:36
  33.2 1.8 copy.21
  35.0 6.7 %all-to-all-start = ((f32[32,128,128]{2,1,0:T(8,128)}), f32[32,128,128]{2,1,0:T(8,128)}, u32[]{:S(2)}, u32[]{:S(2)}) async-start(f32[32,128,128]{2,1,0:T(8,128)} %bitcast.1), calls=%async_computation | async-start | bytes 4194304 | tf_op jit(solution)/shard_map/all_to_all | solution.py:86
  41.8 1.2 slice_bitcast_fusion.6
  43.2 1.3 copy-done.11
  44.6 1.7 collective-permute-start.4
  46.3 1.2 collective-permute-start.8
  47.5 1.2 collective-permute-done.8
  48.7 2.4 collective-permute-start.9
  51.1 39.6 %collective-permute-done.4.refs_2_.refs_3_ = f32[128,4096]{1,0:T(8,128)} collective-permute-done((f32[128,4096]{1,0:T(8,128)S(1)}, f32[128,4096]{1,0:T(8,128)}, u32[]{:S(2)}, u32[]{:S(2)}) %collective-permute-start.4) | collective-permute-done | bytes 2097184 | tf_op jit(solution)/shard_map/ppermute | solution.py:36
  90.7 1.3 slice.123
  92.2 2.4 collective-permute-start.10
  94.6 15.8 %collective-permute-done.10 = f32[16,4096]{1,0:T(8,128)S(1)} collective-permute-done((f32[16,4096]{1,0:T(8,128)S(1)}, f32[16,4096]{1,0:T(8,128)S(1)}, u32[]{:S(2)}, u32[]{:S(2)}) %collective-permute-start.10) | collective-permute-done | bytes 262176 | tf_op jit(solution)/shard_map/ppermute | solution.py:36
  115.4 1.5 pad_maximum_fusion.1.refs_7_.refs_2_
  119.6 2.1 collective-permute-start.17
  121.7 8.0 %work.4 = f32[1024,128]{1,0:T(8,128)} custom-call(f32[32,128,128]{2,1,0:T(8,128)} %all-to-all-done.refs_0_, f32[128,4096]{1,0:T(8,128)} %copy-done.11, f32[128,4096]{1,0:T(8,128)} %collective-permute-done.4.refs_2_.refs_3_, f32[64,4096]{1,0:T(8,128)S(1)} %collective-permute-done.5.refs_3_.refs_4_, f32[128,4096]{1,0:T(8,128)} %collective-permute-done.6.refs_4_.refs_5_, ...), custom_call_target="tpu_custom_call" | custom-call | flops 1610612736 | bytes 12582912 | tf_op jit(solution)/shard_map/work/pallas_call | solution.py:201
  129.7 10.2 %all-to-all-start.1 = ((f32[8,128,128]{2,1,0:T(8,128)}), f32[8,128,128]{2,1,0:T(8,128)S(1)}, u32[]{:S(2)}, u32[]{:S(2)}) async-start(f32[8,128,128]{2,1,0:T(8,128)} %bitcast.56), calls=%async_computation.1 | async-start | bytes 1048576 | tf_op jit(solution)/shard_map/all_to_all | solution.py:91
  140.3 9.3 %all-to-all-done.1 = f32[8,128,128]{2,1,0:T(8,128)S(1)} async-done(((f32[8,128,128]{2,1,0:T(8,128)}), f32[8,128,128]{2,1,0:T(8,128)S(1)}, u32[]{:S(2)}, u32[]{:S(2)}) %all-to-all-start.1) | async-done | bytes 524320 | tf_op jit(solution)/shard_map/all_to_all | solution.py:91
  149.6 1.3 collective-permute-start.18
  150.9 2.3 slice.131
  154.0 1.3 fusion.15.t_ref
  156.1 5.1 %all-to-all-start.2 = ((f32[8,128,128]{2,1,0:T(8,128)}), f32[8,128,128]{2,1,0:T(8,128)}, u32[]{:S(2)}, u32[]{:S(2)}) async-start(f32[8,128,128]{2,1,0:T(8,128)} %broadcast_in_dim.4), calls=%async_computation.2 | async-start | bytes 1048576 | tf_op jit(solution)/shard_map/all_to_all | solution.py:98
  161.8 7.6 %collective-permute-done.13.refs_9_.refs_4_ = f32[64,4096]{1,0:T(8,128)S(1)} collective-permute-done((f32[64,4096]{1,0:T(8,128)}, f32[64,4096]{1,0:T(8,128)S(1)}, u32[]{:S(2)}, u32[]{:S(2)}) %collective-permute-start.13) | collective-permute-done | bytes 1048608 | tf_op jit(solution)/shard_map/ppermute | solution.py:36
  170.6 1.3 copy-done.8
  171.9 2.5 %solve.3.refs_1_ = f32[128,512]{1,0:T(8,128)S(1)} custom-call(f32[2,256,256]{2,1,0:T(8,128)S(1)} %copy-done.8, f32[1024,128]{1,0:T(8,128)} %bitcast.57.w_ref), custom_call_target="tpu_custom_call" | custom-call | flops 201326592 | bytes 1048576 | tf_op jit(solution)/shard_map/solve/pallas_call | solution.py:230
  174.5 1.2 copy-done.5
  175.7 1.2 copy-done.7
  176.9 10.4 %work.5 = (f32[128,4096]{1,0:T(8,128)}, f32[1024,128]{1,0:T(8,128)S(1)}) custom-call(f32[32,128,128]{2,1,0:T(8,128)} %all-to-all-done.refs_0_, f32[128,512]{1,0:T(8,128)S(1)} %solve.3.refs_1_, f32[128,4096]{1,0:T(8,128)} %copy-done.11, f32[128,4096]{1,0:T(8,128)} %collective-permute-done.4.refs_2_.refs_3_, f32[64,4096]{1,0:T(8,128)S(1)} %copy-done.5, ...), custom_call_target="tpu_custom_call" | custom-call | flops 3221225472 | bytes 20971520 | tf_op jit(solution)/shard_map/work/pallas_call | solution.py:201
  188.1 4.7 %all-to-all-start.3 = ((f32[8,128,128]{2,1,0:T(8,128)}), f32[8,128,128]{2,1,0:T(8,128)}, u32[]{:S(2)}, u32[]{:S(2)}) async-start(f32[8,128,128]{2,1,0:T(8,128)} %bitcast.145), calls=%async_computation.3 | async-start | bytes 1048576 | tf_op jit(solution)/shard_map/all_to_all | solution.py:91
  194.1 8.8 %all-to-all-done.3 = f32[8,128,128]{2,1,0:T(8,128)} async-done(((f32[8,128,128]{2,1,0:T(8,128)}), f32[8,128,128]{2,1,0:T(8,128)}, u32[]{:S(2)}, u32[]{:S(2)}) %all-to-all-start.3) | async-done | bytes 524320 | tf_op jit(solution)/shard_map/all_to_all | solution.py:91
  204.8 4.6 %all-to-all-start.4 = ((f32[8,128,128]{2,1,0:T(8,128)}), f32[8,128,128]{2,1,0:T(8,128)}, u32[]{:S(2)}, u32[]{:S(2)}) async-start(f32[8,128,128]{2,1,0:T(8,128)} %broadcast_in_dim.5), calls=%async_computation.4 | async-start | bytes 1048576 | tf_op jit(solution)/shard_map/all_to_all | solution.py:98
  209.4 1.4 fusion.4
  210.8 1.3 fusion.12.t_ref
  212.1 6.4 %all-to-all-done.4 = f32[8,128,128]{2,1,0:T(8,128)} async-done(((f32[8,128,128]{2,1,0:T(8,128)}), f32[8,128,128]{2,1,0:T(8,128)}, u32[]{:S(2)}, u32[]{:S(2)}) %all-to-all-start.4) | async-done | bytes 524320 | tf_op jit(solution)/shard_map/all_to_all | solution.py:98
  219.6 2.5 %solve.4.refs_1_ = f32[128,512]{1,0:T(8,128)S(1)} custom-call(f32[2,256,256]{2,1,0:T(8,128)S(1)} %copy-done.9, f32[1024,128]{1,0:T(8,128)} %bitcast.79.w_ref), custom_call_target="tpu_custom_call" | custom-call | flops 201326592 | bytes 1048576 | tf_op jit(solution)/shard_map/solve/pallas_call | solution.py:230
  222.1 8.0 %work.6 = (f32[128,4096]{1,0:T(8,128)}, f32[256,128]{1,0:T(8,128)S(1)}) custom-call(f32[128,4096]{1,0:T(8,128)} %get-tuple-element.25.refs_0_, f32[128,512]{1,0:T(8,128)S(1)} %solve.4.refs_1_, f32[128,4096]{1,0:T(8,128)} %pad_maximum_fusion.1.refs_7_.refs_2_, f32[128,4096]{1,0:T(8,128)} %collective-permute-done.12.refs_8_.refs_3_, ...), custom_call_target="tpu_custom_call" | custom-call | flops 2415919104 | bytes 16777216 | tf_op jit(solution)/shard_map/work/pallas_call | solution.py:201
  231.0 4.3 %collective-permute-done.24 = f32[256,128]{1,0:T(8,128)S(1)} collective-permute-done((f32[256,128]{1,0:T(8,128)S(1)}, f32[256,128]{1,0:T(8,128)S(1)}, u32[]{:S(2)}, u32[]{:S(2)}) %collective-permute-start.24) | collective-permute-done | bytes 131104 | tf_op jit(solution)/shard_map/ppermute | solution.py:28
  235.4 1.8 collective-permute-start.27
  237.1 1.5 collective-permute-start.26
  238.6 1.3 fusion.8
  240.3 1.8 collective-permute-done.27
  242.1 2.3 collective-permute-done.26
  244.4 1.3 collective-permute-done.25
  246.2 4.9 %work.7 = f32[4096,128]{1,0:T(8,128)} custom-call(f32[128,4096]{1,0:T(8,128)} %get-tuple-element.31.refs_0_, f32[128,256]{1,0:T(8,128)S(1)} %solve.5.refs_1_, f32[64,4096]{1,0:T(8,128)S(1)} %copy-done.1, f32[64,4096]{1,0:T(8,128)S(1)} %copy-done.3, f32[32,4096]{1,0:T(8,128)S(1)} %collective-permute-done.21.refs_9_.refs_4_, ...), custom_call_target="tpu_custom_call" | custom-call | flops 805306368 | bytes 8388608 | tf_op jit(solution)/shard_map/work/pallas_call | solution.py:201
  (118 shorter events, 20.5 us)
Async XLA Ops:
  1.9 31.3 %copy-start.12 = (f32[128,4096]{1,0:T(8,128)S(1)}, f32[128,4096]{1,0:T(8,128)}, u32[]{:S(2)}) copy-start(f32[128,4096]{1,0:T(8,128)} %param.3) | copy-start | bytes 6291460
  1.9 1.6 collective-permute-start
  3.6 18.3 %collective-permute-start.1 = (f32[32,4096]{1,0:T(8,128)S(1)}, f32[32,4096]{1,0:T(8,128)S(1)}, u32[]{:S(2)}, u32[]{:S(2)}) collective-permute-start(f32[32,4096]{1,0:T(8,128)S(1)} %pad_maximum_fusion.9), channel_id=1, source_target_pairs={{0,8},{1,25},{8,16},{9,1},{16,24},{17,9},{24,0},{25,17},{2,10},{3,... | collective-permute-start | bytes 1572872 | tf_op jit(solution)/shard_map/ppermute | solution.py:36
  21.9 10.3 %collective-permute-start.2 = (f32[16,4096]{1,0:T(8,128)S(1)}, f32[16,4096]{1,0:T(8,128)S(1)}, u32[]{:S(2)}, u32[]{:S(2)}) collective-permute-start(f32[16,4096]{1,0:T(8,128)S(1)} %get-tuple-element.54), channel_id=1, source_target_pairs={{0,8},{1,25},{8,16},{9,1},{16,24},{17,9},{24,0},{25,17},{2,10},{3,... | collective-permute-start | bytes 786440 | tf_op jit(solution)/shard_map/ppermute | solution.py:36
  33.2 8.6 %collective-permute-start.3 = (f32[48,4096]{1,0:T(8,128)}, f32[48,4096]{1,0:T(8,128)}, u32[]{:S(2)}, u32[]{:S(2)}) collective-permute-start(f32[48,4096]{1,0:T(8,128)} %pad_maximum_fusion.7), channel_id=1, source_target_pairs={{0,1},{1,0},{2,3},{3,2},{4,5},{5,4},{6,7},{7,6},{8,9},{9,8},{10,11... | collective-permute-start | bytes 2359304 | tf_op jit(solution)/shard_map/ppermute | solution.py:28
  35.0 6.7 %copy-start.21 = (f32[16,4096]{1,0:T(8,128)S(1)}, f32[16,4096]{1,0:T(8,128)}, u32[]{:S(2)}) copy-start(f32[16,4096]{1,0:T(8,128)} %copy-done.20) | copy-start | bytes 786436
  35.0 57.0 %all-to-all-start = ((f32[32,128,128]{2,1,0:T(8,128)}), f32[32,128,128]{2,1,0:T(8,128)}, u32[]{:S(2)}, u32[]{:S(2)}) async-start(f32[32,128,128]{2,1,0:T(8,128)} %bitcast.1), calls=%async_computation | async-start | bytes 4194304 | tf_op jit(solution)/shard_map/all_to_all | solution.py:86
  44.6 46.1 %collective-permute-start.4 = (f32[128,4096]{1,0:T(8,128)S(1)}, f32[128,4096]{1,0:T(8,128)}, u32[]{:S(2)}, u32[]{:S(2)}) collective-permute-start(f32[128,4096]{1,0:T(8,128)S(1)} %pad_maximum_fusion.refs_1_.refs_2_), channel_id=1, source_target_pairs={{0,2},{1,7},{2,4},{3,1},{4,6},{5,3},{6,0},{7,5},{8,10},{9,15},{10,... | collective-permute-start | bytes 6291464 | tf_op jit(solution)/shard_map/ppermute | solution.py:36
  46.3 2.3 collective-permute-start.8
  48.7 2.5 copy-start.17
  48.7 43.4 %collective-permute-start.9 = (f32[32,4096]{1,0:T(8,128)S(1)}, f32[32,4096]{1,0:T(8,128)S(1)}, u32[]{:S(2)}, u32[]{:S(2)}) collective-permute-start(f32[32,4096]{1,0:T(8,128)S(1)} %pad_maximum_fusion.10), channel_id=1, source_target_pairs={{0,8},{1,25},{8,16},{9,1},{16,24},{17,9},{24,0},{25,17},{2,10},{3,... | collective-permute-start | bytes 1572872 | tf_op jit(solution)/shard_map/ppermute | solution.py:36
  92.0 19.3 %collective-permute-start.5 = (f32[64,4096]{1,0:T(8,128)S(1)}, f32[64,4096]{1,0:T(8,128)S(1)}, u32[]{:S(2)}, u32[]{:S(2)}) collective-permute-start(f32[64,4096]{1,0:T(8,128)S(1)} %slice.123), channel_id=1, source_target_pairs={{0,2},{1,7},{2,4},{3,1},{4,6},{5,3},{6,0},{7,5},{8,10},{9,15},{10,... | collective-permute-start | bytes 3145736 | tf_op jit(solution)/shard_map/ppermute | solution.py:36
  92.2 18.2 %collective-permute-start.10 = (f32[16,4096]{1,0:T(8,128)S(1)}, f32[16,4096]{1,0:T(8,128)S(1)}, u32[]{:S(2)}, u32[]{:S(2)}) collective-permute-start(f32[16,4096]{1,0:T(8,128)S(1)} %get-tuple-element.21), channel_id=1, source_target_pairs={{0,8},{1,25},{8,16},{9,1},{16,24},{17,9},{24,0},{25,17},{2,10},{3,... | collective-permute-start | bytes 786440 | tf_op jit(solution)/shard_map/ppermute | solution.py:36
  111.3 10.4 %copy-start.4 = (f32[64,4096]{1,0:T(8,128)}, f32[64,4096]{1,0:T(8,128)S(1)}, u32[]{:S(2)}) copy-start(f32[64,4096]{1,0:T(8,128)S(1)} %collective-permute-done.5.refs_3_.refs_4_) | copy-start | bytes 3145732
  111.3 4.0 %copy-start.18 = (f32[16,4096]{1,0:T(8,128)S(1)}, f32[16,4096]{1,0:T(8,128)}, u32[]{:S(2)}) copy-start(f32[16,4096]{1,0:T(8,128)} %copy-done.17) | copy-start | bytes 786436
  111.3 2.8 %collective-permute-start.11 = (f32[48,4096]{1,0:T(8,128)}, f32[48,4096]{1,0:T(8,128)}, u32[]{:S(2)}, u32[]{:S(2)}) collective-permute-start(f32[48,4096]{1,0:T(8,128)} %pad_maximum_fusion.8), channel_id=1, source_target_pairs={{0,1},{1,0},{2,3},{3,2},{4,5},{5,4},{6,7},{7,6},{8,9},{9,8},{10,11... | collective-permute-start | bytes 2359304 | tf_op jit(solution)/shard_map/ppermute | solution.py:28
  111.5 7.2 %collective-permute-start.16 = (f32[8,4096]{1,0:T(8,128)S(1)}, f32[8,4096]{1,0:T(8,128)}, u32[]{:S(2)}, u32[]{:S(2)}) collective-permute-start(f32[8,4096]{1,0:T(8,128)S(1)} %get-tuple-element.44), channel_id=1, source_target_pairs={{0,1},{1,0},{2,3},{3,2},{4,5},{5,4},{6,7},{7,6},{8,9},{9,8},{10,11... | collective-permute-start | bytes 393224 | tf_op jit(solution)/shard_map/ppermute | solution.py:28
  112.1 9.6 %collective-permute-start.6 = (f32[128,4096]{1,0:T(8,128)}, f32[128,4096]{1,0:T(8,128)}, u32[]{:S(2)}, u32[]{:S(2)}) collective-permute-start(f32[128,4096]{1,0:T(8,128)} %collective-permute-done.4.refs_2_.refs_3_), channel_id=1, source_target_pairs={{0,1},{1,0},{2,3},{3,2},{4,5},{5,4},{6,7},{7,6},{8,9},{9,8},{10,11... | collective-permute-start | bytes 6291464 | tf_op jit(solution)/shard_map/ppermute | solution.py:28
  113.3 8.4 %collective-permute-start.7 = (f32[64,4096]{1,0:T(8,128)S(1)}, f32[64,4096]{1,0:T(8,128)S(1)}, u32[]{:S(2)}, u32[]{:S(2)}) collective-permute-start(f32[64,4096]{1,0:T(8,128)S(1)} %collective-permute-done.5.refs_3_.refs_4_), channel_id=1, source_target_pairs={{0,1},{1,0},{2,3},{3,2},{4,5},{5,4},{6,7},{7,6},{8,9},{9,8},{10,11... | collective-permute-start | bytes 3145736 | tf_op jit(solution)/shard_map/ppermute | solution.py:28
  116.9 34.0 %collective-permute-start.12 = (f32[128,4096]{1,0:T(8,128)}, f32[128,4096]{1,0:T(8,128)}, u32[]{:S(2)}, u32[]{:S(2)}) collective-permute-start(f32[128,4096]{1,0:T(8,128)} %pad_maximum_fusion.1.refs_7_.refs_2_), channel_id=1, source_target_pairs={{0,2},{1,7},{2,4},{3,1},{4,6},{5,3},{6,0},{7,5},{8,10},{9,15},{10,... | collective-permute-start | bytes 6291464 | tf_op jit(solution)/shard_map/ppermute | solution.py:36
  119.6 20.3 %copy-start.15 = (f32[1,256,256]{2,1,0:T(8,128)S(1)}, f32[1,256,256]{2,1,0:T(8,128)}, u32[]{:S(2)}) copy-start(f32[1,256,256]{2,1,0:T(8,128)} %get-tuple-element.34) | copy-start | bytes 786436
  119.6 20.2 %copy-start.16 = (f32[1,256,256]{2,1,0:T(8,128)S(1)}, f32[1,256,256]{2,1,0:T(8,128)}, u32[]{:S(2)}) copy-start(f32[1,256,256]{2,1,0:T(8,128)} %get-tuple-element.35) | copy-start | bytes 786436
  119.6 20.2 %copy-start.23 = (s32[256]{0:T(256)S(1)}, s32[256]{0:T(256)}, u32[]{:S(2)}) copy-start(s32[256]{0:T(256)} %add.629) | copy-start | bytes 3076
  119.6 20.7 %collective-permute-start.17 = (f32[16,4096]{1,0:T(8,128)S(1)}, f32[16,4096]{1,0:T(8,128)S(1)}, u32[]{:S(2)}, u32[]{:S(2)}) collective-permute-start(f32[16,4096]{1,0:T(8,128)S(1)} %pad_maximum_fusion.14), channel_id=1, source_target_pairs={{0,8},{1,25},{8,16},{9,1},{16,24},{17,9},{24,0},{25,17},{2,10},{3,... | collective-permute-start | bytes 786440 | tf_op jit(solution)/shard_map/ppermute | solution.py:36
  121.7 8.0 %copy-start.6 = (f32[64,4096]{1,0:T(8,128)}, f32[64,4096]{1,0:T(8,128)S(1)}, u32[]{:S(2)}) copy-start(f32[64,4096]{1,0:T(8,128)S(1)} %collective-permute-done.7.refs_5_.refs_6_) | copy-start | bytes 3145732
  129.7 19.9 %all-to-all-start.1 = ((f32[8,128,128]{2,1,0:T(8,128)}), f32[8,128,128]{2,1,0:T(8,128)S(1)}, u32[]{:S(2)}, u32[]{:S(2)}) async-start(f32[8,128,128]{2,1,0:T(8,128)} %bitcast.56), calls=%async_computation.1 | async-start | bytes 1048576 | tf_op jit(solution)/shard_map/all_to_all | solution.py:91
  149.6 11.5 %collective-permute-start.18 = (f32[8,4096]{1,0:T(8,128)S(1)}, f32[8,4096]{1,0:T(8,128)S(1)}, u32[]{:S(2)}, u32[]{:S(2)}) collective-permute-start(f32[8,4096]{1,0:T(8,128)S(1)} %get-tuple-element.28), channel_id=1, source_target_pairs={{0,8},{1,25},{8,16},{9,1},{16,24},{17,9},{24,0},{25,17},{2,10},{3,... | collective-permute-start | bytes 393224 | tf_op jit(solution)/shard_map/ppermute | solution.py:36
  153.2 8.6 %copy-start.22 = (f32[1,1,8,4096]{3,2,1,0:T(8,128)S(1)}, f32[1,1,8,4096]{3,2,1,0:T(8,128)}, u32[]{:S(2)}) copy-start(f32[1,1,8,4096]{3,2,1,0:T(8,128)} %get-tuple-element.43) | copy-start | bytes 393220
  153.2 16.2 %collective-permute-start.13 = (f32[64,4096]{1,0:T(8,128)}, f32[64,4096]{1,0:T(8,128)S(1)}, u32[]{:S(2)}, u32[]{:S(2)}) collective-permute-start(f32[64,4096]{1,0:T(8,128)} %slice.131), channel_id=1, source_target_pairs={{0,2},{1,7},{2,4},{3,1},{4,6},{5,3},{6,0},{7,5},{8,10},{9,15},{10,... | collective-permute-start | bytes 3145736 | tf_op jit(solution)/shard_map/ppermute | solution.py:36
  156.1 14.5 %all-to-all-start.2 = ((f32[8,128,128]{2,1,0:T(8,128)}), f32[8,128,128]{2,1,0:T(8,128)}, u32[]{:S(2)}, u32[]{:S(2)}) async-start(f32[8,128,128]{2,1,0:T(8,128)} %broadcast_in_dim.4), calls=%async_computation.2 | async-start | bytes 1048576 | tf_op jit(solution)/shard_map/all_to_all | solution.py:98
  161.2 8.2 %collective-permute-start.19 = (f32[24,4096]{1,0:T(8,128)S(1)}, f32[24,4096]{1,0:T(8,128)S(1)}, u32[]{:S(2)}, u32[]{:S(2)}) collective-permute-start(f32[24,4096]{1,0:T(8,128)S(1)} %pad_maximum_fusion.11), channel_id=1, source_target_pairs={{0,1},{1,0},{2,3},{3,2},{4,5},{5,4},{6,7},{7,6},{8,9},{9,8},{10,11... | collective-permute-start | bytes 1179656 | tf_op jit(solution)/shard_map/ppermute | solution.py:28
  161.3 13.2 %collective-permute-start.14 = (f32[128,4096]{1,0:T(8,128)}, f32[128,4096]{1,0:T(8,128)}, u32[]{:S(2)}, u32[]{:S(2)}) collective-permute-start(f32[128,4096]{1,0:T(8,128)} %collective-permute-done.12.refs_8_.refs_3_), channel_id=1, source_target_pairs={{0,1},{1,0},{2,3},{3,2},{4,5},{5,4},{6,7},{7,6},{8,9},{9,8},{10,11... | collective-permute-start | bytes 6291464 | tf_op jit(solution)/shard_map/ppermute | solution.py:28
  169.4 5.0 %collective-permute-start.15 = (f32[64,4096]{1,0:T(8,128)S(1)}, f32[64,4096]{1,0:T(8,128)}, u32[]{:S(2)}, u32[]{:S(2)}) collective-permute-start(f32[64,4096]{1,0:T(8,128)S(1)} %collective-permute-done.13.refs_9_.refs_4_), channel_id=1, source_target_pairs={{0,1},{1,0},{2,3},{3,2},{4,5},{5,4},{6,7},{7,6},{8,9},{9,8},{10,11... | collective-permute-start | bytes 3145736 | tf_op jit(solution)/shard_map/ppermute | solution.py:28
  170.5 16.9 %copy-start = (f32[64,4096]{1,0:T(8,128)}, f32[64,4096]{1,0:T(8,128)S(1)}, u32[]{:S(2)}) copy-start(f32[64,4096]{1,0:T(8,128)S(1)} %pad_maximum_fusion.6.refs_7_.refs_2_) | copy-start | bytes 3145732
  170.5 22.4 %collective-permute-start.20 = (f32[64,4096]{1,0:T(8,128)S(1)}, f32[64,4096]{1,0:T(8,128)S(1)}, u32[]{:S(2)}, u32[]{:S(2)}) collective-permute-start(f32[64,4096]{1,0:T(8,128)S(1)} %pad_maximum_fusion.6.refs_7_.refs_2_), channel_id=1, source_target_pairs={{0,2},{1,7},{2,4},{3,1},{4,6},{5,3},{6,0},{7,5},{8,10},{9,15},{10,... | collective-permute-start | bytes 3145736 | tf_op jit(solution)/shard_map/ppermute | solution.py:36
  188.1 21.2 %copy-start.14 = (f32[1,256,256]{2,1,0:T(8,128)S(1)}, f32[1,256,256]{2,1,0:T(8,128)}, u32[]{:S(2)}) copy-start(f32[1,256,256]{2,1,0:T(8,128)} %get-tuple-element.33) | copy-start | bytes 786436
  188.1 14.7 %all-to-all-start.3 = ((f32[8,128,128]{2,1,0:T(8,128)}), f32[8,128,128]{2,1,0:T(8,128)}, u32[]{:S(2)}, u32[]{:S(2)}) async-start(f32[8,128,128]{2,1,0:T(8,128)} %bitcast.145), calls=%async_computation.3 | async-start | bytes 1048576 | tf_op jit(solution)/shard_map/all_to_all | solution.py:91
  192.9 17.9 %copy-start.2 = (f32[64,4096]{1,0:T(8,128)}, f32[64,4096]{1,0:T(8,128)S(1)}, u32[]{:S(2)}) copy-start(f32[64,4096]{1,0:T(8,128)S(1)} %collective-permute-done.20.refs_8_.refs_3_) | copy-start | bytes 3145732
  192.9 16.4 %collective-permute-start.21 = (f32[32,4096]{1,0:T(8,128)S(1)}, f32[32,4096]{1,0:T(8,128)S(1)}, u32[]{:S(2)}, u32[]{:S(2)}) collective-permute-start(f32[32,4096]{1,0:T(8,128)S(1)} %slice.138), channel_id=1, source_target_pairs={{0,2},{1,7},{2,4},{3,1},{4,6},{5,3},{6,0},{7,5},{8,10},{9,15},{10,... | collective-permute-start | bytes 1572872 | tf_op jit(solution)/shard_map/ppermute | solution.py:36
  193.7 28.4 %collective-permute-start.22 = (f32[64,4096]{1,0:T(8,128)S(1)}, f32[64,4096]{1,0:T(8,128)}, u32[]{:S(2)}, u32[]{:S(2)}) collective-permute-start(f32[64,4096]{1,0:T(8,128)S(1)} %collective-permute-done.20.refs_8_.refs_3_), channel_id=1, source_target_pairs={{0,1},{1,0},{2,3},{3,2},{4,5},{5,4},{6,7},{7,6},{8,9},{9,8},{10,11... | collective-permute-start | bytes 3145736 | tf_op jit(solution)/shard_map/ppermute | solution.py:28
  204.8 13.7 %all-to-all-start.4 = ((f32[8,128,128]{2,1,0:T(8,128)}), f32[8,128,128]{2,1,0:T(8,128)}, u32[]{:S(2)}, u32[]{:S(2)}) async-start(f32[8,128,128]{2,1,0:T(8,128)} %broadcast_in_dim.5), calls=%async_computation.4 | async-start | bytes 1048576 | tf_op jit(solution)/shard_map/all_to_all | solution.py:98
  209.3 12.7 %collective-permute-start.23 = (f32[32,4096]{1,0:T(8,128)S(1)}, f32[32,4096]{1,0:T(8,128)S(1)}, u32[]{:S(2)}, u32[]{:S(2)}) collective-permute-start(f32[32,4096]{1,0:T(8,128)S(1)} %collective-permute-done.21.refs_9_.refs_4_), channel_id=1, source_target_pairs={{0,1},{1,0},{2,3},{3,2},{4,5},{5,4},{6,7},{7,6},{8,9},{9,8},{10,11... | collective-permute-start | bytes 1572872 | tf_op jit(solution)/shard_map/ppermute | solution.py:28
  230.1 16.1 %copy-start.1 = (f32[64,4096]{1,0:T(8,128)S(1)}, f32[64,4096]{1,0:T(8,128)}, u32[]{:S(2)}) copy-start(f32[64,4096]{1,0:T(8,128)} %copy-done) | copy-start | bytes 3145732
  230.1 16.1 %copy-start.3 = (f32[64,4096]{1,0:T(8,128)S(1)}, f32[64,4096]{1,0:T(8,128)}, u32[]{:S(2)}) copy-start(f32[64,4096]{1,0:T(8,128)} %copy-done.2) | copy-start | bytes 3145732
  230.1 5.2 %collective-permute-start.24 = (f32[256,128]{1,0:T(8,128)S(1)}, f32[256,128]{1,0:T(8,128)S(1)}, u32[]{:S(2)}, u32[]{:S(2)}) collective-permute-start(f32[256,128]{1,0:T(8,128)S(1)} %get-tuple-element.32), channel_id=1, source_target_pairs={{0,128},{128,0},{1,129},{129,1},{2,130},{130,2},{3,131},{131,3},{4... | collective-permute-start | bytes 393224 | tf_op jit(solution)/shard_map/ppermute | solution.py:28
  235.4 6.7 %collective-permute-start.27 = (f32[256,128]{1,0:T(8,128)S(1)}, f32[256,128]{1,0:T(8,128)S(1)}, u32[]{:S(2)}, u32[]{:S(2)}) collective-permute-start(f32[256,128]{1,0:T(8,128)S(1)} %add.630), channel_id=1, source_target_pairs={{0,96},{32,0},{64,32},{96,64},{1,97},{33,1},{65,33},{97,65},{2,98}... | collective-permute-start | bytes 393224 | tf_op jit(solution)/shard_map/ppermute | solution.py:28
  237.1 7.3 %collective-permute-start.26 = (f32[256,128]{1,0:T(8,128)S(1)}, f32[256,128]{1,0:T(8,128)S(1)}, u32[]{:S(2)}, u32[]{:S(2)}) collective-permute-start(f32[256,128]{1,0:T(8,128)S(1)} %add.630), channel_id=1, source_target_pairs={{0,64},{32,96},{64,0},{96,32},{1,65},{33,97},{65,1},{97,33},{2,66}... | collective-permute-start | bytes 393224 | tf_op jit(solution)/shard_map/ppermute | solution.py:28
  238.6 7.1 %collective-permute-start.25 = (f32[256,128]{1,0:T(8,128)S(1)}, f32[256,128]{1,0:T(8,128)S(1)}, u32[]{:S(2)}, u32[]{:S(2)}) collective-permute-start(f32[256,128]{1,0:T(8,128)S(1)} %add.630), channel_id=1, source_target_pairs={{0,32},{32,64},{64,96},{96,0},{1,33},{33,65},{65,97},{97,1},{2,34}... | collective-permute-start | bytes 393224 | tf_op jit(solution)/shard_map/ppermute | solution.py:28
  (9 other events, 11.1 us)

commit v3 on v2

--- a/solution.py
+++ b/solution.py
@@ -242,9 +242,9 @@
     v43, v21 = jnp.concatenate([v[4], v[3]], 0), jnp.concatenate([v[2], v[1]], 0)
     full43, _ = gather_z(v43, swap(v43))
     cur = exchange(eigvecs)
-    pieces43 = gather_x(full43, (), (cur,))
+    pieces43 = gather_x(full43, (), ())
     near43, far43 = pieces43[1:3]
-    full21, _ = gather_z(v21, swap(v21), (full43,), (near43, cur), (far43,))
+    full21, _ = gather_z(v21, swap(v21), (full43,), (near43, cur), ())
     (w,) = work(cur, None, (), pieces43)
     share = row_share(w)
     pieces21 = gather_x(full21, (far43,), (share,))

time: 252 us -> 251 us (level)
  waiting for transfers between devices: 125 us -> 113 us
  starting transfers between devices: 54.4 us -> 62.6 us
    ppermute x12, waiting for transfers between devices: 87.7 us -> 80.8 us  [both_ways(): return lax.ppermute(a, (axis, 'core'), pairs)]
    ppermute x12, starting transfers between devices: 15.5 us -> 21.9 us  [both_ways(): return lax.ppermute(a, (axis, 'core'), pairs)]
    all_to_all x2, waiting for transfers between devices: 18 us -> 14.3 us  [row_share(): lax.all_to_all(a.reshape(8, n // 8, width), ROW, split_axis=0, concat_axi...]
    unnamed x48 -> x56, local copies, waits for them, and re-layouts: 6.98 us -> 7.37 us
where the time goes in v3:
time: 251 us; the launch traced here: 249 us
  waiting for transfers between devices  113 us (45%)
  starting transfers between devices  62.6 us (25%)
  Pallas kernels  36.8 us (15%)
  local copies, waits for them, and re-layouts  22.2 us (9%)
  other arithmetic  8.3 us (3%)
  matrix products  6.11 us (2%)
    ppermute x12, waiting for transfers between devices, both_ways(): return lax.ppermute(a, (axis, 'core'), pairs)  80.8 us
    pallas_call x4, Pallas kernels, work(): pl.pallas_call(functools.partial(work_kernel, bool(old), bool(new)), grid...  31.3 us
    ppermute x12, starting transfers between devices, both_ways(): return lax.ppermute(a, (axis, 'core'), pairs)  21.9 us
    all_to_all x2, waiting for transfers between devices, row_share(): lax.all_to_all(a.reshape(8, n // 8, width), ROW, split_axis=0, concat_axi...  14.3 us
    all_to_all x2, starting transfers between devices, row_share(): lax.all_to_all(a.reshape(8, n // 8, width), ROW, split_axis=0, concat_axi...  14.2 us
    ppermute x16, waiting for transfers between devices, shift(): return lax.ppermute(a, axis, [(i, (i + by) % n) for i in range(n)])  11.6 us
    all_to_all x2, starting transfers between devices, hand_on(): lax.all_to_all(a, ROW, split_axis=0, concat_axis=0, tiled=True)  9.7 us
    all_to_all x1, starting transfers between devices, exchange(): lax.all_to_all(eigvecs.T.reshape(32, K, 128), COL, split_axis=0, concat_a...  8.66 us
  transfers between devices with their start and end apart: 33, of which 15 were waited for; matrix products, arithmetic and copies ran while one was open for 10% of the time, Pallas kernels for 9%

profile of v3, /device:TPU:32, one launch (start us, length us, event | category | flops | bytes accessed | tf_op | source)
XLA Modules:
  0.0 249.3 jit_solution(6737633646377005026)
XLA Ops:
  0.0 2.0 slice_bitcast_fusion.17
  2.2 1.5 collective-permute-done
  4.4 3.3 %collective-permute-start.1 = (f32[32,4096]{1,0:T(8,128)S(1)}, f32[32,4096]{1,0:T(8,128)S(1)}, u32[]{:S(2)}, u32[]{:S(2)}) collective-permute-start(f32[32,4096]{1,0:T(8,128)S(1)} %pad_maximum_fusion.9), channel_id=1, source_target_pairs={{0,8},{1,25},{8,16},{9,1},{16,24},{17,9},{24,0},{25,17},{2,10},{3,... | collective-permute-start | bytes 1572872 | tf_op jit(solution)/shard_map/ppermute | solution.py:36
  7.8 14.9 %collective-permute-done.1 = f32[32,4096]{1,0:T(8,128)S(1)} collective-permute-done((f32[32,4096]{1,0:T(8,128)S(1)}, f32[32,4096]{1,0:T(8,128)S(1)}, u32[]{:S(2)}, u32[]{:S(2)}) %collective-permute-start.1) | collective-permute-done | bytes 524320 | tf_op jit(solution)/shard_map/ppermute | solution.py:36
  24.0 1.8 copy.21
  25.8 8.7 %all-to-all-start = ((f32[32,128,128]{2,1,0:T(8,128)}), f32[32,128,128]{2,1,0:T(8,128)S(1)}, u32[]{:S(2)}, u32[]{:S(2)}) async-start(f32[32,128,128]{2,1,0:T(8,128)} %bitcast.146), calls=%async_computation | async-start | bytes 4194304 | tf_op jit(solution)/shard_map/all_to_all | solution.py:86
  37.3 1.9 collective-permute-start.4
  39.9 2.4 collective-permute-start.9
  42.3 38.0 %collective-permute-done.9 = f32[32,4096]{1,0:T(8,128)S(1)} collective-permute-done((f32[32,4096]{1,0:T(8,128)S(1)}, f32[32,4096]{1,0:T(8,128)S(1)}, u32[]{:S(2)}, u32[]{:S(2)}) %collective-permute-start.9) | collective-permute-done | bytes 524320 | tf_op jit(solution)/shard_map/ppermute | solution.py:36
  81.1 2.5 %collective-permute-done.4.refs_2_.refs_3_ = f32[128,4096]{1,0:T(8,128)} collective-permute-done((f32[128,4096]{1,0:T(8,128)S(1)}, f32[128,4096]{1,0:T(8,128)}, u32[]{:S(2)}, u32[]{:S(2)}) %collective-permute-start.4) | collective-permute-done | bytes 2097184 | tf_op jit(solution)/shard_map/ppermute | solution.py:36
  83.6 2.4 collective-permute-start.10
  86.0 2.3 slice.123
  88.3 18.1 %collective-permute-done.10 = f32[16,4096]{1,0:T(8,128)S(1)} collective-permute-done((f32[16,4096]{1,0:T(8,128)}, f32[16,4096]{1,0:T(8,128)S(1)}, u32[]{:S(2)}, u32[]{:S(2)}) %collective-permute-start.10) | collective-permute-done | bytes 262176 | tf_op jit(solution)/shard_map/ppermute | solution.py:36
  110.3 1.2 slice_bitcast_fusion.2
  111.5 1.5 pad_maximum_fusion.1.refs_7_.refs_2_
  113.0 1.1 collective-permute-start.12
  116.9 3.4 %collective-permute-start.17 = (f32[16,4096]{1,0:T(8,128)S(1)}, f32[16,4096]{1,0:T(8,128)S(1)}, u32[]{:S(2)}, u32[]{:S(2)}) collective-permute-start(f32[16,4096]{1,0:T(8,128)S(1)} %pad_maximum_fusion.14), channel_id=1, source_target_pairs={{0,8},{1,25},{8,16},{9,1},{16,24},{17,9},{24,0},{25,17},{2,10},{3,... | collective-permute-start | bytes 786440 | tf_op jit(solution)/shard_map/ppermute | solution.py:36
  120.3 8.0 %work.4 = f32[1024,128]{1,0:T(8,128)} custom-call(f32[32,128,128]{2,1,0:T(8,128)} %copy-done.11, f32[128,4096]{1,0:T(8,128)} %copy-done.12, f32[128,4096]{1,0:T(8,128)} %collective-permute-done.4.refs_2_.refs_3_, f32[64,4096]{1,0:T(8,128)S(1)} %collective-permute-done.5.refs_3_.refs_4_, f32[128,4096]{1,0:T(8,128)} %collective-permute-done.6.refs_4_.refs_5_, ...), custom_call_target="tpu_custom_call" | custom-call | flops 1610612736 | bytes 12582912 | tf_op jit(solution)/shard_map/work/pallas_call | solution.py:201
  128.3 9.2 %all-to-all-start.1 = ((f32[8,128,128]{2,1,0:T(8,128)}), f32[8,128,128]{2,1,0:T(8,128)S(1)}, u32[]{:S(2)}, u32[]{:S(2)}) async-start(f32[8,128,128]{2,1,0:T(8,128)} %bitcast.56), calls=%async_computation.1 | async-start | bytes 1048576 | tf_op jit(solution)/shard_map/all_to_all | solution.py:91
  138.0 6.7 %all-to-all-done.1 = f32[8,128,128]{2,1,0:T(8,128)S(1)} async-done(((f32[8,128,128]{2,1,0:T(8,128)}), f32[8,128,128]{2,1,0:T(8,128)S(1)}, u32[]{:S(2)}, u32[]{:S(2)}) %all-to-all-start.1) | async-done | bytes 524320 | tf_op jit(solution)/shard_map/all_to_all | solution.py:91
  144.7 4.8 %collective-permute-start.18 = (f32[8,4096]{1,0:T(8,128)S(1)}, f32[8,4096]{1,0:T(8,128)S(1)}, u32[]{:S(2)}, u32[]{:S(2)}) collective-permute-start(f32[8,4096]{1,0:T(8,128)S(1)} %get-tuple-element.24), channel_id=1, source_target_pairs={{0,8},{1,25},{8,16},{9,1},{16,24},{17,9},{24,0},{25,17},{2,10},{3,... | collective-permute-start | bytes 393224 | tf_op jit(solution)/shard_map/ppermute | solution.py:36
  149.5 2.3 slice.131
  152.1 1.3 fusion.15.t_ref
  154.2 5.1 %all-to-all-start.2 = ((f32[8,128,128]{2,1,0:T(8,128)}), f32[8,128,128]{2,1,0:T(8,128)}, u32[]{:S(2)}, u32[]{:S(2)}) async-start(f32[8,128,128]{2,1,0:T(8,128)} %broadcast_in_dim.4), calls=%async_computation.2 | async-start | bytes 1048576 | tf_op jit(solution)/shard_map/all_to_all | solution.py:98
  159.3 1.3 collective-permute-start.19
  160.8 7.3 %collective-permute-done.13.refs_9_.refs_4_ = f32[64,4096]{1,0:T(8,128)S(1)} collective-permute-done((f32[64,4096]{1,0:T(8,128)}, f32[64,4096]{1,0:T(8,128)S(1)}, u32[]{:S(2)}, u32[]{:S(2)}) %collective-permute-start.13) | collective-permute-done | bytes 1048608 | tf_op jit(solution)/shard_map/ppermute | solution.py:36
  169.2 1.3 copy-done.8
  170.5 2.5 %solve.3.refs_1_ = f32[128,512]{1,0:T(8,128)S(1)} custom-call(f32[2,256,256]{2,1,0:T(8,128)S(1)} %copy-done.8, f32[1024,128]{1,0:T(8,128)} %bitcast.57.w_ref), custom_call_target="tpu_custom_call" | custom-call | flops 201326592 | bytes 1048576 | tf_op jit(solution)/shard_map/solve/pallas_call | solution.py:230
  173.1 1.2 copy-done.5
  174.3 1.2 copy-done.7
  175.5 10.4 %work.5 = (f32[128,4096]{1,0:T(8,128)}, f32[1024,128]{1,0:T(8,128)S(1)}) custom-call(f32[32,128,128]{2,1,0:T(8,128)} %copy-done.11, f32[128,512]{1,0:T(8,128)S(1)} %solve.3.refs_1_, f32[128,4096]{1,0:T(8,128)} %copy-done.12, f32[128,4096]{1,0:T(8,128)} %collective-permute-done.4.refs_2_.refs_3_, f32[64,4096]{1,0:T(8,128)S(1)} %copy-done.5, ...), custom_call_target="tpu_custom_call" | custom-call | flops 3221225472 | bytes 20971520 | tf_op jit(solution)/shard_map/work/pallas_call | solution.py:201
  186.8 5.0 %all-to-all-start.3 = ((f32[8,128,128]{2,1,0:T(8,128)}), f32[8,128,128]{2,1,0:T(8,128)}, u32[]{:S(2)}, u32[]{:S(2)}) async-start(f32[8,128,128]{2,1,0:T(8,128)} %bitcast.145), calls=%async_computation.3 | async-start | bytes 1048576 | tf_op jit(solution)/shard_map/all_to_all | solution.py:91
  191.9 1.8 collective-permute-start.21
  193.9 7.6 %all-to-all-done.3 = f32[8,128,128]{2,1,0:T(8,128)} async-done(((f32[8,128,128]{2,1,0:T(8,128)}), f32[8,128,128]{2,1,0:T(8,128)}, u32[]{:S(2)}, u32[]{:S(2)}) %all-to-all-start.3) | async-done | bytes 524320 | tf_op jit(solution)/shard_map/all_to_all | solution.py:91
  203.5 4.6 %all-to-all-start.4 = ((f32[8,128,128]{2,1,0:T(8,128)}), f32[8,128,128]{2,1,0:T(8,128)}, u32[]{:S(2)}, u32[]{:S(2)}) async-start(f32[8,128,128]{2,1,0:T(8,128)} %broadcast_in_dim.5), calls=%async_computation.4 | async-start | bytes 1048576 | tf_op jit(solution)/shard_map/all_to_all | solution.py:98
  208.1 1.4 fusion.4
  209.5 1.3 fusion.12.t_ref
  210.8 5.9 %all-to-all-done.4 = f32[8,128,128]{2,1,0:T(8,128)} async-done(((f32[8,128,128]{2,1,0:T(8,128)}), f32[8,128,128]{2,1,0:T(8,128)}, u32[]{:S(2)}, u32[]{:S(2)}) %all-to-all-start.4) | async-done | bytes 524320 | tf_op jit(solution)/shard_map/all_to_all | solution.py:98
  217.8 2.5 %solve.4.refs_1_ = f32[128,512]{1,0:T(8,128)S(1)} custom-call(f32[2,256,256]{2,1,0:T(8,128)S(1)} %copy-done.9, f32[1024,128]{1,0:T(8,128)} %bitcast.79.w_ref), custom_call_target="tpu_custom_call" | custom-call | flops 201326592 | bytes 1048576 | tf_op jit(solution)/shard_map/solve/pallas_call | solution.py:230
  220.3 8.0 %work.6 = (f32[128,4096]{1,0:T(8,128)}, f32[256,128]{1,0:T(8,128)S(1)}) custom-call(f32[128,4096]{1,0:T(8,128)} %get-tuple-element.21.refs_0_, f32[128,512]{1,0:T(8,128)S(1)} %solve.4.refs_1_, f32[128,4096]{1,0:T(8,128)} %pad_maximum_fusion.1.refs_7_.refs_2_, f32[128,4096]{1,0:T(8,128)} %collective-permute-done.12.refs_8_.refs_3_, ...), custom_call_target="tpu_custom_call" | custom-call | flops 2415919104 | bytes 16777216 | tf_op jit(solution)/shard_map/work/pallas_call | solution.py:201
  229.4 4.0 %collective-permute-done.24 = f32[256,128]{1,0:T(8,128)S(1)} collective-permute-done((f32[256,128]{1,0:T(8,128)S(1)}, f32[256,128]{1,0:T(8,128)S(1)}, u32[]{:S(2)}, u32[]{:S(2)}) %collective-permute-start.24) | collective-permute-done | bytes 131104 | tf_op jit(solution)/shard_map/ppermute | solution.py:28
  233.4 1.9 collective-permute-start.27
  235.3 1.5 collective-permute-start.26
  236.8 1.3 fusion.8
  238.5 1.7 collective-permute-done.27
  240.2 2.3 collective-permute-done.26
  242.5 1.3 collective-permute-done.25
  244.4 4.9 %work.7 = f32[4096,128]{1,0:T(8,128)} custom-call(f32[128,4096]{1,0:T(8,128)} %get-tuple-element.27.refs_0_, f32[128,256]{1,0:T(8,128)S(1)} %solve.5.refs_1_, f32[64,4096]{1,0:T(8,128)S(1)} %copy-done.1, f32[64,4096]{1,0:T(8,128)S(1)} %copy-done.3, f32[32,4096]{1,0:T(8,128)S(1)} %collective-permute-done.21.refs_9_.refs_4_, ...), custom_call_target="tpu_custom_call" | custom-call | flops 805306368 | bytes 8388608 | tf_op jit(solution)/shard_map/work/pallas_call | solution.py:201
  (126 shorter events, 21.9 us)
Async XLA Ops:
  0.0 24.0 %copy-start.13 = (f32[128,4096]{1,0:T(8,128)S(1)}, f32[128,4096]{1,0:T(8,128)}, u32[]{:S(2)}) copy-start(f32[128,4096]{1,0:T(8,128)} %param.3) | copy-start | bytes 6291460
  2.1 1.6 collective-permute-start
  4.4 18.3 %collective-permute-start.1 = (f32[32,4096]{1,0:T(8,128)S(1)}, f32[32,4096]{1,0:T(8,128)S(1)}, u32[]{:S(2)}, u32[]{:S(2)}) collective-permute-start(f32[32,4096]{1,0:T(8,128)S(1)} %pad_maximum_fusion.9), channel_id=1, source_target_pairs={{0,8},{1,25},{8,16},{9,1},{16,24},{17,9},{24,0},{25,17},{2,10},{3,... | collective-permute-start | bytes 1572872 | tf_op jit(solution)/shard_map/ppermute | solution.py:36
  23.6 10.9 %collective-permute-start.2 = (f32[16,4096]{1,0:T(8,128)}, f32[16,4096]{1,0:T(8,128)S(1)}, u32[]{:S(2)}, u32[]{:S(2)}) collective-permute-start(f32[16,4096]{1,0:T(8,128)} %get-tuple-element.50), channel_id=1, source_target_pairs={{0,8},{1,25},{8,16},{9,1},{16,24},{17,9},{24,0},{25,17},{2,10},{3,... | collective-permute-start | bytes 786440 | tf_op jit(solution)/shard_map/ppermute | solution.py:36
  25.8 57.8 %all-to-all-start = ((f32[32,128,128]{2,1,0:T(8,128)}), f32[32,128,128]{2,1,0:T(8,128)S(1)}, u32[]{:S(2)}, u32[]{:S(2)}) async-start(f32[32,128,128]{2,1,0:T(8,128)} %bitcast.146), calls=%async_computation | async-start | bytes 4194304 | tf_op jit(solution)/shard_map/all_to_all | solution.py:86
  34.6 2.4 collective-permute-start.3
  35.2 3.9 %collective-permute-start.8 = (f32[16,4096]{1,0:T(8,128)S(1)}, f32[16,4096]{1,0:T(8,128)S(1)}, u32[]{:S(2)}, u32[]{:S(2)}) collective-permute-start(f32[16,4096]{1,0:T(8,128)S(1)} %get-tuple-element.58), channel_id=1, source_target_pairs={{0,1},{1,0},{2,3},{3,2},{4,5},{5,4},{6,7},{7,6},{8,9},{9,8},{10,11... | collective-permute-start | bytes 786440 | tf_op jit(solution)/shard_map/ppermute | solution.py:28
  37.3 43.8 %copy-start.12 = (f32[128,4096]{1,0:T(8,128)}, f32[128,4096]{1,0:T(8,128)S(1)}, u32[]{:S(2)}) copy-start(f32[128,4096]{1,0:T(8,128)S(1)} %pad_maximum_fusion.refs_1_.refs_2_) | copy-start | bytes 6291460
  37.3 46.3 %collective-permute-start.4 = (f32[128,4096]{1,0:T(8,128)S(1)}, f32[128,4096]{1,0:T(8,128)}, u32[]{:S(2)}, u32[]{:S(2)}) collective-permute-start(f32[128,4096]{1,0:T(8,128)S(1)} %pad_maximum_fusion.refs_1_.refs_2_), channel_id=1, source_target_pairs={{0,2},{1,7},{2,4},{3,1},{4,6},{5,3},{6,0},{7,5},{8,10},{9,15},{10,... | collective-permute-start | bytes 6291464 | tf_op jit(solution)/shard_map/ppermute | solution.py:36
  39.9 40.4 %collective-permute-start.9 = (f32[32,4096]{1,0:T(8,128)S(1)}, f32[32,4096]{1,0:T(8,128)S(1)}, u32[]{:S(2)}, u32[]{:S(2)}) collective-permute-start(f32[32,4096]{1,0:T(8,128)S(1)} %pad_maximum_fusion.10), channel_id=1, source_target_pairs={{0,8},{1,25},{8,16},{9,1},{16,24},{17,9},{24,0},{25,17},{2,10},{3,... | collective-permute-start | bytes 1572872 | tf_op jit(solution)/shard_map/ppermute | solution.py:36
  83.6 22.8 %collective-permute-start.10 = (f32[16,4096]{1,0:T(8,128)}, f32[16,4096]{1,0:T(8,128)S(1)}, u32[]{:S(2)}, u32[]{:S(2)}) collective-permute-start(f32[16,4096]{1,0:T(8,128)} %get-tuple-element.18), channel_id=1, source_target_pairs={{0,8},{1,25},{8,16},{9,1},{16,24},{17,9},{24,0},{25,17},{2,10},{3,... | collective-permute-start | bytes 786440 | tf_op jit(solution)/shard_map/ppermute | solution.py:36
  88.3 21.0 %collective-permute-start.5 = (f32[64,4096]{1,0:T(8,128)}, f32[64,4096]{1,0:T(8,128)S(1)}, u32[]{:S(2)}, u32[]{:S(2)}) collective-permute-start(f32[64,4096]{1,0:T(8,128)} %slice.123), channel_id=1, source_target_pairs={{0,2},{1,7},{2,4},{3,1},{4,6},{5,3},{6,0},{7,5},{8,10},{9,15},{10,... | collective-permute-start | bytes 3145736 | tf_op jit(solution)/shard_map/ppermute | solution.py:36
  107.4 4.0 %copy-start.21 = (f32[16,4096]{1,0:T(8,128)S(1)}, f32[16,4096]{1,0:T(8,128)}, u32[]{:S(2)}) copy-start(f32[16,4096]{1,0:T(8,128)} %copy-done.20) | copy-start | bytes 786436
  107.5 2.8 %collective-permute-start.11 = (f32[48,4096]{1,0:T(8,128)}, f32[48,4096]{1,0:T(8,128)}, u32[]{:S(2)}, u32[]{:S(2)}) collective-permute-start(f32[48,4096]{1,0:T(8,128)} %pad_maximum_fusion.8), channel_id=1, source_target_pairs={{0,1},{1,0},{2,3},{3,2},{4,5},{5,4},{6,7},{7,6},{8,9},{9,8},{10,11... | collective-permute-start | bytes 2359304 | tf_op jit(solution)/shard_map/ppermute | solution.py:28
  107.5 8.5 %collective-permute-start.16 = (f32[8,4096]{1,0:T(8,128)S(1)}, f32[8,4096]{1,0:T(8,128)}, u32[]{:S(2)}, u32[]{:S(2)}) collective-permute-start(f32[8,4096]{1,0:T(8,128)S(1)} %get-tuple-element.40), channel_id=1, source_target_pairs={{0,1},{1,0},{2,3},{3,2},{4,5},{5,4},{6,7},{7,6},{8,9},{9,8},{10,11... | collective-permute-start | bytes 393224 | tf_op jit(solution)/shard_map/ppermute | solution.py:28
  108.1 12.2 %collective-permute-start.6 = (f32[128,4096]{1,0:T(8,128)}, f32[128,4096]{1,0:T(8,128)}, u32[]{:S(2)}, u32[]{:S(2)}) collective-permute-start(f32[128,4096]{1,0:T(8,128)} %collective-permute-done.4.refs_2_.refs_3_), channel_id=1, source_target_pairs={{0,1},{1,0},{2,3},{3,2},{4,5},{5,4},{6,7},{7,6},{8,9},{9,8},{10,11... | collective-permute-start | bytes 6291464 | tf_op jit(solution)/shard_map/ppermute | solution.py:28
  109.3 11.0 %copy-start.4 = (f32[64,4096]{1,0:T(8,128)}, f32[64,4096]{1,0:T(8,128)S(1)}, u32[]{:S(2)}) copy-start(f32[64,4096]{1,0:T(8,128)S(1)} %collective-permute-done.5.refs_3_.refs_4_) | copy-start | bytes 3145732
  109.3 11.0 %collective-permute-start.7 = (f32[64,4096]{1,0:T(8,128)S(1)}, f32[64,4096]{1,0:T(8,128)S(1)}, u32[]{:S(2)}, u32[]{:S(2)}) collective-permute-start(f32[64,4096]{1,0:T(8,128)S(1)} %collective-permute-done.5.refs_3_.refs_4_), channel_id=1, source_target_pairs={{0,1},{1,0},{2,3},{3,2},{4,5},{5,4},{6,7},{7,6},{8,9},{9,8},{10,11... | collective-permute-start | bytes 3145736 | tf_op jit(solution)/shard_map/ppermute | solution.py:28
  111.5 3.4 %copy-start.14 = (f32[5,256,256]{2,1,0:T(8,128)S(1)}, f32[5,256,256]{2,1,0:T(8,128)}, u32[]{:S(2)}) copy-start(f32[5,256,256]{2,1,0:T(8,128)} %param.5) | copy-start | bytes 3932164
  113.0 36.5 %collective-permute-start.12 = (f32[128,4096]{1,0:T(8,128)}, f32[128,4096]{1,0:T(8,128)}, u32[]{:S(2)}, u32[]{:S(2)}) collective-permute-start(f32[128,4096]{1,0:T(8,128)} %pad_maximum_fusion.1.refs_7_.refs_2_), channel_id=1, source_target_pairs={{0,2},{1,7},{2,4},{3,1},{4,6},{5,3},{6,0},{7,5},{8,10},{9,15},{10,... | collective-permute-start | bytes 6291464 | tf_op jit(solution)/shard_map/ppermute | solution.py:36
  116.8 20.6 %copy-start.18 = (f32[1,256,256]{2,1,0:T(8,128)S(1)}, f32[1,256,256]{2,1,0:T(8,128)}, u32[]{:S(2)}) copy-start(f32[1,256,256]{2,1,0:T(8,128)} %get-tuple-element.30) | copy-start | bytes 786436
  116.9 20.6 %copy-start.19 = (f32[1,256,256]{2,1,0:T(8,128)S(1)}, f32[1,256,256]{2,1,0:T(8,128)}, u32[]{:S(2)}) copy-start(f32[1,256,256]{2,1,0:T(8,128)} %get-tuple-element.31) | copy-start | bytes 786436
  116.9 20.6 %copy-start.27 = (s32[256]{0:T(256)S(1)}, s32[256]{0:T(256)}, u32[]{:S(2)}) copy-start(s32[256]{0:T(256)} %add.629) | copy-start | bytes 3076
  116.9 21.1 %collective-permute-start.17 = (f32[16,4096]{1,0:T(8,128)S(1)}, f32[16,4096]{1,0:T(8,128)S(1)}, u32[]{:S(2)}, u32[]{:S(2)}) collective-permute-start(f32[16,4096]{1,0:T(8,128)S(1)} %pad_maximum_fusion.14), channel_id=1, source_target_pairs={{0,8},{1,25},{8,16},{9,1},{16,24},{17,9},{24,0},{25,17},{2,10},{3,... | collective-permute-start | bytes 786440 | tf_op jit(solution)/shard_map/ppermute | solution.py:36
  120.3 8.0 %copy-start.6 = (f32[64,4096]{1,0:T(8,128)}, f32[64,4096]{1,0:T(8,128)S(1)}, u32[]{:S(2)}) copy-start(f32[64,4096]{1,0:T(8,128)S(1)} %collective-permute-done.7.refs_5_.refs_6_) | copy-start | bytes 3145732
  128.3 16.4 %all-to-all-start.1 = ((f32[8,128,128]{2,1,0:T(8,128)}), f32[8,128,128]{2,1,0:T(8,128)S(1)}, u32[]{:S(2)}, u32[]{:S(2)}) async-start(f32[8,128,128]{2,1,0:T(8,128)} %bitcast.56), calls=%async_computation.1 | async-start | bytes 1048576 | tf_op jit(solution)/shard_map/all_to_all | solution.py:91
  144.7 14.6 %collective-permute-start.18 = (f32[8,4096]{1,0:T(8,128)S(1)}, f32[8,4096]{1,0:T(8,128)S(1)}, u32[]{:S(2)}, u32[]{:S(2)}) collective-permute-start(f32[8,4096]{1,0:T(8,128)S(1)} %get-tuple-element.24), channel_id=1, source_target_pairs={{0,8},{1,25},{8,16},{9,1},{16,24},{17,9},{24,0},{25,17},{2,10},{3,... | collective-permute-start | bytes 393224 | tf_op jit(solution)/shard_map/ppermute | solution.py:36
  151.8 8.9 %copy-start.26 = (f32[1,1,8,4096]{3,2,1,0:T(8,128)S(1)}, f32[1,1,8,4096]{3,2,1,0:T(8,128)}, u32[]{:S(2)}) copy-start(f32[1,1,8,4096]{3,2,1,0:T(8,128)} %get-tuple-element.39) | copy-start | bytes 393220
  151.8 16.2 %collective-permute-start.13 = (f32[64,4096]{1,0:T(8,128)}, f32[64,4096]{1,0:T(8,128)S(1)}, u32[]{:S(2)}, u32[]{:S(2)}) collective-permute-start(f32[64,4096]{1,0:T(8,128)} %slice.131), channel_id=1, source_target_pairs={{0,2},{1,7},{2,4},{3,1},{4,6},{5,3},{6,0},{7,5},{8,10},{9,15},{10,... | collective-permute-start | bytes 3145736 | tf_op jit(solution)/shard_map/ppermute | solution.py:36
  154.2 15.0 %all-to-all-start.2 = ((f32[8,128,128]{2,1,0:T(8,128)}), f32[8,128,128]{2,1,0:T(8,128)}, u32[]{:S(2)}, u32[]{:S(2)}) async-start(f32[8,128,128]{2,1,0:T(8,128)} %broadcast_in_dim.4), calls=%async_computation.2 | async-start | bytes 1048576 | tf_op jit(solution)/shard_map/all_to_all | solution.py:98
  159.3 8.7 %collective-permute-start.19 = (f32[24,4096]{1,0:T(8,128)S(1)}, f32[24,4096]{1,0:T(8,128)S(1)}, u32[]{:S(2)}, u32[]{:S(2)}) collective-permute-start(f32[24,4096]{1,0:T(8,128)S(1)} %pad_maximum_fusion.11), channel_id=1, source_target_pairs={{0,1},{1,0},{2,3},{3,2},{4,5},{5,4},{6,7},{7,6},{8,9},{9,8},{10,11... | collective-permute-start | bytes 1179656 | tf_op jit(solution)/shard_map/ppermute | solution.py:28
  160.6 12.5 %collective-permute-start.14 = (f32[128,4096]{1,0:T(8,128)}, f32[128,4096]{1,0:T(8,128)}, u32[]{:S(2)}, u32[]{:S(2)}) collective-permute-start(f32[128,4096]{1,0:T(8,128)} %collective-permute-done.12.refs_8_.refs_3_), channel_id=1, source_target_pairs={{0,1},{1,0},{2,3},{3,2},{4,5},{5,4},{6,7},{7,6},{8,9},{9,8},{10,11... | collective-permute-start | bytes 6291464 | tf_op jit(solution)/shard_map/ppermute | solution.py:28
  168.0 5.0 %collective-permute-start.15 = (f32[64,4096]{1,0:T(8,128)S(1)}, f32[64,4096]{1,0:T(8,128)}, u32[]{:S(2)}, u32[]{:S(2)}) collective-permute-start(f32[64,4096]{1,0:T(8,128)S(1)} %collective-permute-done.13.refs_9_.refs_4_), channel_id=1, source_target_pairs={{0,1},{1,0},{2,3},{3,2},{4,5},{5,4},{6,7},{7,6},{8,9},{9,8},{10,11... | collective-permute-start | bytes 3145736 | tf_op jit(solution)/shard_map/ppermute | solution.py:28
  169.1 16.9 %copy-start = (f32[64,4096]{1,0:T(8,128)}, f32[64,4096]{1,0:T(8,128)S(1)}, u32[]{:S(2)}) copy-start(f32[64,4096]{1,0:T(8,128)S(1)} %pad_maximum_fusion.6.refs_7_.refs_2_) | copy-start | bytes 3145732
  169.1 22.7 %collective-permute-start.20 = (f32[64,4096]{1,0:T(8,128)S(1)}, f32[64,4096]{1,0:T(8,128)S(1)}, u32[]{:S(2)}, u32[]{:S(2)}) collective-permute-start(f32[64,4096]{1,0:T(8,128)S(1)} %pad_maximum_fusion.6.refs_7_.refs_2_), channel_id=1, source_target_pairs={{0,2},{1,7},{2,4},{3,1},{4,6},{5,3},{6,0},{7,5},{8,10},{9,15},{10,... | collective-permute-start | bytes 3145736 | tf_op jit(solution)/shard_map/ppermute | solution.py:36
  186.8 21.3 %copy-start.15 = (f32[1,256,256]{2,1,0:T(8,128)S(1)}, f32[1,256,256]{2,1,0:T(8,128)}, u32[]{:S(2)}) copy-start(f32[1,256,256]{2,1,0:T(8,128)} %get-tuple-element.29) | copy-start | bytes 786436
  186.8 14.8 %all-to-all-start.3 = ((f32[8,128,128]{2,1,0:T(8,128)}), f32[8,128,128]{2,1,0:T(8,128)}, u32[]{:S(2)}, u32[]{:S(2)}) async-start(f32[8,128,128]{2,1,0:T(8,128)} %bitcast.145), calls=%async_computation.3 | async-start | bytes 1048576 | tf_op jit(solution)/shard_map/all_to_all | solution.py:91
  191.8 17.7 %copy-start.2 = (f32[64,4096]{1,0:T(8,128)}, f32[64,4096]{1,0:T(8,128)S(1)}, u32[]{:S(2)}) copy-start(f32[64,4096]{1,0:T(8,128)S(1)} %collective-permute-done.20.refs_8_.refs_3_) | copy-start | bytes 3145732
  191.9 16.2 %collective-permute-start.21 = (f32[32,4096]{1,0:T(8,128)S(1)}, f32[32,4096]{1,0:T(8,128)S(1)}, u32[]{:S(2)}, u32[]{:S(2)}) collective-permute-start(f32[32,4096]{1,0:T(8,128)S(1)} %slice.138), channel_id=1, source_target_pairs={{0,2},{1,7},{2,4},{3,1},{4,6},{5,3},{6,0},{7,5},{8,10},{9,15},{10,... | collective-permute-start | bytes 1572872 | tf_op jit(solution)/shard_map/ppermute | solution.py:36
  193.7 26.6 %collective-permute-start.22 = (f32[64,4096]{1,0:T(8,128)S(1)}, f32[64,4096]{1,0:T(8,128)}, u32[]{:S(2)}, u32[]{:S(2)}) collective-permute-start(f32[64,4096]{1,0:T(8,128)S(1)} %collective-permute-done.20.refs_8_.refs_3_), channel_id=1, source_target_pairs={{0,1},{1,0},{2,3},{3,2},{4,5},{5,4},{6,7},{7,6},{8,9},{9,8},{10,11... | collective-permute-start | bytes 3145736 | tf_op jit(solution)/shard_map/ppermute | solution.py:28
  203.5 13.2 %all-to-all-start.4 = ((f32[8,128,128]{2,1,0:T(8,128)}), f32[8,128,128]{2,1,0:T(8,128)}, u32[]{:S(2)}, u32[]{:S(2)}) async-start(f32[8,128,128]{2,1,0:T(8,128)} %broadcast_in_dim.5), calls=%async_computation.4 | async-start | bytes 1048576 | tf_op jit(solution)/shard_map/all_to_all | solution.py:98
  208.1 12.2 %collective-permute-start.23 = (f32[32,4096]{1,0:T(8,128)S(1)}, f32[32,4096]{1,0:T(8,128)S(1)}, u32[]{:S(2)}, u32[]{:S(2)}) collective-permute-start(f32[32,4096]{1,0:T(8,128)S(1)} %collective-permute-done.21.refs_9_.refs_4_), channel_id=1, source_target_pairs={{0,1},{1,0},{2,3},{3,2},{4,5},{5,4},{6,7},{7,6},{8,9},{9,8},{10,11... | collective-permute-start | bytes 1572872 | tf_op jit(solution)/shard_map/ppermute | solution.py:28
  228.3 16.0 %copy-start.1 = (f32[64,4096]{1,0:T(8,128)S(1)}, f32[64,4096]{1,0:T(8,128)}, u32[]{:S(2)}) copy-start(f32[64,4096]{1,0:T(8,128)} %copy-done) | copy-start | bytes 3145732
  228.3 16.0 %copy-start.3 = (f32[64,4096]{1,0:T(8,128)S(1)}, f32[64,4096]{1,0:T(8,128)}, u32[]{:S(2)}) copy-start(f32[64,4096]{1,0:T(8,128)} %copy-done.2) | copy-start | bytes 3145732
  228.3 5.1 %collective-permute-start.24 = (f32[256,128]{1,0:T(8,128)S(1)}, f32[256,128]{1,0:T(8,128)S(1)}, u32[]{:S(2)}, u32[]{:S(2)}) collective-permute-start(f32[256,128]{1,0:T(8,128)S(1)} %get-tuple-element.28), channel_id=1, source_target_pairs={{0,128},{128,0},{1,129},{129,1},{2,130},{130,2},{3,131},{131,3},{4... | collective-permute-start | bytes 393224 | tf_op jit(solution)/shard_map/ppermute | solution.py:28
  233.4 6.8 %collective-permute-start.27 = (f32[256,128]{1,0:T(8,128)S(1)}, f32[256,128]{1,0:T(8,128)S(1)}, u32[]{:S(2)}, u32[]{:S(2)}) collective-permute-start(f32[256,128]{1,0:T(8,128)S(1)} %add.630), channel_id=1, source_target_pairs={{0,96},{32,0},{64,32},{96,64},{1,97},{33,1},{65,33},{97,65},{2,98}... | collective-permute-start | bytes 393224 | tf_op jit(solution)/shard_map/ppermute | solution.py:28
  235.3 7.2 %collective-permute-start.26 = (f32[256,128]{1,0:T(8,128)S(1)}, f32[256,128]{1,0:T(8,128)S(1)}, u32[]{:S(2)}, u32[]{:S(2)}) collective-permute-start(f32[256,128]{1,0:T(8,128)S(1)} %add.630), channel_id=1, source_target_pairs={{0,64},{32,96},{64,0},{96,32},{1,65},{33,97},{65,1},{97,33},{2,66}... | collective-permute-start | bytes 393224 | tf_op jit(solution)/shard_map/ppermute | solution.py:28
  236.8 7.1 %collective-permute-start.25 = (f32[256,128]{1,0:T(8,128)S(1)}, f32[256,128]{1,0:T(8,128)S(1)}, u32[]{:S(2)}, u32[]{:S(2)}) collective-permute-start(f32[256,128]{1,0:T(8,128)S(1)} %add.630), channel_id=1, source_target_pairs={{0,32},{32,64},{64,96},{96,0},{1,33},{33,65},{65,97},{97,1},{2,34}... | collective-permute-start | bytes 393224 | tf_op jit(solution)/shard_map/ppermute | solution.py:28
  (13 other events, 15.2 us)

commit v4 on v3

--- a/solution.py
+++ b/solution.py
@@ -16,6 +16,7 @@
 NB = 256
 K = 128
 STEP = 1024
+PIECES = 8
 HIGHEST = lax.Precision.HIGHEST
 
 
@@ -47,7 +48,7 @@
     got = swap(tie(jnp.concatenate([near, far], 0), *after))
     mine = by_block((v, near[:n], near[n:], far))
     theirs = by_block((other, got[:n], got[n : 2 * n], got[2 * n :]))
-    return jnp.concatenate([mine, theirs], 0), near
+    return mine, theirs
 
 
 def by_block(parts):
@@ -55,15 +56,15 @@
     return jnp.stack([p.reshape(n, 8, ROWS) for p in parts], 1).reshape(32 * n, ROWS)
 
 
-def gather_x(full, before=(), between=()):
-    half = full.shape[0] // 2
-    near = both_ways(tie(full, *before), "x")
-    far = both_ways(tie(near[:half], *between), "x")
-    return (full, near, far, swap(near), swap(far))
+def gather_x(mine, theirs, before=(), between=()):
+    near = both_ways(tie(mine, *before), "x")
+    near2 = both_ways(tie(theirs, *before), "x")
+    far = both_ways(tie(near, *between), "x")
+    return (mine, theirs, near, near2, far, swap(near), swap(near2), swap(far))
 
 
 def chunks(n, i):
-    return (i, n + i, 2 * n + i, 3 * n + i, 4 * n + i, 5 * n + i, 6 * n + i, 7 * n + i)
+    return tuple(n * piece + i for piece in range(PIECES))
 
 
 def column_order(ring):
@@ -141,12 +142,12 @@
     cur_ref, refs = refs[0], refs[1:]
     cur = cur_ref[...] if len(cur_ref.shape) == 2 else jnp.concatenate([cur_ref[i] for i in range(STEP // 128)], 1)
     if has_old:
-        applied, old, refs = split(refs[0][...]), split(stacked(refs[1:6])), refs[6:]
+        applied, old, refs = split(refs[0][...]), split(stacked(refs[1 : 1 + PIECES])), refs[1 + PIECES :]
         cur = cur - spread_out(applied, old)
     if not has_new:
         refs[0][...] = cur.T
         return
-    new, refs = stacked(refs[:5]), refs[5:]
+    new, refs = stacked(refs[:PIECES]), refs[PIECES:]
     if has_old:
         refs[0][...] = cur
         refs = refs[1:]
@@ -240,17 +241,17 @@
     v = jnp.swapaxes(householder, 1, 2)
 
     v43, v21 = jnp.concatenate([v[4], v[3]], 0), jnp.concatenate([v[2], v[1]], 0)
-    full43, _ = gather_z(v43, swap(v43))
+    ring43 = gather_z(v43, swap(v43))
     cur = exchange(eigvecs)
-    pieces43 = gather_x(full43, (), ())
-    near43, far43 = pieces43[1:3]
-    full21, _ = gather_z(v21, swap(v21), (full43,), (near43, cur), ())
+    pieces43 = gather_x(*ring43)
+    near43, far43 = pieces43[2], pieces43[4]
+    ring21 = gather_z(v21, swap(v21), (near43,cur), (), ())
     (w,) = work(cur, None, (), pieces43)
     share = row_share(w)
-    pieces21 = gather_x(full21, (far43,), (share,))
-    near21, far21 = pieces21[1:3]
-    full0, _ = gather_z(v[0], swap(v[0]), (far43,), (share,))
-    pieces0 = gather_x(full0, (near21,), (far21,))
+    pieces21 = gather_x(*ring21, (far43,), (share,))
+    near21, far21 = pieces21[3], pieces21[4]
+    ring0 = gather_z(v[0], swap(v[0]), (far43,), (share,))
+    pieces0 = gather_x(*ring0, (near21,), (far21,))
 
     def ordered(ring, *blocks):
         pick = (column_order(ring)[:, None] == jnp.arange(NB)[None, :]).astype(jnp.float32)

time: 251 us -> 272 us (1.084)
  starting transfers between devices: 62.6 us -> 89.1 us
  waiting for transfers between devices: 113 us -> 107 us
  other arithmetic: 8.3 us -> 12.4 us
  local copies, waits for them, and re-layouts: 22.2 us -> 19.1 us
    ppermute x16 -> x19, starting transfers between devices: 8.17 us -> 40.3 us  [shift(): return lax.ppermute(a, axis, [(i, (i + by) % n) for i in range(n)])]
    all_to_all x2, waiting for transfers between devices: 14.3 us -> 7.93 us  [row_share(): lax.all_to_all(a.reshape(8, n // 8, width), ROW, split_axis=0, concat_axi...]
    slice x3 -> x0, local copies, waits for them, and re-layouts: 4.62 us -> none  [gather_x(): far = both_ways(tie(near[:half], *between), 'x')]
    all_to_all x2, starting transfers between devices: 14.2 us -> 10.4 us  [row_share(): lax.all_to_all(a.reshape(8, n // 8, width), ROW, split_axis=0, concat_axi...]
    all_to_all x2, waiting for transfers between devices: 5.91 us -> 9.54 us  [hand_on(): lax.all_to_all(a, ROW, split_axis=0, concat_axis=0, tiled=True)]
    ppermute x12 -> x15, starting transfers between devices: 21.9 us -> 19.1 us  [both_ways(): return lax.ppermute(a, (axis, 'core'), pairs)]
    concatenate x3, other arithmetic: 1.08 us -> 3.81 us  [gather_z(): got = swap(tie(jnp.concatenate([near, far], 0), *after))]
    unnamed x56 -> x40, local copies, waits for them, and re-layouts: 7.37 us -> 5.53 us
  transfers between devices with their start and end apart: 33 -> 39, of which waited for: 15 -> 18; matrix products, arithmetic and copies ran while one was open for 10% -> 11% of each run, Pallas kernels for 9% -> 8%
where the time goes in v4:
time: 272 us; the launch traced here: 269 us
  waiting for transfers between devices  107 us (39%)
  starting transfers between devices  89.1 us (33%)
  Pallas kernels  35.3 us (13%)
  local copies, waits for them, and re-layouts  19.1 us (7%)
  other arithmetic  12.4 us (5%)
  matrix products  5.28 us (2%)
    ppermute x15, waiting for transfers between devices, both_ways(): return lax.ppermute(a, (axis, 'core'), pairs)  79.3 us
    ppermute x19, starting transfers between devices, shift(): return lax.ppermute(a, axis, [(i, (i + by) % n) for i in range(n)])  40.3 us
    pallas_call x4, Pallas kernels, work(): pl.pallas_call(functools.partial(work_kernel, bool(old), bool(new)), grid...  29.8 us
    ppermute x15, starting transfers between devices, both_ways(): return lax.ppermute(a, (axis, 'core'), pairs)  19.1 us
    all_to_all x2, starting transfers between devices, hand_on(): lax.all_to_all(a, ROW, split_axis=0, concat_axis=0, tiled=True)  10.5 us
    all_to_all x2, starting transfers between devices, row_share(): lax.all_to_all(a.reshape(8, n // 8, width), ROW, split_axis=0, concat_axi...  10.4 us
    ppermute x19, waiting for transfers between devices, shift(): return lax.ppermute(a, axis, [(i, (i + by) % n) for i in range(n)])  10.2 us
    all_to_all x2, waiting for transfers between devices, hand_on(): lax.all_to_all(a, ROW, split_axis=0, concat_axis=0, tiled=True)  9.54 us
  transfers between devices with their start and end apart: 39, of which 18 were waited for; matrix products, arithmetic and copies ran while one was open for 11% of the time, Pallas kernels for 8%

profile of v4, /device:TPU:32, one launch (start us, length us, event | category | flops | bytes accessed | tf_op | source)
XLA Modules:
  0.0 268.5 jit_solution(9497923799080319146)
XLA Ops:
  0.0 2.1 slice_bitcast_fusion.17
  2.2 1.5 collective-permute-done
  5.3 3.3 %collective-permute-start.1 = (f32[32,4096]{1,0:T(8,128)}, f32[32,4096]{1,0:T(8,128)S(1)}, u32[]{:S(2)}, u32[]{:S(2)}) collective-permute-start(f32[32,4096]{1,0:T(8,128)} %pad_maximum_fusion.6), channel_id=1, source_target_pairs={{0,8},{1,25},{8,16},{9,1},{16,24},{17,9},{24,0},{25,17},{2,10},{3,... | collective-permute-start | bytes 1572872 | tf_op jit(solution)/shard_map/ppermute | solution.py:37
  8.6 1.8 copy.21
  10.4 8.7 %all-to-all-start = ((f32[32,128,128]{2,1,0:T(8,128)}), f32[32,128,128]{2,1,0:T(8,128)}, u32[]{:S(2)}, u32[]{:S(2)}) async-start(f32[32,128,128]{2,1,0:T(8,128)} %bitcast.1), calls=%async_computation | async-start | bytes 4194304 | tf_op jit(solution)/shard_map/all_to_all | solution.py:87
  19.1 4.7 %collective-permute-done.1 = f32[32,4096]{1,0:T(8,128)S(1)} collective-permute-done((f32[32,4096]{1,0:T(8,128)}, f32[32,4096]{1,0:T(8,128)S(1)}, u32[]{:S(2)}, u32[]{:S(2)}) %collective-permute-start.1) | collective-permute-done | bytes 524320 | tf_op jit(solution)/shard_map/ppermute | solution.py:37
  25.1 14.4 %collective-permute-done.2 = f32[16,4096]{1,0:T(8,128)S(1)} collective-permute-done((f32[16,4096]{1,0:T(8,128)S(1)}, f32[16,4096]{1,0:T(8,128)S(1)}, u32[]{:S(2)}, u32[]{:S(2)}) %collective-permute-start.2) | collective-permute-done | bytes 262176 | tf_op jit(solution)/shard_map/ppermute | solution.py:37
  39.6 34.7 %collective-permute-start.3 = (f32[48,4096]{1,0:T(8,128)S(1)}, f32[48,4096]{1,0:T(8,128)S(1)}, u32[]{:S(2)}, u32[]{:S(2)}) collective-permute-start(f32[48,4096]{1,0:T(8,128)S(1)} %pad_maximum_fusion.4), channel_id=1, source_target_pairs={{0,1},{1,0},{2,3},{3,2},{4,5},{5,4},{6,7},{7,6},{8,9},{9,8},{10,11... | collective-permute-start | bytes 2359304 | tf_op jit(solution)/shard_map/ppermute | solution.py:29
  75.0 1.5 collective-permute-start.4
  76.7 1.6 collective-permute-start.5
  78.3 12.8 %collective-permute-done.4.refs_3_.refs_4_ = f32[64,4096]{1,0:T(8,128)S(1)} collective-permute-done((f32[64,4096]{1,0:T(8,128)S(1)}, f32[64,4096]{1,0:T(8,128)S(1)}, u32[]{:S(2)}, u32[]{:S(2)}) %collective-permute-start.4) | collective-permute-done | bytes 1048608 | tf_op jit(solution)/shard_map/ppermute | solution.py:37
  93.1 2.4 collective-permute-start.11
  96.2 2.2 fusion.28
  98.4 4.0 %collective-permute-done.5.refs_4_.refs_5_ = f32[64,4096]{1,0:T(8,128)} collective-permute-done((f32[64,4096]{1,0:T(8,128)S(1)}, f32[64,4096]{1,0:T(8,128)}, u32[]{:S(2)}, u32[]{:S(2)}) %collective-permute-start.5) | collective-permute-done | bytes 1048608 | tf_op jit(solution)/shard_map/ppermute | solution.py:37
  102.5 11.2 %collective-permute-done.6.refs_5_.refs_6_ = f32[64,4096]{1,0:T(8,128)} collective-permute-done((f32[64,4096]{1,0:T(8,128)S(1)}, f32[64,4096]{1,0:T(8,128)}, u32[]{:S(2)}, u32[]{:S(2)}) %collective-permute-start.6) | collective-permute-done | bytes 1048608 | tf_op jit(solution)/shard_map/ppermute | solution.py:37
  113.7 1.9 slice_bitcast_fusion.19
  115.7 2.4 collective-permute-start.12
  118.8 6.6 %work.4 = f32[1024,128]{1,0:T(8,128)S(1)} custom-call(f32[32,128,128]{2,1,0:T(8,128)} %all-to-all-done.refs_0_, f32[64,4096]{1,0:T(8,128)S(1)} %bitcast.146, f32[64,4096]{1,0:T(8,128)S(1)} %bitcast.149, f32[64,4096]{1,0:T(8,128)S(1)} %collective-permute-done.4.refs_3_.refs_4_, f32[64,4096]{1,0:T(8,128)} %collective-permute-done.5.refs_4_.refs_5_, ...), custom_call_target="tpu_custom_call" | custom-call | flops 1610612736 | bytes 12582912 | tf_op jit(solution)/shard_map/work/pallas_call | solution.py:202
  126.3 6.2 %all-to-all-start.1 = ((f32[8,128,128]{2,1,0:T(8,128)}), f32[8,128,128]{2,1,0:T(8,128)}, u32[]{:S(2)}, u32[]{:S(2)}) async-start(f32[8,128,128]{2,1,0:T(8,128)} %bitcast.151), calls=%async_computation.1 | async-start | bytes 1048576 | tf_op jit(solution)/shard_map/all_to_all | solution.py:92
  132.5 2.1 pad_maximum_fusion.5
  135.6 2.9 %collective-permute-start.21 = (f32[16,4096]{1,0:T(8,128)}, f32[16,4096]{1,0:T(8,128)S(1)}, u32[]{:S(2)}, u32[]{:S(2)}) collective-permute-start(f32[16,4096]{1,0:T(8,128)} %pad_maximum_fusion.11), channel_id=1, source_target_pairs={{0,8},{1,25},{8,16},{9,1},{16,24},{17,9},{24,0},{25,17},{2,10},{3,... | collective-permute-start | bytes 786440 | tf_op jit(solution)/shard_map/ppermute | solution.py:37
  140.1 2.1 all-to-all-done.1
  142.2 1.7 reduce_sum.18
  146.6 9.3 %collective-permute-done.14.refs_12_.refs_4_ = f32[64,4096]{1,0:T(8,128)} collective-permute-done((f32[64,4096]{1,0:T(8,128)S(1)}, f32[64,4096]{1,0:T(8,128)}, u32[]{:S(2)}, u32[]{:S(2)}) %collective-permute-start.14) | collective-permute-done | bytes 1048608 | tf_op jit(solution)/shard_map/ppermute | solution.py:37
  157.8 9.4 %collective-permute-done.15.refs_13_.refs_5_ = f32[64,4096]{1,0:T(8,128)} collective-permute-done((f32[64,4096]{1,0:T(8,128)S(1)}, f32[64,4096]{1,0:T(8,128)}, u32[]{:S(2)}, u32[]{:S(2)}) %collective-permute-start.15) | collective-permute-done | bytes 1048608 | tf_op jit(solution)/shard_map/ppermute | solution.py:37
  167.2 11.2 %collective-permute-done.16.refs_14_.refs_6_ = f32[64,4096]{1,0:T(8,128)} collective-permute-done((f32[64,4096]{1,0:T(8,128)}, f32[64,4096]{1,0:T(8,128)}, u32[]{:S(2)}, u32[]{:S(2)}) %collective-permute-start.16) | collective-permute-done | bytes 1048608 | tf_op jit(solution)/shard_map/ppermute | solution.py:37
  179.8 5.7 %all-to-all-start.2 = ((f32[8,128,128]{2,1,0:T(8,128)}), f32[8,128,128]{2,1,0:T(8,128)}, u32[]{:S(2)}, u32[]{:S(2)}) async-start(f32[8,128,128]{2,1,0:T(8,128)} %broadcast_in_dim.4), calls=%async_computation.2 | async-start | bytes 1048576 | tf_op jit(solution)/shard_map/all_to_all | solution.py:99
  185.5 1.7 pad_maximum_fusion.8
  188.3 6.6 %all-to-all-done.2 = f32[8,128,128]{2,1,0:T(8,128)} async-done(((f32[8,128,128]{2,1,0:T(8,128)}), f32[8,128,128]{2,1,0:T(8,128)}, u32[]{:S(2)}, u32[]{:S(2)}) %all-to-all-start.2) | async-done | bytes 524320 | tf_op jit(solution)/shard_map/all_to_all | solution.py:99
  194.9 2.6 solve.3.refs_1_
  199.0 10.4 %work.5 = (f32[128,4096]{1,0:T(8,128)}, f32[1024,128]{1,0:T(8,128)S(1)}) custom-call(f32[32,128,128]{2,1,0:T(8,128)} %all-to-all-done.refs_0_, f32[128,512]{1,0:T(8,128)S(1)} %solve.3.refs_1_, f32[64,4096]{1,0:T(8,128)S(1)} %bitcast.147, f32[64,4096]{1,0:T(8,128)S(1)} %bitcast.150, f32[64,4096]{1,0:T(8,128)S(1)} %copy-done.1, ...), custom_call_target="tpu_custom_call" | custom-call | flops 3221225472 | bytes 20971520 | tf_op jit(solution)/shard_map/work/pallas_call | solution.py:202
  210.3 4.2 %all-to-all-start.3 = ((f32[8,128,128]{2,1,0:T(8,128)}), f32[8,128,128]{2,1,0:T(8,128)S(1)}, u32[]{:S(2)}, u32[]{:S(2)}) async-start(f32[8,128,128]{2,1,0:T(8,128)} %bitcast.152), calls=%async_computation.3 | async-start | bytes 1048576 | tf_op jit(solution)/shard_map/all_to_all | solution.py:92
  216.2 1.3 collective-permute-start.26
  217.5 5.8 %all-to-all-done.3 = f32[8,128,128]{2,1,0:T(8,128)S(1)} async-done(((f32[8,128,128]{2,1,0:T(8,128)}), f32[8,128,128]{2,1,0:T(8,128)S(1)}, u32[]{:S(2)}, u32[]{:S(2)}) %all-to-all-start.3) | async-done | bytes 524320 | tf_op jit(solution)/shard_map/all_to_all | solution.py:92
  224.2 4.8 %all-to-all-start.4 = ((f32[8,128,128]{2,1,0:T(8,128)}), f32[8,128,128]{2,1,0:T(8,128)}, u32[]{:S(2)}, u32[]{:S(2)}) async-start(f32[8,128,128]{2,1,0:T(8,128)} %broadcast_in_dim.5), calls=%async_computation.4 | async-start | bytes 1048576 | tf_op jit(solution)/shard_map/all_to_all | solution.py:99
  229.6 2.1 collective-permute-done.26.refs_14_.refs_6_
  231.7 1.4 fusion.4
  233.1 1.3 fusion.12.t_ref
  234.4 2.9 %all-to-all-done.4 = f32[8,128,128]{2,1,0:T(8,128)} async-done(((f32[8,128,128]{2,1,0:T(8,128)}), f32[8,128,128]{2,1,0:T(8,128)}, u32[]{:S(2)}, u32[]{:S(2)}) %all-to-all-start.4) | async-done | bytes 524320 | tf_op jit(solution)/shard_map/all_to_all | solution.py:99
  238.4 2.5 solve.4.refs_1_
  240.9 7.8 %work.6 = (f32[128,4096]{1,0:T(8,128)}, f32[256,128]{1,0:T(8,128)S(1)}) custom-call(f32[128,4096]{1,0:T(8,128)} %get-tuple-element.22.refs_0_, f32[128,512]{1,0:T(8,128)S(1)} %solve.4.refs_1_, f32[64,4096]{1,0:T(8,128)} %bitcast.155, f32[64,4096]{1,0:T(8,128)} %bitcast.158, f32[64,4096]{1,0:T(8,128)} %collective-permute-done.14.refs_12_.refs_4_, ...), custom_call_target="tpu_custom_call" | custom-call | flops 2415919104 | bytes 16777216 | tf_op jit(solution)/shard_map/work/pallas_call | solution.py:202
  249.8 3.9 %collective-permute-done.30 = f32[256,128]{1,0:T(8,128)S(1)} collective-permute-done((f32[256,128]{1,0:T(8,128)S(1)}, f32[256,128]{1,0:T(8,128)S(1)}, u32[]{:S(2)}, u32[]{:S(2)}) %collective-permute-start.30) | collective-permute-done | bytes 131104 | tf_op jit(solution)/shard_map/ppermute | solution.py:29
  253.7 1.5 collective-permute-start.33
  255.2 1.5 collective-permute-start.32
  256.7 1.3 fusion.8
  258.7 3.0 %collective-permute-done.32 = f32[256,128]{1,0:T(8,128)S(1)} collective-permute-done((f32[256,128]{1,0:T(8,128)S(1)}, f32[256,128]{1,0:T(8,128)S(1)}, u32[]{:S(2)}, u32[]{:S(2)}) %collective-permute-start.32) | collective-permute-done | bytes 131104 | tf_op jit(solution)/shard_map/ppermute | solution.py:29
  261.7 1.4 collective-permute-done.31
  263.6 5.0 %work.7 = f32[4096,128]{1,0:T(8,128)} custom-call(f32[128,4096]{1,0:T(8,128)} %get-tuple-element.29.refs_0_, f32[128,256]{1,0:T(8,128)S(1)} %solve.5.refs_1_, f32[32,4096]{1,0:T(8,128)S(1)} %maximum_bitcast_fusion.refs_10_.refs_2_, f32[32,4096]{1,0:T(8,128)S(1)} %maximum_bitcast_fusion.1.refs_11_.refs_3_, ...), custom_call_target="tpu_custom_call" | custom-call | flops 805306368 | bytes 8388608 | tf_op jit(solution)/shard_map/work/pallas_call | solution.py:202
  (116 shorter events, 26.6 us)
Async XLA Ops:
  2.1 1.6 collective-permute-start
  5.3 18.5 %collective-permute-start.1 = (f32[32,4096]{1,0:T(8,128)}, f32[32,4096]{1,0:T(8,128)S(1)}, u32[]{:S(2)}, u32[]{:S(2)}) collective-permute-start(f32[32,4096]{1,0:T(8,128)} %pad_maximum_fusion.6), channel_id=1, source_target_pairs={{0,8},{1,25},{8,16},{9,1},{16,24},{17,9},{24,0},{25,17},{2,10},{3,... | collective-permute-start | bytes 1572872 | tf_op jit(solution)/shard_map/ppermute | solution.py:37
  10.4 82.7 %all-to-all-start = ((f32[32,128,128]{2,1,0:T(8,128)}), f32[32,128,128]{2,1,0:T(8,128)}, u32[]{:S(2)}, u32[]{:S(2)}) async-start(f32[32,128,128]{2,1,0:T(8,128)} %bitcast.1), calls=%async_computation | async-start | bytes 4194304 | tf_op jit(solution)/shard_map/all_to_all | solution.py:87
  23.8 15.7 %collective-permute-start.2 = (f32[16,4096]{1,0:T(8,128)S(1)}, f32[16,4096]{1,0:T(8,128)S(1)}, u32[]{:S(2)}, u32[]{:S(2)}) collective-permute-start(f32[16,4096]{1,0:T(8,128)S(1)} %get-tuple-element.52), channel_id=1, source_target_pairs={{0,8},{1,25},{8,16},{9,1},{16,24},{17,9},{24,0},{25,17},{2,10},{3,... | collective-permute-start | bytes 786440 | tf_op jit(solution)/shard_map/ppermute | solution.py:37
  39.6 37.0 %collective-permute-start.3 = (f32[48,4096]{1,0:T(8,128)S(1)}, f32[48,4096]{1,0:T(8,128)S(1)}, u32[]{:S(2)}, u32[]{:S(2)}) collective-permute-start(f32[48,4096]{1,0:T(8,128)S(1)} %pad_maximum_fusion.4), channel_id=1, source_target_pairs={{0,1},{1,0},{2,3},{3,2},{4,5},{5,4},{6,7},{7,6},{8,9},{9,8},{10,11... | collective-permute-start | bytes 2359304 | tf_op jit(solution)/shard_map/ppermute | solution.py:29
  74.9 16.4 %collective-permute-start.10 = (f32[16,4096]{1,0:T(8,128)S(1)}, f32[16,4096]{1,0:T(8,128)S(1)}, u32[]{:S(2)}, u32[]{:S(2)}) collective-permute-start(f32[16,4096]{1,0:T(8,128)S(1)} %get-tuple-element.60), channel_id=1, source_target_pairs={{0,1},{1,0},{2,3},{3,2},{4,5},{5,4},{6,7},{7,6},{8,9},{9,8},{10,11... | collective-permute-start | bytes 786440 | tf_op jit(solution)/shard_map/ppermute | solution.py:29
  75.0 16.1 %collective-permute-start.4 = (f32[64,4096]{1,0:T(8,128)S(1)}, f32[64,4096]{1,0:T(8,128)S(1)}, u32[]{:S(2)}, u32[]{:S(2)}) collective-permute-start(f32[64,4096]{1,0:T(8,128)S(1)} %bitcast.145), channel_id=1, source_target_pairs={{0,2},{1,7},{2,4},{3,1},{4,6},{5,3},{6,0},{7,5},{8,10},{9,15},{10,... | collective-permute-start | bytes 3145736 | tf_op jit(solution)/shard_map/ppermute | solution.py:37
  76.7 25.7 %collective-permute-start.5 = (f32[64,4096]{1,0:T(8,128)S(1)}, f32[64,4096]{1,0:T(8,128)}, u32[]{:S(2)}, u32[]{:S(2)}) collective-permute-start(f32[64,4096]{1,0:T(8,128)S(1)} %bitcast.148), channel_id=1, source_target_pairs={{0,2},{1,7},{2,4},{3,1},{4,6},{5,3},{6,0},{7,5},{8,10},{9,15},{10,... | collective-permute-start | bytes 3145736 | tf_op jit(solution)/shard_map/ppermute | solution.py:37
  91.1 27.7 %copy-start = (f32[64,4096]{1,0:T(8,128)}, f32[64,4096]{1,0:T(8,128)S(1)}, u32[]{:S(2)}) copy-start(f32[64,4096]{1,0:T(8,128)S(1)} %collective-permute-done.4.refs_3_.refs_4_) | copy-start | bytes 3145732
  91.1 22.6 %collective-permute-start.6 = (f32[64,4096]{1,0:T(8,128)S(1)}, f32[64,4096]{1,0:T(8,128)}, u32[]{:S(2)}, u32[]{:S(2)}) collective-permute-start(f32[64,4096]{1,0:T(8,128)S(1)} %collective-permute-done.4.refs_3_.refs_4_), channel_id=1, source_target_pairs={{0,2},{1,7},{2,4},{3,1},{4,6},{5,3},{6,0},{7,5},{8,10},{9,15},{10,... | collective-permute-start | bytes 3145736 | tf_op jit(solution)/shard_map/ppermute | solution.py:37
  93.1 20.6 %collective-permute-start.11 = (f32[32,4096]{1,0:T(8,128)}, f32[32,4096]{1,0:T(8,128)}, u32[]{:S(2)}, u32[]{:S(2)}) collective-permute-start(f32[32,4096]{1,0:T(8,128)} %pad_maximum_fusion.7), channel_id=1, source_target_pairs={{0,8},{1,25},{8,16},{9,1},{16,24},{17,9},{24,0},{25,17},{2,10},{3,... | collective-permute-start | bytes 1572872 | tf_op jit(solution)/shard_map/ppermute | solution.py:37
  95.5 39.4 %collective-permute-start.20 = (f32[8,4096]{1,0:T(8,128)}, f32[8,4096]{1,0:T(8,128)S(1)}, u32[]{:S(2)}, u32[]{:S(2)}) collective-permute-start(f32[8,4096]{1,0:T(8,128)} %get-tuple-element.42), channel_id=1, source_target_pairs={{0,1},{1,0},{2,3},{3,2},{4,5},{5,4},{6,7},{7,6},{8,9},{9,8},{10,11... | collective-permute-start | bytes 393224 | tf_op jit(solution)/shard_map/ppermute | solution.py:29
  98.4 20.4 %collective-permute-start.7 = (f32[64,4096]{1,0:T(8,128)S(1)}, f32[64,4096]{1,0:T(8,128)}, u32[]{:S(2)}, u32[]{:S(2)}) collective-permute-start(f32[64,4096]{1,0:T(8,128)S(1)} %collective-permute-done.4.refs_3_.refs_4_), channel_id=1, source_target_pairs={{0,1},{1,0},{2,3},{3,2},{4,5},{5,4},{6,7},{7,6},{8,9},{9,8},{10,11... | collective-permute-start | bytes 3145736 | tf_op jit(solution)/shard_map/ppermute | solution.py:29
  102.5 16.3 %collective-permute-start.8 = (f32[64,4096]{1,0:T(8,128)}, f32[64,4096]{1,0:T(8,128)}, u32[]{:S(2)}, u32[]{:S(2)}) collective-permute-start(f32[64,4096]{1,0:T(8,128)} %collective-permute-done.5.refs_4_.refs_5_), channel_id=1, source_target_pairs={{0,1},{1,0},{2,3},{3,2},{4,5},{5,4},{6,7},{7,6},{8,9},{9,8},{10,11... | collective-permute-start | bytes 3145736 | tf_op jit(solution)/shard_map/ppermute | solution.py:29
  113.7 5.1 %collective-permute-start.9 = (f32[64,4096]{1,0:T(8,128)}, f32[64,4096]{1,0:T(8,128)}, u32[]{:S(2)}, u32[]{:S(2)}) collective-permute-start(f32[64,4096]{1,0:T(8,128)} %collective-permute-done.6.refs_5_.refs_6_), channel_id=1, source_target_pairs={{0,1},{1,0},{2,3},{3,2},{4,5},{5,4},{6,7},{7,6},{8,9},{9,8},{10,11... | collective-permute-start | bytes 3145736 | tf_op jit(solution)/shard_map/ppermute | solution.py:29
  115.7 16.8 %collective-permute-start.12 = (f32[16,4096]{1,0:T(8,128)}, f32[16,4096]{1,0:T(8,128)S(1)}, u32[]{:S(2)}, u32[]{:S(2)}) collective-permute-start(f32[16,4096]{1,0:T(8,128)} %get-tuple-element.49), channel_id=1, source_target_pairs={{0,8},{1,25},{8,16},{9,1},{16,24},{17,9},{24,0},{25,17},{2,10},{3,... | collective-permute-start | bytes 786440 | tf_op jit(solution)/shard_map/ppermute | solution.py:37
  126.3 15.9 %all-to-all-start.1 = ((f32[8,128,128]{2,1,0:T(8,128)}), f32[8,128,128]{2,1,0:T(8,128)}, u32[]{:S(2)}, u32[]{:S(2)}) async-start(f32[8,128,128]{2,1,0:T(8,128)} %bitcast.151), calls=%async_computation.1 | async-start | bytes 1048576 | tf_op jit(solution)/shard_map/all_to_all | solution.py:92
  134.6 9.4 %collective-permute-start.13 = (f32[48,4096]{1,0:T(8,128)}, f32[48,4096]{1,0:T(8,128)}, u32[]{:S(2)}, u32[]{:S(2)}) collective-permute-start(f32[48,4096]{1,0:T(8,128)} %pad_maximum_fusion.5), channel_id=1, source_target_pairs={{0,1},{1,0},{2,3},{3,2},{4,5},{5,4},{6,7},{7,6},{8,9},{9,8},{10,11... | collective-permute-start | bytes 2359304 | tf_op jit(solution)/shard_map/ppermute | solution.py:29
  134.9 10.3 %copy-start.15 = (f32[8,4096]{1,0:T(8,128)}, f32[8,4096]{1,0:T(8,128)S(1)}, u32[]{:S(2)}) copy-start(f32[8,4096]{1,0:T(8,128)S(1)} %collective-permute-done.20) | copy-start | bytes 393220
  135.6 20.8 %collective-permute-start.21 = (f32[16,4096]{1,0:T(8,128)}, f32[16,4096]{1,0:T(8,128)S(1)}, u32[]{:S(2)}, u32[]{:S(2)}) collective-permute-start(f32[16,4096]{1,0:T(8,128)} %pad_maximum_fusion.11), channel_id=1, source_target_pairs={{0,8},{1,25},{8,16},{9,1},{16,24},{17,9},{24,0},{25,17},{2,10},{3,... | collective-permute-start | bytes 786440 | tf_op jit(solution)/shard_map/ppermute | solution.py:37
  139.8 16.2 %copy-start.19 = (s32[256]{0:T(256)S(1)}, s32[256]{0:T(256)}, u32[]{:S(2)}) copy-start(s32[256]{0:T(256)} %add.629) | copy-start | bytes 3076
  139.8 16.2 %collective-permute-start.14 = (f32[64,4096]{1,0:T(8,128)S(1)}, f32[64,4096]{1,0:T(8,128)}, u32[]{:S(2)}, u32[]{:S(2)}) collective-permute-start(f32[64,4096]{1,0:T(8,128)S(1)} %bitcast.153), channel_id=1, source_target_pairs={{0,2},{1,7},{2,4},{3,1},{4,6},{5,3},{6,0},{7,5},{8,10},{9,15},{10,... | collective-permute-start | bytes 3145736 | tf_op jit(solution)/shard_map/ppermute | solution.py:37
  143.9 12.0 %copy-start.9 = (f32[1,256,256]{2,1,0:T(8,128)S(1)}, f32[1,256,256]{2,1,0:T(8,128)}, u32[]{:S(2)}) copy-start(f32[1,256,256]{2,1,0:T(8,128)} %get-tuple-element.32) | copy-start | bytes 786436
  143.9 12.1 %copy-start.10 = (f32[1,256,256]{2,1,0:T(8,128)S(1)}, f32[1,256,256]{2,1,0:T(8,128)}, u32[]{:S(2)}) copy-start(f32[1,256,256]{2,1,0:T(8,128)} %get-tuple-element.33) | copy-start | bytes 786436
  145.2 33.8 %copy-start.18 = (f32[128,128]{1,0:T(8,128)S(1)}, f32[128,128]{1,0:T(8,128)}, u32[]{:S(2)}) copy-start(f32[128,128]{1,0:T(8,128)} %reduce_sum.18) | copy-start | bytes 196612
  146.3 32.2 %copy-start.6 = (f32[2,4,8,4096]{3,2,1,0:T(8,128)}, f32[2,4,8,4096]{3,2,1,0:T(8,128)S(1)}, u32[]{:S(2)}) copy-start(f32[2,4,8,4096]{3,2,1,0:T(8,128)S(1)} %pad_maximum_fusion.3) | copy-start | bytes 3145732
  146.3 20.9 %collective-permute-start.15 = (f32[64,4096]{1,0:T(8,128)S(1)}, f32[64,4096]{1,0:T(8,128)}, u32[]{:S(2)}, u32[]{:S(2)}) collective-permute-start(f32[64,4096]{1,0:T(8,128)S(1)} %bitcast.156), channel_id=1, source_target_pairs={{0,2},{1,7},{2,4},{3,1},{4,6},{5,3},{6,0},{7,5},{8,10},{9,15},{10,... | collective-permute-start | bytes 3145736 | tf_op jit(solution)/shard_map/ppermute | solution.py:37
  156.0 22.5 %collective-permute-start.16 = (f32[64,4096]{1,0:T(8,128)}, f32[64,4096]{1,0:T(8,128)}, u32[]{:S(2)}, u32[]{:S(2)}) collective-permute-start(f32[64,4096]{1,0:T(8,128)} %collective-permute-done.14.refs_12_.refs_4_), channel_id=1, source_target_pairs={{0,2},{1,7},{2,4},{3,1},{4,6},{5,3},{6,0},{7,5},{8,10},{9,15},{10,... | collective-permute-start | bytes 3145736 | tf_op jit(solution)/shard_map/ppermute | solution.py:37
  157.2 28.3 %collective-permute-start.22 = (f32[8,4096]{1,0:T(8,128)}, f32[8,4096]{1,0:T(8,128)}, u32[]{:S(2)}, u32[]{:S(2)}) collective-permute-start(f32[8,4096]{1,0:T(8,128)} %get-tuple-element.25), channel_id=1, source_target_pairs={{0,8},{1,25},{8,16},{9,1},{16,24},{17,9},{24,0},{25,17},{2,10},{3,... | collective-permute-start | bytes 393224 | tf_op jit(solution)/shard_map/ppermute | solution.py:37
  157.8 40.0 %collective-permute-start.17 = (f32[64,4096]{1,0:T(8,128)}, f32[64,4096]{1,0:T(8,128)}, u32[]{:S(2)}, u32[]{:S(2)}) collective-permute-start(f32[64,4096]{1,0:T(8,128)} %collective-permute-done.14.refs_12_.refs_4_), channel_id=1, source_target_pairs={{0,1},{1,0},{2,3},{3,2},{4,5},{5,4},{6,7},{7,6},{8,9},{9,8},{10,11... | collective-permute-start | bytes 3145736 | tf_op jit(solution)/shard_map/ppermute | solution.py:29
  167.2 30.6 %collective-permute-start.18 = (f32[64,4096]{1,0:T(8,128)}, f32[64,4096]{1,0:T(8,128)}, u32[]{:S(2)}, u32[]{:S(2)}) collective-permute-start(f32[64,4096]{1,0:T(8,128)} %collective-permute-done.15.refs_13_.refs_5_), channel_id=1, source_target_pairs={{0,1},{1,0},{2,3},{3,2},{4,5},{5,4},{6,7},{7,6},{8,9},{9,8},{10,11... | collective-permute-start | bytes 3145736 | tf_op jit(solution)/shard_map/ppermute | solution.py:29
  178.4 19.3 %collective-permute-start.19 = (f32[64,4096]{1,0:T(8,128)}, f32[64,4096]{1,0:T(8,128)}, u32[]{:S(2)}, u32[]{:S(2)}) collective-permute-start(f32[64,4096]{1,0:T(8,128)} %collective-permute-done.16.refs_14_.refs_6_), channel_id=1, source_target_pairs={{0,1},{1,0},{2,3},{3,2},{4,5},{5,4},{6,7},{7,6},{8,9},{9,8},{10,11... | collective-permute-start | bytes 3145736 | tf_op jit(solution)/shard_map/ppermute | solution.py:29
  179.8 15.1 %all-to-all-start.2 = ((f32[8,128,128]{2,1,0:T(8,128)}), f32[8,128,128]{2,1,0:T(8,128)}, u32[]{:S(2)}, u32[]{:S(2)}) async-start(f32[8,128,128]{2,1,0:T(8,128)} %broadcast_in_dim.4), calls=%async_computation.2 | async-start | bytes 1048576 | tf_op jit(solution)/shard_map/all_to_all | solution.py:99
  187.2 27.3 %collective-permute-start.23 = (f32[24,4096]{1,0:T(8,128)}, f32[24,4096]{1,0:T(8,128)}, u32[]{:S(2)}, u32[]{:S(2)}) collective-permute-start(f32[24,4096]{1,0:T(8,128)} %pad_maximum_fusion.8), channel_id=1, source_target_pairs={{0,1},{1,0},{2,3},{3,2},{4,5},{5,4},{6,7},{7,6},{8,9},{9,8},{10,11... | collective-permute-start | bytes 1179656 | tf_op jit(solution)/shard_map/ppermute | solution.py:29
  194.9 20.7 %copy-start.16 = (f32[8,4096]{1,0:T(8,128)S(1)}, f32[8,4096]{1,0:T(8,128)}, u32[]{:S(2)}) copy-start(f32[8,4096]{1,0:T(8,128)} %copy-done.15) | copy-start | bytes 393220
  197.5 18.8 %collective-permute-start.24 = (f32[32,4096]{1,0:T(8,128)S(1)}, f32[32,4096]{1,0:T(8,128)S(1)}, u32[]{:S(2)}, u32[]{:S(2)}) collective-permute-start(f32[32,4096]{1,0:T(8,128)S(1)} %maximum_bitcast_fusion.refs_10_.refs_2_), channel_id=1, source_target_pairs={{0,2},{1,7},{2,4},{3,1},{4,6},{5,3},{6,0},{7,5},{8,10},{9,15},{10,... | collective-permute-start | bytes 1572872 | tf_op jit(solution)/shard_map/ppermute | solution.py:37
  210.3 13.1 %all-to-all-start.3 = ((f32[8,128,128]{2,1,0:T(8,128)}), f32[8,128,128]{2,1,0:T(8,128)S(1)}, u32[]{:S(2)}, u32[]{:S(2)}) async-start(f32[8,128,128]{2,1,0:T(8,128)} %bitcast.152), calls=%async_computation.3 | async-start | bytes 1048576 | tf_op jit(solution)/shard_map/all_to_all | solution.py:92
  214.5 17.3 %copy-start.8 = (f32[1,256,256]{2,1,0:T(8,128)S(1)}, f32[1,256,256]{2,1,0:T(8,128)}, u32[]{:S(2)}) copy-start(f32[1,256,256]{2,1,0:T(8,128)} %get-tuple-element.31) | copy-start | bytes 786436
  215.6 13.4 %collective-permute-start.25 = (f32[32,4096]{1,0:T(8,128)S(1)}, f32[32,4096]{1,0:T(8,128)S(1)}, u32[]{:S(2)}, u32[]{:S(2)}) collective-permute-start(f32[32,4096]{1,0:T(8,128)S(1)} %maximum_bitcast_fusion.1.refs_11_.refs_3_), channel_id=1, source_target_pairs={{0,2},{1,7},{2,4},{3,1},{4,6},{5,3},{6,0},{7,5},{8,10},{9,15},{10,... | collective-permute-start | bytes 1572872 | tf_op jit(solution)/shard_map/ppermute | solution.py:37
  216.2 15.5 %collective-permute-start.26 = (f32[32,4096]{1,0:T(8,128)S(1)}, f32[32,4096]{1,0:T(8,128)S(1)}, u32[]{:S(2)}, u32[]{:S(2)}) collective-permute-start(f32[32,4096]{1,0:T(8,128)S(1)} %collective-permute-done.24.refs_12_.refs_4_), channel_id=1, source_target_pairs={{0,2},{1,7},{2,4},{3,1},{4,6},{5,3},{6,0},{7,5},{8,10},{9,15},{10,... | collective-permute-start | bytes 1572872 | tf_op jit(solution)/shard_map/ppermute | solution.py:37
  224.2 13.1 %all-to-all-start.4 = ((f32[8,128,128]{2,1,0:T(8,128)}), f32[8,128,128]{2,1,0:T(8,128)}, u32[]{:S(2)}, u32[]{:S(2)}) async-start(f32[8,128,128]{2,1,0:T(8,128)} %broadcast_in_dim.5), calls=%async_computation.4 | async-start | bytes 1048576 | tf_op jit(solution)/shard_map/all_to_all | solution.py:99
  229.1 11.8 %collective-permute-start.27 = (f32[32,4096]{1,0:T(8,128)S(1)}, f32[32,4096]{1,0:T(8,128)S(1)}, u32[]{:S(2)}, u32[]{:S(2)}) collective-permute-start(f32[32,4096]{1,0:T(8,128)S(1)} %collective-permute-done.24.refs_12_.refs_4_), channel_id=1, source_target_pairs={{0,1},{1,0},{2,3},{3,2},{4,5},{5,4},{6,7},{7,6},{8,9},{9,8},{10,11... | collective-permute-start | bytes 1572872 | tf_op jit(solution)/shard_map/ppermute | solution.py:29
  229.1 11.8 %collective-permute-start.28 = (f32[32,4096]{1,0:T(8,128)S(1)}, f32[32,4096]{1,0:T(8,128)}, u32[]{:S(2)}, u32[]{:S(2)}) collective-permute-start(f32[32,4096]{1,0:T(8,128)S(1)} %collective-permute-done.25.refs_13_.refs_5_), channel_id=1, source_target_pairs={{0,1},{1,0},{2,3},{3,2},{4,5},{5,4},{6,7},{7,6},{8,9},{9,8},{10,11... | collective-permute-start | bytes 1572872 | tf_op jit(solution)/shard_map/ppermute | solution.py:29
  231.7 9.2 %collective-permute-start.29 = (f32[32,4096]{1,0:T(8,128)S(1)}, f32[32,4096]{1,0:T(8,128)}, u32[]{:S(2)}, u32[]{:S(2)}) collective-permute-start(f32[32,4096]{1,0:T(8,128)S(1)} %collective-permute-done.26.refs_14_.refs_6_), channel_id=1, source_target_pairs={{0,1},{1,0},{2,3},{3,2},{4,5},{5,4},{6,7},{7,6},{8,9},{9,8},{10,11... | collective-permute-start | bytes 1572872 | tf_op jit(solution)/shard_map/ppermute | solution.py:29
  248.7 5.0 %collective-permute-start.30 = (f32[256,128]{1,0:T(8,128)S(1)}, f32[256,128]{1,0:T(8,128)S(1)}, u32[]{:S(2)}, u32[]{:S(2)}) collective-permute-start(f32[256,128]{1,0:T(8,128)S(1)} %get-tuple-element.30), channel_id=1, source_target_pairs={{0,128},{128,0},{1,129},{129,1},{2,130},{130,2},{3,131},{131,3},{4... | collective-permute-start | bytes 393224 | tf_op jit(solution)/shard_map/ppermute | solution.py:29
  253.7 5.0 %collective-permute-start.33 = (f32[256,128]{1,0:T(8,128)S(1)}, f32[256,128]{1,0:T(8,128)S(1)}, u32[]{:S(2)}, u32[]{:S(2)}) collective-permute-start(f32[256,128]{1,0:T(8,128)S(1)} %add.630), channel_id=1, source_target_pairs={{0,96},{32,0},{64,32},{96,64},{1,97},{33,1},{65,33},{97,65},{2,98}... | collective-permute-start | bytes 393224 | tf_op jit(solution)/shard_map/ppermute | solution.py:29
  255.2 6.5 %collective-permute-start.32 = (f32[256,128]{1,0:T(8,128)S(1)}, f32[256,128]{1,0:T(8,128)S(1)}, u32[]{:S(2)}, u32[]{:S(2)}) collective-permute-start(f32[256,128]{1,0:T(8,128)S(1)} %add.630), channel_id=1, source_target_pairs={{0,64},{32,96},{64,0},{96,32},{1,65},{33,97},{65,1},{97,33},{2,66}... | collective-permute-start | bytes 393224 | tf_op jit(solution)/shard_map/ppermute | solution.py:29
  256.7 6.4 %collective-permute-start.31 = (f32[256,128]{1,0:T(8,128)S(1)}, f32[256,128]{1,0:T(8,128)S(1)}, u32[]{:S(2)}, u32[]{:S(2)}) collective-permute-start(f32[256,128]{1,0:T(8,128)S(1)} %add.630), channel_id=1, source_target_pairs={{0,32},{32,64},{64,96},{96,0},{1,33},{33,65},{65,97},{97,1},{2,34}... | collective-permute-start | bytes 393224 | tf_op jit(solution)/shard_map/ppermute | solution.py:29
  (11 other events, 33.9 us)

commit v5 on v4

--- a/solution.py
+++ b/solution.py
@@ -56,11 +56,11 @@
     return jnp.stack([p.reshape(n, 8, ROWS) for p in parts], 1).reshape(32 * n, ROWS)
 
 
-def gather_x(mine, theirs, before=(), between=()):
+def gather_x(mine, theirs, before=(), between=(), after=()):
     near = both_ways(tie(mine, *before), "x")
     near2 = both_ways(tie(theirs, *before), "x")
     far = both_ways(tie(near, *between), "x")
-    return (mine, theirs, near, near2, far, swap(near), swap(near2), swap(far))
+    return (mine, theirs, near, near2, far, swap(near), swap(tie(near2, *after)), swap(tie(far, *after)))
 
 
 def chunks(n, i):
@@ -245,12 +245,13 @@
     cur = exchange(eigvecs)
     pieces43 = gather_x(*ring43)
     near43, far43 = pieces43[2], pieces43[4]
-    ring21 = gather_z(v21, swap(v21), (near43,cur), (), ())
+    ring21 = gather_z(v21, swap(v21), (ring43[1],), (near43, cur), ())
     (w,) = work(cur, None, (), pieces43)
     share = row_share(w)
-    pieces21 = gather_x(*ring21, (far43,), (share,))
+    total = hand_on(share)
+    pieces21 = gather_x(*ring21, (far43,), (), (total,))
     near21, far21 = pieces21[3], pieces21[4]
-    ring0 = gather_z(v[0], swap(v[0]), (far43,), (share,))
+    ring0 = gather_z(v[0], swap(v[0]), (far43,), (total,))
     pieces0 = gather_x(*ring0, (near21,), (far21,))
 
     def ordered(ring, *blocks):
@@ -258,7 +259,7 @@
         part = jnp.stack([tfactor[b] for b in blocks])
         return jnp.einsum("ij,bjk,lk->bil", pick, part, pick, precision=HIGHEST)
 
-    applied = solve(ordered(True, 4, 3), hand_on(share))
+    applied = solve(ordered(True, 4, 3), total)
     cur, w = work(cur, applied, pieces43, pieces21)
     applied = solve(ordered(True, 2, 1), hand_on(row_share(w)))
     cur, w = work(cur, applied, pieces21, pieces0)

time: 272 us -> 245 us (0.901)
  starting transfers between devices: 89.1 us -> 57.7 us
  waiting for transfers between devices: 107 us -> 110 us
    ppermute x19, starting transfers between devices: 40.3 us -> 9.91 us  [shift(): return lax.ppermute(a, axis, [(i, (i + by) % n) for i in range(n)])]
    ppermute x15, waiting for transfers between devices: 79.3 us -> 87.6 us  [both_ways(): return lax.ppermute(a, (axis, 'core'), pairs)]
    all_to_all x2, waiting for transfers between devices: 9.54 us -> 4.86 us  [hand_on(): lax.all_to_all(a, ROW, split_axis=0, concat_axis=0, tiled=True)]
    another operation x6, other arithmetic: 3.22 us -> 5.95 us  [by_block(): jnp.stack([p.reshape(n, 8, ROWS) for p in parts], 1).reshape(32 * n, ROWS)]
    unnamed x40 -> x44, local copies, waits for them, and re-layouts: 5.53 us -> 5.35 us
  transfers between devices with their start and end apart: 39 -> 39, of which waited for: 18 -> 17; matrix products, arithmetic and copies ran while one was open for 11% -> 14% of each run, Pallas kernels for 8% -> 9%
where the time goes in v5:
time: 245 us; the launch traced here: 244 us
  waiting for transfers between devices  110 us (45%)
  starting transfers between devices  57.7 us (24%)
  Pallas kernels  34.2 us (14%)
  local copies, waits for them, and re-layouts  19.7 us (8%)
  other arithmetic  14.9 us (6%)
  matrix products  7.12 us (3%)
    ppermute x15, waiting for transfers between devices, both_ways(): return lax.ppermute(a, (axis, 'core'), pairs)  87.6 us
    pallas_call x4, Pallas kernels, work(): pl.pallas_call(functools.partial(work_kernel, bool(old), bool(new)), grid...  29.8 us
    ppermute x15, starting transfers between devices, both_ways(): return lax.ppermute(a, (axis, 'core'), pairs)  17 us
    all_to_all x2, starting transfers between devices, row_share(): lax.all_to_all(a.reshape(8, n // 8, width), ROW, split_axis=0, concat_axi...  11.9 us
    ppermute x19, waiting for transfers between devices, shift(): return lax.ppermute(a, axis, [(i, (i + by) % n) for i in range(n)])  11.6 us
    all_to_all x2, starting transfers between devices, hand_on(): lax.all_to_all(a, ROW, split_axis=0, concat_axis=0, tiled=True)  10 us
    ppermute x19, starting transfers between devices, shift(): return lax.ppermute(a, axis, [(i, (i + by) % n) for i in range(n)])  9.91 us
    all_to_all x1, starting transfers between devices, exchange(): lax.all_to_all(eigvecs.T.reshape(32, K, 128), COL, split_axis=0, concat_a...  8.78 us
  transfers between devices with their start and end apart: 39, of which 17 were waited for; matrix products, arithmetic and copies ran while one was open for 14% of the time, Pallas kernels for 9%

profile of v5, /device:TPU:32, one launch (start us, length us, event | category | flops | bytes accessed | tf_op | source)
XLA Modules:
  0.0 244.2 jit_solution(7808644586763905686)
XLA Ops:
  0.0 2.1 slice_bitcast_fusion.17
  2.2 1.5 collective-permute-done
  4.5 3.3 %collective-permute-start.1 = (f32[32,4096]{1,0:T(8,128)S(1)}, f32[32,4096]{1,0:T(8,128)S(1)}, u32[]{:S(2)}, u32[]{:S(2)}) collective-permute-start(f32[32,4096]{1,0:T(8,128)S(1)} %pad_maximum_fusion.6), channel_id=1, source_target_pairs={{0,8},{1,25},{8,16},{9,1},{16,24},{17,9},{24,0},{25,17},{2,10},{3,... | collective-permute-start | bytes 1572872 | tf_op jit(solution)/shard_map/ppermute | solution.py:37
  7.8 14.9 %collective-permute-done.1 = f32[32,4096]{1,0:T(8,128)S(1)} collective-permute-done((f32[32,4096]{1,0:T(8,128)S(1)}, f32[32,4096]{1,0:T(8,128)S(1)}, u32[]{:S(2)}, u32[]{:S(2)}) %collective-permute-start.1) | collective-permute-done | bytes 524320 | tf_op jit(solution)/shard_map/ppermute | solution.py:37
  23.9 1.8 copy.21
  25.7 8.8 %all-to-all-start = ((f32[32,128,128]{2,1,0:T(8,128)}), f32[32,128,128]{2,1,0:T(8,128)}, u32[]{:S(2)}, u32[]{:S(2)}) async-start(f32[32,128,128]{2,1,0:T(8,128)} %bitcast.1), calls=%async_computation | async-start | bytes 4194304 | tf_op jit(solution)/shard_map/all_to_all | solution.py:87
  38.0 1.8 collective-permute-start.4
  39.9 1.5 collective-permute-start.5
  41.5 30.0 %collective-permute-done.4.refs_3_.refs_4_ = f32[64,4096]{1,0:T(8,128)S(1)} collective-permute-done((f32[64,4096]{1,0:T(8,128)S(1)}, f32[64,4096]{1,0:T(8,128)S(1)}, u32[]{:S(2)}, u32[]{:S(2)}) %collective-permute-start.4) | collective-permute-done | bytes 1048608 | tf_op jit(solution)/shard_map/ppermute | solution.py:37
  72.4 2.4 collective-permute-start.11
  74.8 1.6 collective-permute-start.20
  77.2 2.2 fusion.28
  79.4 4.2 %collective-permute-done.5.refs_4_.refs_5_ = f32[64,4096]{1,0:T(8,128)} collective-permute-done((f32[64,4096]{1,0:T(8,128)S(1)}, f32[64,4096]{1,0:T(8,128)}, u32[]{:S(2)}, u32[]{:S(2)}) %collective-permute-start.5) | collective-permute-done | bytes 1048608 | tf_op jit(solution)/shard_map/ppermute | solution.py:37
  83.6 11.2 %collective-permute-done.6.refs_5_.refs_6_ = f32[64,4096]{1,0:T(8,128)} collective-permute-done((f32[64,4096]{1,0:T(8,128)S(1)}, f32[64,4096]{1,0:T(8,128)}, u32[]{:S(2)}, u32[]{:S(2)}) %collective-permute-start.6) | collective-permute-done | bytes 1048608 | tf_op jit(solution)/shard_map/ppermute | solution.py:37
  94.8 1.9 collective-permute-done.11
  96.7 1.9 slice_bitcast_fusion.19
  100.5 6.6 %work.4 = f32[1024,128]{1,0:T(8,128)S(1)} custom-call(f32[32,128,128]{2,1,0:T(8,128)} %all-to-all-done.refs_0_, f32[64,4096]{1,0:T(8,128)S(1)} %bitcast.146, f32[64,4096]{1,0:T(8,128)S(1)} %bitcast.149, f32[64,4096]{1,0:T(8,128)S(1)} %collective-permute-done.4.refs_3_.refs_4_, f32[64,4096]{1,0:T(8,128)} %collective-permute-done.5.refs_4_.refs_5_, ...), custom_call_target="tpu_custom_call" | custom-call | flops 1610612736 | bytes 12582912 | tf_op jit(solution)/shard_map/work/pallas_call | solution.py:202
  107.9 6.2 %all-to-all-start.1 = ((f32[8,128,128]{2,1,0:T(8,128)}), f32[8,128,128]{2,1,0:T(8,128)S(1)}, u32[]{:S(2)}, u32[]{:S(2)}) async-start(f32[8,128,128]{2,1,0:T(8,128)} %bitcast.152), calls=%async_computation.1 | async-start | bytes 1048576 | tf_op jit(solution)/shard_map/all_to_all | solution.py:92
  114.1 2.1 pad_maximum_fusion.5
  117.2 1.7 pad_maximum_fusion.11
  118.9 2.7 %collective-permute-start.21 = (f32[16,4096]{1,0:T(8,128)}, f32[16,4096]{1,0:T(8,128)S(1)}, u32[]{:S(2)}, u32[]{:S(2)}) collective-permute-start(f32[16,4096]{1,0:T(8,128)} %pad_maximum_fusion.11), channel_id=1, source_target_pairs={{0,8},{1,25},{8,16},{9,1},{16,24},{17,9},{24,0},{25,17},{2,10},{3,... | collective-permute-start | bytes 786440 | tf_op jit(solution)/shard_map/ppermute | solution.py:37
  121.5 2.1 pad_maximum_fusion.2
  124.8 5.4 %all-to-all-start.2 = ((f32[8,128,128]{2,1,0:T(8,128)}), f32[8,128,128]{2,1,0:T(8,128)S(1)}, u32[]{:S(2)}, u32[]{:S(2)}) async-start(f32[8,128,128]{2,1,0:T(8,128)} %broadcast_in_dim.4), calls=%async_computation.2 | async-start | bytes 1048576 | tf_op jit(solution)/shard_map/all_to_all | solution.py:99
  131.4 2.0 pad_maximum_fusion.3
  133.5 1.4 collective-permute-start.15
  134.8 5.1 %collective-permute-done.14.refs_12_.refs_4_ = f32[64,4096]{1,0:T(8,128)} collective-permute-done((f32[64,4096]{1,0:T(8,128)}, f32[64,4096]{1,0:T(8,128)}, u32[]{:S(2)}, u32[]{:S(2)}) %collective-permute-start.14) | collective-permute-done | bytes 1048608 | tf_op jit(solution)/shard_map/ppermute | solution.py:37
  141.9 1.7 collective-permute-start.17
  143.6 7.5 %collective-permute-done.15.refs_13_.refs_5_ = f32[64,4096]{1,0:T(8,128)} collective-permute-done((f32[64,4096]{1,0:T(8,128)}, f32[64,4096]{1,0:T(8,128)}, u32[]{:S(2)}, u32[]{:S(2)}) %collective-permute-start.15) | collective-permute-done | bytes 1048608 | tf_op jit(solution)/shard_map/ppermute | solution.py:37
  151.1 11.2 %collective-permute-done.16.refs_14_.refs_6_ = f32[64,4096]{1,0:T(8,128)} collective-permute-done((f32[64,4096]{1,0:T(8,128)}, f32[64,4096]{1,0:T(8,128)}, u32[]{:S(2)}, u32[]{:S(2)}) %collective-permute-start.16) | collective-permute-done | bytes 1048608 | tf_op jit(solution)/shard_map/ppermute | solution.py:37
  162.4 1.5 fusion.15.t_ref
  163.9 1.5 solve.3.refs_1_
  170.0 10.4 %work.5 = (f32[128,4096]{1,0:T(8,128)}, f32[1024,128]{1,0:T(8,128)S(1)}) custom-call(f32[32,128,128]{2,1,0:T(8,128)} %all-to-all-done.refs_0_, f32[128,512]{1,0:T(8,128)S(1)} %solve.3.refs_1_, f32[64,4096]{1,0:T(8,128)S(1)} %bitcast.147, f32[64,4096]{1,0:T(8,128)S(1)} %bitcast.150, f32[64,4096]{1,0:T(8,128)S(1)} %copy-done.1, ...), custom_call_target="tpu_custom_call" | custom-call | flops 3221225472 | bytes 20971520 | tf_op jit(solution)/shard_map/work/pallas_call | solution.py:202
  181.2 5.7 %all-to-all-start.3 = ((f32[8,128,128]{2,1,0:T(8,128)}), f32[8,128,128]{2,1,0:T(8,128)S(1)}, u32[]{:S(2)}, u32[]{:S(2)}) async-start(f32[8,128,128]{2,1,0:T(8,128)} %bitcast.153), calls=%async_computation.3 | async-start | bytes 1048576 | tf_op jit(solution)/shard_map/all_to_all | solution.py:92
  188.4 2.4 collective-permute-start.26
  190.8 5.9 %all-to-all-done.3 = f32[8,128,128]{2,1,0:T(8,128)S(1)} async-done(((f32[8,128,128]{2,1,0:T(8,128)}), f32[8,128,128]{2,1,0:T(8,128)S(1)}, u32[]{:S(2)}, u32[]{:S(2)}) %all-to-all-start.3) | async-done | bytes 524320 | tf_op jit(solution)/shard_map/all_to_all | solution.py:92
  197.6 4.6 %all-to-all-start.4 = ((f32[8,128,128]{2,1,0:T(8,128)}), f32[8,128,128]{2,1,0:T(8,128)}, u32[]{:S(2)}, u32[]{:S(2)}) async-start(f32[8,128,128]{2,1,0:T(8,128)} %broadcast_in_dim.5), calls=%async_computation.4 | async-start | bytes 1048576 | tf_op jit(solution)/shard_map/all_to_all | solution.py:99
  202.7 1.5 collective-permute-done.26.refs_14_.refs_6_
  204.2 1.4 fusion.4
  206.9 4.9 %all-to-all-done.4 = f32[8,128,128]{2,1,0:T(8,128)} async-done(((f32[8,128,128]{2,1,0:T(8,128)}), f32[8,128,128]{2,1,0:T(8,128)}, u32[]{:S(2)}, u32[]{:S(2)}) %all-to-all-start.4) | async-done | bytes 524320 | tf_op jit(solution)/shard_map/all_to_all | solution.py:99
  212.8 2.5 %solve.4.refs_1_ = f32[128,512]{1,0:T(8,128)S(1)} custom-call(f32[2,256,256]{2,1,0:T(8,128)S(1)} %copy-done.2, f32[1024,128]{1,0:T(8,128)} %bitcast.79.w_ref), custom_call_target="tpu_custom_call" | custom-call | flops 201326592 | bytes 1048576 | tf_op jit(solution)/shard_map/solve/pallas_call | solution.py:231
  215.3 7.8 %work.6 = (f32[128,4096]{1,0:T(8,128)}, f32[256,128]{1,0:T(8,128)S(1)}) custom-call(f32[128,4096]{1,0:T(8,128)} %get-tuple-element.26.refs_0_, f32[128,512]{1,0:T(8,128)S(1)} %solve.4.refs_1_, f32[64,4096]{1,0:T(8,128)} %bitcast.68.refs_10_.refs_2_, f32[64,4096]{1,0:T(8,128)} %bitcast.77.refs_11_.refs_3_, ...), custom_call_target="tpu_custom_call" | custom-call | flops 2415919104 | bytes 16777216 | tf_op jit(solution)/shard_map/work/pallas_call | solution.py:202
  223.8 4.5 %collective-permute-done.30 = f32[256,128]{1,0:T(8,128)S(1)} collective-permute-done((f32[256,128]{1,0:T(8,128)S(1)}, f32[256,128]{1,0:T(8,128)S(1)}, u32[]{:S(2)}, u32[]{:S(2)}) %collective-permute-start.30) | collective-permute-done | bytes 131104 | tf_op jit(solution)/shard_map/ppermute | solution.py:29
  228.3 1.8 collective-permute-start.33
  230.1 1.5 collective-permute-start.32
  233.2 1.8 collective-permute-done.33
  235.1 2.3 collective-permute-done.32
  237.4 1.3 collective-permute-done.31
  239.2 5.0 %work.7 = f32[4096,128]{1,0:T(8,128)} custom-call(f32[128,4096]{1,0:T(8,128)} %get-tuple-element.33.refs_0_, f32[128,256]{1,0:T(8,128)S(1)} %solve.5.refs_1_, f32[32,4096]{1,0:T(8,128)S(1)} %maximum_bitcast_fusion.refs_10_.refs_2_, f32[32,4096]{1,0:T(8,128)S(1)} %maximum_bitcast_fusion.1.refs_11_.refs_3_, ...), custom_call_target="tpu_custom_call" | custom-call | flops 805306368 | bytes 8388608 | tf_op jit(solution)/shard_map/work/pallas_call | solution.py:202
  (120 shorter events, 28.6 us)
Async XLA Ops:
  0.0 23.9 %copy-start.7 = (f32[128,4096]{1,0:T(8,128)S(1)}, f32[128,4096]{1,0:T(8,128)}, u32[]{:S(2)}) copy-start(f32[128,4096]{1,0:T(8,128)} %param.3) | copy-start | bytes 6291460
  2.1 1.6 collective-permute-start
  4.5 18.3 %collective-permute-start.1 = (f32[32,4096]{1,0:T(8,128)S(1)}, f32[32,4096]{1,0:T(8,128)S(1)}, u32[]{:S(2)}, u32[]{:S(2)}) collective-permute-start(f32[32,4096]{1,0:T(8,128)S(1)} %pad_maximum_fusion.6), channel_id=1, source_target_pairs={{0,8},{1,25},{8,16},{9,1},{16,24},{17,9},{24,0},{25,17},{2,10},{3,... | collective-permute-start | bytes 1572872 | tf_op jit(solution)/shard_map/ppermute | solution.py:37
  23.6 11.0 %collective-permute-start.2 = (f32[16,4096]{1,0:T(8,128)}, f32[16,4096]{1,0:T(8,128)}, u32[]{:S(2)}, u32[]{:S(2)}) collective-permute-start(f32[16,4096]{1,0:T(8,128)} %get-tuple-element.56), channel_id=1, source_target_pairs={{0,8},{1,25},{8,16},{9,1},{16,24},{17,9},{24,0},{25,17},{2,10},{3,... | collective-permute-start | bytes 786440 | tf_op jit(solution)/shard_map/ppermute | solution.py:37
  25.7 72.9 %all-to-all-start = ((f32[32,128,128]{2,1,0:T(8,128)}), f32[32,128,128]{2,1,0:T(8,128)}, u32[]{:S(2)}, u32[]{:S(2)}) async-start(f32[32,128,128]{2,1,0:T(8,128)} %bitcast.1), calls=%async_computation | async-start | bytes 4194304 | tf_op jit(solution)/shard_map/all_to_all | solution.py:87
  35.6 4.2 %collective-permute-start.3 = (f32[48,4096]{1,0:T(8,128)S(1)}, f32[48,4096]{1,0:T(8,128)S(1)}, u32[]{:S(2)}, u32[]{:S(2)}) collective-permute-start(f32[48,4096]{1,0:T(8,128)S(1)} %pad_maximum_fusion.4), channel_id=1, source_target_pairs={{0,1},{1,0},{2,3},{3,2},{4,5},{5,4},{6,7},{7,6},{8,9},{9,8},{10,11... | collective-permute-start | bytes 2359304 | tf_op jit(solution)/shard_map/ppermute | solution.py:29
  36.6 34.9 %collective-permute-start.10 = (f32[16,4096]{1,0:T(8,128)S(1)}, f32[16,4096]{1,0:T(8,128)S(1)}, u32[]{:S(2)}, u32[]{:S(2)}) collective-permute-start(f32[16,4096]{1,0:T(8,128)S(1)} %get-tuple-element.64), channel_id=1, source_target_pairs={{0,1},{1,0},{2,3},{3,2},{4,5},{5,4},{6,7},{7,6},{8,9},{9,8},{10,11... | collective-permute-start | bytes 786440 | tf_op jit(solution)/shard_map/ppermute | solution.py:29
  38.0 33.5 %collective-permute-start.4 = (f32[64,4096]{1,0:T(8,128)S(1)}, f32[64,4096]{1,0:T(8,128)S(1)}, u32[]{:S(2)}, u32[]{:S(2)}) collective-permute-start(f32[64,4096]{1,0:T(8,128)S(1)} %bitcast.145), channel_id=1, source_target_pairs={{0,2},{1,7},{2,4},{3,1},{4,6},{5,3},{6,0},{7,5},{8,10},{9,15},{10,... | collective-permute-start | bytes 3145736 | tf_op jit(solution)/shard_map/ppermute | solution.py:37
  39.9 43.6 %collective-permute-start.5 = (f32[64,4096]{1,0:T(8,128)S(1)}, f32[64,4096]{1,0:T(8,128)}, u32[]{:S(2)}, u32[]{:S(2)}) collective-permute-start(f32[64,4096]{1,0:T(8,128)S(1)} %bitcast.148), channel_id=1, source_target_pairs={{0,2},{1,7},{2,4},{3,1},{4,6},{5,3},{6,0},{7,5},{8,10},{9,15},{10,... | collective-permute-start | bytes 3145736 | tf_op jit(solution)/shard_map/ppermute | solution.py:37
  71.5 29.0 %copy-start = (f32[64,4096]{1,0:T(8,128)}, f32[64,4096]{1,0:T(8,128)S(1)}, u32[]{:S(2)}) copy-start(f32[64,4096]{1,0:T(8,128)S(1)} %collective-permute-done.4.refs_3_.refs_4_) | copy-start | bytes 3145732
  71.5 23.3 %collective-permute-start.6 = (f32[64,4096]{1,0:T(8,128)S(1)}, f32[64,4096]{1,0:T(8,128)}, u32[]{:S(2)}, u32[]{:S(2)}) collective-permute-start(f32[64,4096]{1,0:T(8,128)S(1)} %collective-permute-done.4.refs_3_.refs_4_), channel_id=1, source_target_pairs={{0,2},{1,7},{2,4},{3,1},{4,6},{5,3},{6,0},{7,5},{8,10},{9,15},{10,... | collective-permute-start | bytes 3145736 | tf_op jit(solution)/shard_map/ppermute | solution.py:37
  72.4 24.3 %collective-permute-start.11 = (f32[32,4096]{1,0:T(8,128)}, f32[32,4096]{1,0:T(8,128)}, u32[]{:S(2)}, u32[]{:S(2)}) collective-permute-start(f32[32,4096]{1,0:T(8,128)} %pad_maximum_fusion.7), channel_id=1, source_target_pairs={{0,8},{1,25},{8,16},{9,1},{16,24},{17,9},{24,0},{25,17},{2,10},{3,... | collective-permute-start | bytes 1572872 | tf_op jit(solution)/shard_map/ppermute | solution.py:37
  74.8 42.4 %collective-permute-start.20 = (f32[8,4096]{1,0:T(8,128)}, f32[8,4096]{1,0:T(8,128)S(1)}, u32[]{:S(2)}, u32[]{:S(2)}) collective-permute-start(f32[8,4096]{1,0:T(8,128)} %get-tuple-element.46), channel_id=1, source_target_pairs={{0,1},{1,0},{2,3},{3,2},{4,5},{5,4},{6,7},{7,6},{8,9},{9,8},{10,11... | collective-permute-start | bytes 393224 | tf_op jit(solution)/shard_map/ppermute | solution.py:29
  79.4 21.1 %collective-permute-start.7 = (f32[64,4096]{1,0:T(8,128)S(1)}, f32[64,4096]{1,0:T(8,128)}, u32[]{:S(2)}, u32[]{:S(2)}) collective-permute-start(f32[64,4096]{1,0:T(8,128)S(1)} %collective-permute-done.4.refs_3_.refs_4_), channel_id=1, source_target_pairs={{0,1},{1,0},{2,3},{3,2},{4,5},{5,4},{6,7},{7,6},{8,9},{9,8},{10,11... | collective-permute-start | bytes 3145736 | tf_op jit(solution)/shard_map/ppermute | solution.py:29
  83.6 16.9 %collective-permute-start.8 = (f32[64,4096]{1,0:T(8,128)}, f32[64,4096]{1,0:T(8,128)}, u32[]{:S(2)}, u32[]{:S(2)}) collective-permute-start(f32[64,4096]{1,0:T(8,128)} %collective-permute-done.5.refs_4_.refs_5_), channel_id=1, source_target_pairs={{0,1},{1,0},{2,3},{3,2},{4,5},{5,4},{6,7},{7,6},{8,9},{9,8},{10,11... | collective-permute-start | bytes 3145736 | tf_op jit(solution)/shard_map/ppermute | solution.py:29
  94.8 5.7 %collective-permute-start.9 = (f32[64,4096]{1,0:T(8,128)}, f32[64,4096]{1,0:T(8,128)}, u32[]{:S(2)}, u32[]{:S(2)}) collective-permute-start(f32[64,4096]{1,0:T(8,128)} %collective-permute-done.6.refs_5_.refs_6_), channel_id=1, source_target_pairs={{0,1},{1,0},{2,3},{3,2},{4,5},{5,4},{6,7},{7,6},{8,9},{9,8},{10,11... | collective-permute-start | bytes 3145736 | tf_op jit(solution)/shard_map/ppermute | solution.py:29
  98.7 15.5 %collective-permute-start.12 = (f32[16,4096]{1,0:T(8,128)}, f32[16,4096]{1,0:T(8,128)S(1)}, u32[]{:S(2)}, u32[]{:S(2)}) collective-permute-start(f32[16,4096]{1,0:T(8,128)} %get-tuple-element.21), channel_id=1, source_target_pairs={{0,8},{1,25},{8,16},{9,1},{16,24},{17,9},{24,0},{25,17},{2,10},{3,... | collective-permute-start | bytes 786440 | tf_op jit(solution)/shard_map/ppermute | solution.py:37
  107.9 13.6 %copy-start.8 = (f32[2,1,8,4096]{3,2,1,0:T(8,128)S(1)}, f32[2,1,8,4096]{3,2,1,0:T(8,128)}, u32[]{:S(2)}) copy-start(f32[2,1,8,4096]{3,2,1,0:T(8,128)} %get-tuple-element.63) | copy-start | bytes 786436
  107.9 13.6 %copy-start.12 = (f32[2,1,8,4096]{3,2,1,0:T(8,128)S(1)}, f32[2,1,8,4096]{3,2,1,0:T(8,128)}, u32[]{:S(2)}) copy-start(f32[2,1,8,4096]{3,2,1,0:T(8,128)} %get-tuple-element.51) | copy-start | bytes 786436
  107.9 16.0 %all-to-all-start.1 = ((f32[8,128,128]{2,1,0:T(8,128)}), f32[8,128,128]{2,1,0:T(8,128)S(1)}, u32[]{:S(2)}, u32[]{:S(2)}) async-start(f32[8,128,128]{2,1,0:T(8,128)} %bitcast.152), calls=%async_computation.1 | async-start | bytes 1048576 | tf_op jit(solution)/shard_map/all_to_all | solution.py:92
  116.2 14.0 %collective-permute-start.13 = (f32[48,4096]{1,0:T(8,128)}, f32[48,4096]{1,0:T(8,128)}, u32[]{:S(2)}, u32[]{:S(2)}) collective-permute-start(f32[48,4096]{1,0:T(8,128)} %pad_maximum_fusion.5), channel_id=1, source_target_pairs={{0,1},{1,0},{2,3},{3,2},{4,5},{5,4},{6,7},{7,6},{8,9},{9,8},{10,11... | collective-permute-start | bytes 2359304 | tf_op jit(solution)/shard_map/ppermute | solution.py:29
  118.9 22.3 %collective-permute-start.21 = (f32[16,4096]{1,0:T(8,128)}, f32[16,4096]{1,0:T(8,128)S(1)}, u32[]{:S(2)}, u32[]{:S(2)}) collective-permute-start(f32[16,4096]{1,0:T(8,128)} %pad_maximum_fusion.11), channel_id=1, source_target_pairs={{0,8},{1,25},{8,16},{9,1},{16,24},{17,9},{24,0},{25,17},{2,10},{3,... | collective-permute-start | bytes 786440 | tf_op jit(solution)/shard_map/ppermute | solution.py:37
  123.6 16.3 %collective-permute-start.14 = (f32[64,4096]{1,0:T(8,128)}, f32[64,4096]{1,0:T(8,128)}, u32[]{:S(2)}, u32[]{:S(2)}) collective-permute-start(f32[64,4096]{1,0:T(8,128)} %bitcast.68.refs_10_.refs_2_), channel_id=1, source_target_pairs={{0,2},{1,7},{2,4},{3,1},{4,6},{5,3},{6,0},{7,5},{8,10},{9,15},{10,... | collective-permute-start | bytes 3145736 | tf_op jit(solution)/shard_map/ppermute | solution.py:37
  124.8 18.8 %all-to-all-start.2 = ((f32[8,128,128]{2,1,0:T(8,128)}), f32[8,128,128]{2,1,0:T(8,128)S(1)}, u32[]{:S(2)}, u32[]{:S(2)}) async-start(f32[8,128,128]{2,1,0:T(8,128)} %broadcast_in_dim.4), calls=%async_computation.2 | async-start | bytes 1048576 | tf_op jit(solution)/shard_map/all_to_all | solution.py:99
  130.2 9.7 %copy-start.21 = (s32[256]{0:T(256)S(1)}, s32[256]{0:T(256)}, u32[]{:S(2)}) copy-start(s32[256]{0:T(256)} %add.629) | copy-start | bytes 3076
  133.5 17.7 %collective-permute-start.15 = (f32[64,4096]{1,0:T(8,128)}, f32[64,4096]{1,0:T(8,128)}, u32[]{:S(2)}, u32[]{:S(2)}) collective-permute-start(f32[64,4096]{1,0:T(8,128)} %bitcast.77.refs_11_.refs_3_), channel_id=1, source_target_pairs={{0,2},{1,7},{2,4},{3,1},{4,6},{5,3},{6,0},{7,5},{8,10},{9,15},{10,... | collective-permute-start | bytes 3145736 | tf_op jit(solution)/shard_map/ppermute | solution.py:37
  139.9 22.5 %collective-permute-start.16 = (f32[64,4096]{1,0:T(8,128)}, f32[64,4096]{1,0:T(8,128)}, u32[]{:S(2)}, u32[]{:S(2)}) collective-permute-start(f32[64,4096]{1,0:T(8,128)} %collective-permute-done.14.refs_12_.refs_4_), channel_id=1, source_target_pairs={{0,2},{1,7},{2,4},{3,1},{4,6},{5,3},{6,0},{7,5},{8,10},{9,15},{10,... | collective-permute-start | bytes 3145736 | tf_op jit(solution)/shard_map/ppermute | solution.py:37
  141.9 26.1 %collective-permute-start.17 = (f32[64,4096]{1,0:T(8,128)}, f32[64,4096]{1,0:T(8,128)}, u32[]{:S(2)}, u32[]{:S(2)}) collective-permute-start(f32[64,4096]{1,0:T(8,128)} %collective-permute-done.14.refs_12_.refs_4_), channel_id=1, source_target_pairs={{0,1},{1,0},{2,3},{3,2},{4,5},{5,4},{6,7},{7,6},{8,9},{9,8},{10,11... | collective-permute-start | bytes 3145736 | tf_op jit(solution)/shard_map/ppermute | solution.py:29
  143.6 23.1 %copy-start.18 = (f32[1,1,8,4096]{3,2,1,0:T(8,128)S(1)}, f32[1,1,8,4096]{3,2,1,0:T(8,128)}, u32[]{:S(2)}) copy-start(f32[1,1,8,4096]{3,2,1,0:T(8,128)} %get-tuple-element.61) | copy-start | bytes 393220
  143.6 26.4 %copy-start.1 = (f32[64,4096]{1,0:T(8,128)S(1)}, f32[64,4096]{1,0:T(8,128)}, u32[]{:S(2)}) copy-start(f32[64,4096]{1,0:T(8,128)} %copy-done) | copy-start | bytes 3145732
  143.6 21.8 %collective-permute-start.22 = (f32[8,4096]{1,0:T(8,128)}, f32[8,4096]{1,0:T(8,128)S(1)}, u32[]{:S(2)}, u32[]{:S(2)}) collective-permute-start(f32[8,4096]{1,0:T(8,128)} %get-tuple-element.29), channel_id=1, source_target_pairs={{0,8},{1,25},{8,16},{9,1},{16,24},{17,9},{24,0},{25,17},{2,10},{3,... | collective-permute-start | bytes 393224 | tf_op jit(solution)/shard_map/ppermute | solution.py:37
  151.1 16.9 %collective-permute-start.18 = (f32[64,4096]{1,0:T(8,128)}, f32[64,4096]{1,0:T(8,128)S(1)}, u32[]{:S(2)}, u32[]{:S(2)}) collective-permute-start(f32[64,4096]{1,0:T(8,128)} %collective-permute-done.15.refs_13_.refs_5_), channel_id=1, source_target_pairs={{0,1},{1,0},{2,3},{3,2},{4,5},{5,4},{6,7},{7,6},{8,9},{9,8},{10,11... | collective-permute-start | bytes 3145736 | tf_op jit(solution)/shard_map/ppermute | solution.py:29
  162.4 5.6 %collective-permute-start.19 = (f32[64,4096]{1,0:T(8,128)}, f32[64,4096]{1,0:T(8,128)S(1)}, u32[]{:S(2)}, u32[]{:S(2)}) collective-permute-start(f32[64,4096]{1,0:T(8,128)} %collective-permute-done.16.refs_14_.refs_6_), channel_id=1, source_target_pairs={{0,1},{1,0},{2,3},{3,2},{4,5},{5,4},{6,7},{7,6},{8,9},{9,8},{10,11... | collective-permute-start | bytes 3145736 | tf_op jit(solution)/shard_map/ppermute | solution.py:29
  166.2 20.7 %collective-permute-start.23 = (f32[24,4096]{1,0:T(8,128)}, f32[24,4096]{1,0:T(8,128)}, u32[]{:S(2)}, u32[]{:S(2)}) collective-permute-start(f32[24,4096]{1,0:T(8,128)} %pad_maximum_fusion.8), channel_id=1, source_target_pairs={{0,1},{1,0},{2,3},{3,2},{4,5},{5,4},{6,7},{7,6},{8,9},{9,8},{10,11... | collective-permute-start | bytes 1179656 | tf_op jit(solution)/shard_map/ppermute | solution.py:29
  167.7 20.3 %copy-start.20 = (f32[8,4096]{1,0:T(8,128)S(1)}, f32[8,4096]{1,0:T(8,128)}, u32[]{:S(2)}) copy-start(f32[8,4096]{1,0:T(8,128)} %copy-done.19) | copy-start | bytes 393220
  167.7 20.7 %collective-permute-start.24 = (f32[32,4096]{1,0:T(8,128)S(1)}, f32[32,4096]{1,0:T(8,128)S(1)}, u32[]{:S(2)}, u32[]{:S(2)}) collective-permute-start(f32[32,4096]{1,0:T(8,128)S(1)} %maximum_bitcast_fusion.refs_10_.refs_2_), channel_id=1, source_target_pairs={{0,2},{1,7},{2,4},{3,1},{4,6},{5,3},{6,0},{7,5},{8,10},{9,15},{10,... | collective-permute-start | bytes 1572872 | tf_op jit(solution)/shard_map/ppermute | solution.py:37
  181.2 15.5 %all-to-all-start.3 = ((f32[8,128,128]{2,1,0:T(8,128)}), f32[8,128,128]{2,1,0:T(8,128)S(1)}, u32[]{:S(2)}, u32[]{:S(2)}) async-start(f32[8,128,128]{2,1,0:T(8,128)} %bitcast.153), calls=%async_computation.3 | async-start | bytes 1048576 | tf_op jit(solution)/shard_map/all_to_all | solution.py:92
  186.9 17.3 %copy-start.9 = (f32[1,256,256]{2,1,0:T(8,128)S(1)}, f32[1,256,256]{2,1,0:T(8,128)}, u32[]{:S(2)}) copy-start(f32[1,256,256]{2,1,0:T(8,128)} %get-tuple-element.35) | copy-start | bytes 786436
  188.1 14.2 %collective-permute-start.25 = (f32[32,4096]{1,0:T(8,128)S(1)}, f32[32,4096]{1,0:T(8,128)S(1)}, u32[]{:S(2)}, u32[]{:S(2)}) collective-permute-start(f32[32,4096]{1,0:T(8,128)S(1)} %maximum_bitcast_fusion.1.refs_11_.refs_3_), channel_id=1, source_target_pairs={{0,2},{1,7},{2,4},{3,1},{4,6},{5,3},{6,0},{7,5},{8,10},{9,15},{10,... | collective-permute-start | bytes 1572872 | tf_op jit(solution)/shard_map/ppermute | solution.py:37
  188.4 15.7 %collective-permute-start.26 = (f32[32,4096]{1,0:T(8,128)S(1)}, f32[32,4096]{1,0:T(8,128)S(1)}, u32[]{:S(2)}, u32[]{:S(2)}) collective-permute-start(f32[32,4096]{1,0:T(8,128)S(1)} %collective-permute-done.24.refs_12_.refs_4_), channel_id=1, source_target_pairs={{0,2},{1,7},{2,4},{3,1},{4,6},{5,3},{6,0},{7,5},{8,10},{9,15},{10,... | collective-permute-start | bytes 1572872 | tf_op jit(solution)/shard_map/ppermute | solution.py:37
  197.6 14.1 %all-to-all-start.4 = ((f32[8,128,128]{2,1,0:T(8,128)}), f32[8,128,128]{2,1,0:T(8,128)}, u32[]{:S(2)}, u32[]{:S(2)}) async-start(f32[8,128,128]{2,1,0:T(8,128)} %broadcast_in_dim.5), calls=%async_computation.4 | async-start | bytes 1048576 | tf_op jit(solution)/shard_map/all_to_all | solution.py:99
  202.2 13.1 %collective-permute-start.27 = (f32[32,4096]{1,0:T(8,128)S(1)}, f32[32,4096]{1,0:T(8,128)S(1)}, u32[]{:S(2)}, u32[]{:S(2)}) collective-permute-start(f32[32,4096]{1,0:T(8,128)S(1)} %collective-permute-done.24.refs_12_.refs_4_), channel_id=1, source_target_pairs={{0,1},{1,0},{2,3},{3,2},{4,5},{5,4},{6,7},{7,6},{8,9},{9,8},{10,11... | collective-permute-start | bytes 1572872 | tf_op jit(solution)/shard_map/ppermute | solution.py:29
  202.2 13.1 %collective-permute-start.28 = (f32[32,4096]{1,0:T(8,128)S(1)}, f32[32,4096]{1,0:T(8,128)}, u32[]{:S(2)}, u32[]{:S(2)}) collective-permute-start(f32[32,4096]{1,0:T(8,128)S(1)} %collective-permute-done.25.refs_13_.refs_5_), channel_id=1, source_target_pairs={{0,1},{1,0},{2,3},{3,2},{4,5},{5,4},{6,7},{7,6},{8,9},{9,8},{10,11... | collective-permute-start | bytes 1572872 | tf_op jit(solution)/shard_map/ppermute | solution.py:29
  204.1 11.2 %collective-permute-start.29 = (f32[32,4096]{1,0:T(8,128)S(1)}, f32[32,4096]{1,0:T(8,128)}, u32[]{:S(2)}, u32[]{:S(2)}) collective-permute-start(f32[32,4096]{1,0:T(8,128)S(1)} %collective-permute-done.26.refs_14_.refs_6_), channel_id=1, source_target_pairs={{0,1},{1,0},{2,3},{3,2},{4,5},{5,4},{6,7},{7,6},{8,9},{9,8},{10,11... | collective-permute-start | bytes 1572872 | tf_op jit(solution)/shard_map/ppermute | solution.py:29
  223.1 5.2 %collective-permute-start.30 = (f32[256,128]{1,0:T(8,128)S(1)}, f32[256,128]{1,0:T(8,128)S(1)}, u32[]{:S(2)}, u32[]{:S(2)}) collective-permute-start(f32[256,128]{1,0:T(8,128)S(1)} %get-tuple-element.34), channel_id=1, source_target_pairs={{0,128},{128,0},{1,129},{129,1},{2,130},{130,2},{3,131},{131,3},{4... | collective-permute-start | bytes 393224 | tf_op jit(solution)/shard_map/ppermute | solution.py:29
  228.3 6.8 %collective-permute-start.33 = (f32[256,128]{1,0:T(8,128)S(1)}, f32[256,128]{1,0:T(8,128)S(1)}, u32[]{:S(2)}, u32[]{:S(2)}) collective-permute-start(f32[256,128]{1,0:T(8,128)S(1)} %add.630), channel_id=1, source_target_pairs={{0,96},{32,0},{64,32},{96,64},{1,97},{33,1},{65,33},{97,65},{2,98}... | collective-permute-start | bytes 393224 | tf_op jit(solution)/shard_map/ppermute | solution.py:29
  230.1 7.3 %collective-permute-start.32 = (f32[256,128]{1,0:T(8,128)S(1)}, f32[256,128]{1,0:T(8,128)S(1)}, u32[]{:S(2)}, u32[]{:S(2)}) collective-permute-start(f32[256,128]{1,0:T(8,128)S(1)} %add.630), channel_id=1, source_target_pairs={{0,64},{32,96},{64,0},{96,32},{1,65},{33,97},{65,1},{97,33},{2,66}... | collective-permute-start | bytes 393224 | tf_op jit(solution)/shard_map/ppermute | solution.py:29
  231.5 7.2 %collective-permute-start.31 = (f32[256,128]{1,0:T(8,128)S(1)}, f32[256,128]{1,0:T(8,128)S(1)}, u32[]{:S(2)}, u32[]{:S(2)}) collective-permute-start(f32[256,128]{1,0:T(8,128)S(1)} %add.630), channel_id=1, source_target_pairs={{0,32},{32,64},{64,96},{96,0},{1,33},{33,65},{65,97},{97,1},{2,34}... | collective-permute-start | bytes 393224 | tf_op jit(solution)/shard_map/ppermute | solution.py:29
  (13 other events, 42.7 us)

commit v6 on v5

--- a/solution.py
+++ b/solution.py
@@ -48,7 +48,7 @@
     got = swap(tie(jnp.concatenate([near, far], 0), *after))
     mine = by_block((v, near[:n], near[n:], far))
     theirs = by_block((other, got[:n], got[n : 2 * n], got[2 * n :]))
-    return mine, theirs
+    return mine, theirs, near
 
 
 def by_block(parts):
@@ -242,17 +242,19 @@
 
     v43, v21 = jnp.concatenate([v[4], v[3]], 0), jnp.concatenate([v[2], v[1]], 0)
     ring43 = gather_z(v43, swap(v43))
-    cur = exchange(eigvecs)
-    pieces43 = gather_x(*ring43)
-    near43, far43 = pieces43[2], pieces43[4]
-    ring21 = gather_z(v21, swap(v21), (ring43[1],), (near43, cur), ())
+    cur = exchange(tie(eigvecs, ring43[2]))
+    mine, theirs, _ = ring43
+    near43, other43 = both_ways(mine, "x"), both_ways(theirs, "x")
+    far43 = both_ways(near43, "x")
+    ring21 = gather_z(v21, swap(v21), (theirs,), (near43, cur), ())
+    pieces43 = (mine, theirs, near43, other43, far43, swap(near43), swap(other43), swap(tie(far43, ring21[0])))
     (w,) = work(cur, None, (), pieces43)
     share = row_share(w)
     total = hand_on(share)
-    pieces21 = gather_x(*ring21, (far43,), (), (total,))
+    pieces21 = gather_x(*ring21[:2], (far43,), (), (total,))
     near21, far21 = pieces21[3], pieces21[4]
     ring0 = gather_z(v[0], swap(v[0]), (far43,), (total,))
-    pieces0 = gather_x(*ring0, (near21,), (far21,))
+    pieces0 = gather_x(*ring0[:2], (near21,), (far21,))
 
     def ordered(ring, *blocks):
         pick = (column_order(ring)[:, None] == jnp.arange(NB)[None, :]).astype(jnp.float32)

time: 245 us -> 252 us (1.029)
  waiting for transfers between devices: 110 us -> 116 us
    all_to_all x2, waiting for transfers between devices: 4.86 us -> 10.3 us  [hand_on(): lax.all_to_all(a, ROW, split_axis=0, concat_axis=0, tiled=True)]
    all_to_all x2, waiting for transfers between devices: 6.17 us -> 8.76 us  [row_share(): lax.all_to_all(a.reshape(8, n // 8, width), ROW, split_axis=0, concat_axi...]
    unnamed x44 -> x40, local copies, waits for them, and re-layouts: 5.35 us -> 7.49 us
  transfers between devices with their start and end apart: 39 -> 39, of which waited for: 17 -> 17; matrix products, arithmetic and copies ran while one was open for 14% -> 13% of each run, Pallas kernels for 9% -> 8%
where the time goes in v6:
time: 252 us; the launch traced here: 251 us
  waiting for transfers between devices  116 us (46%)
  starting transfers between devices  56.1 us (22%)
  Pallas kernels  34.2 us (14%)
  local copies, waits for them, and re-layouts  21.5 us (9%)
  other arithmetic  15.4 us (6%)
  matrix products  7.11 us (3%)
    ppermute x15, waiting for transfers between devices, both_ways(): return lax.ppermute(a, (axis, 'core'), pairs)  85.4 us
    pallas_call x4, Pallas kernels, work(): pl.pallas_call(functools.partial(work_kernel, bool(old), bool(new)), grid...  29.7 us
    ppermute x15, starting transfers between devices, both_ways(): return lax.ppermute(a, (axis, 'core'), pairs)  15.3 us
    all_to_all x2, starting transfers between devices, row_share(): lax.all_to_all(a.reshape(8, n // 8, width), ROW, split_axis=0, concat_axi...  14 us
    ppermute x19, waiting for transfers between devices, shift(): return lax.ppermute(a, axis, [(i, (i + by) % n) for i in range(n)])  11.7 us
    ppermute x19, starting transfers between devices, shift(): return lax.ppermute(a, axis, [(i, (i + by) % n) for i in range(n)])  11.4 us
    all_to_all x2, waiting for transfers between devices, hand_on(): lax.all_to_all(a, ROW, split_axis=0, concat_axis=0, tiled=True)  10.3 us
    all_to_all x2, waiting for transfers between devices, row_share(): lax.all_to_all(a.reshape(8, n // 8, width), ROW, split_axis=0, concat_axi...  8.76 us
  transfers between devices with their start and end apart: 39, of which 17 were waited for; matrix products, arithmetic and copies ran while one was open for 13% of the time, Pallas kernels for 8%

profile of v6, /device:TPU:32, one launch (start us, length us, event | category | flops | bytes accessed | tf_op | source)
XLA Modules:
  0.0 250.8 jit_solution(1912137533353682942)
XLA Ops:
  0.0 1.9 slice_bitcast_fusion.17
  2.1 1.5 collective-permute-done
  4.3 3.3 %collective-permute-start.1 = (f32[32,4096]{1,0:T(8,128)S(1)}, f32[32,4096]{1,0:T(8,128)S(1)}, u32[]{:S(2)}, u32[]{:S(2)}) collective-permute-start(f32[32,4096]{1,0:T(8,128)S(1)} %pad_maximum_fusion.6), channel_id=1, source_target_pairs={{0,8},{1,25},{8,16},{9,1},{16,24},{17,9},{24,0},{25,17},{2,10},{3,... | collective-permute-start | bytes 1572872 | tf_op jit(solution)/shard_map/ppermute | solution.py:37
  7.7 14.9 %collective-permute-done.1 = f32[32,4096]{1,0:T(8,128)S(1)} collective-permute-done((f32[32,4096]{1,0:T(8,128)S(1)}, f32[32,4096]{1,0:T(8,128)S(1)}, u32[]{:S(2)}, u32[]{:S(2)}) %collective-permute-start.1) | collective-permute-done | bytes 524320 | tf_op jit(solution)/shard_map/ppermute | solution.py:37
  24.7 2.1 collective-permute-start.9
  26.8 1.8 copy.21
  28.6 6.8 %all-to-all-start = ((f32[32,128,128]{2,1,0:T(8,128)}), f32[32,128,128]{2,1,0:T(8,128)}, u32[]{:S(2)}, u32[]{:S(2)}) async-start(f32[32,128,128]{2,1,0:T(8,128)} %bitcast.4), calls=%async_computation | async-start | bytes 4194304 | tf_op jit(solution)/shard_map/all_to_all | solution.py:87
  36.8 1.8 pad_maximum_fusion.7
  39.6 1.7 collective-permute-start.4
  41.5 2.4 collective-permute-start.10
  44.0 2.3 collective-permute-start.20
  46.5 25.9 %collective-permute-done.4.refs_3_.refs_4_ = f32[64,4096]{1,0:T(8,128)S(1)} collective-permute-done((f32[64,4096]{1,0:T(8,128)S(1)}, f32[64,4096]{1,0:T(8,128)S(1)}, u32[]{:S(2)}, u32[]{:S(2)}) %collective-permute-start.4) | collective-permute-done | bytes 1048608 | tf_op jit(solution)/shard_map/ppermute | solution.py:37
  72.4 8.9 %collective-permute-done.10 = f32[32,4096]{1,0:T(8,128)} collective-permute-done((f32[32,4096]{1,0:T(8,128)}, f32[32,4096]{1,0:T(8,128)}, u32[]{:S(2)}, u32[]{:S(2)}) %collective-permute-start.10) | collective-permute-done | bytes 524320 | tf_op jit(solution)/shard_map/ppermute | solution.py:37
  81.2 2.0 slice_bitcast_fusion.19
  84.0 1.7 collective-permute-start.7
  85.7 22.7 %collective-permute-done.11 = f32[16,4096]{1,0:T(8,128)} collective-permute-done((f32[16,4096]{1,0:T(8,128)}, f32[16,4096]{1,0:T(8,128)}, u32[]{:S(2)}, u32[]{:S(2)}) %collective-permute-start.11) | collective-permute-done | bytes 262176 | tf_op jit(solution)/shard_map/ppermute | solution.py:37
  108.4 2.2 pad_maximum_fusion.2
  110.6 2.1 pad_maximum_fusion.5
  114.2 1.6 pad_maximum_fusion.11
  118.1 6.6 %work.4 = f32[1024,128]{1,0:T(8,128)S(1)} custom-call(f32[32,128,128]{2,1,0:T(8,128)} %all-to-all-done.refs_0_, f32[64,4096]{1,0:T(8,128)S(1)} %bitcast.146, f32[64,4096]{1,0:T(8,128)S(1)} %bitcast.149, f32[64,4096]{1,0:T(8,128)S(1)} %collective-permute-done.4.refs_3_.refs_4_, f32[64,4096]{1,0:T(8,128)} %collective-permute-done.5.refs_4_.refs_5_, ...), custom_call_target="tpu_custom_call" | custom-call | flops 1610612736 | bytes 12582912 | tf_op jit(solution)/shard_map/work/pallas_call | solution.py:202
  125.5 7.7 %all-to-all-start.1 = ((f32[8,128,128]{2,1,0:T(8,128)}), f32[8,128,128]{2,1,0:T(8,128)S(1)}, u32[]{:S(2)}, u32[]{:S(2)}) async-start(f32[8,128,128]{2,1,0:T(8,128)} %bitcast.152), calls=%async_computation.1 | async-start | bytes 1048576 | tf_op jit(solution)/shard_map/all_to_all | solution.py:92
  134.4 2.1 pad_maximum_fusion.3
  137.4 1.9 collective-permute-start.16
  139.4 3.7 %all-to-all-done.1 = f32[8,128,128]{2,1,0:T(8,128)S(1)} async-done(((f32[8,128,128]{2,1,0:T(8,128)}), f32[8,128,128]{2,1,0:T(8,128)S(1)}, u32[]{:S(2)}, u32[]{:S(2)}) %all-to-all-start.1) | async-done | bytes 524320 | tf_op jit(solution)/shard_map/all_to_all | solution.py:92
  143.8 1.7 broadcast_in_dim.4
  145.4 4.2 %all-to-all-start.2 = ((f32[8,128,128]{2,1,0:T(8,128)}), f32[8,128,128]{2,1,0:T(8,128)S(1)}, u32[]{:S(2)}, u32[]{:S(2)}) async-start(f32[8,128,128]{2,1,0:T(8,128)} %broadcast_in_dim.4), calls=%async_computation.2 | async-start | bytes 1048576 | tf_op jit(solution)/shard_map/all_to_all | solution.py:99
  152.9 5.7 %all-to-all-done.2 = f32[8,128,128]{2,1,0:T(8,128)S(1)} async-done(((f32[8,128,128]{2,1,0:T(8,128)}), f32[8,128,128]{2,1,0:T(8,128)S(1)}, u32[]{:S(2)}, u32[]{:S(2)}) %all-to-all-start.2) | async-done | bytes 524320 | tf_op jit(solution)/shard_map/all_to_all | solution.py:99
  158.5 5.6 %collective-permute-done.16.refs_14_.refs_6_ = f32[64,4096]{1,0:T(8,128)} collective-permute-done((f32[64,4096]{1,0:T(8,128)}, f32[64,4096]{1,0:T(8,128)}, u32[]{:S(2)}, u32[]{:S(2)}) %collective-permute-start.16) | collective-permute-done | bytes 1048608 | tf_op jit(solution)/shard_map/ppermute | solution.py:37
  164.9 1.5 fusion.15.t_ref
  166.4 1.5 solve.3.refs_1_
  167.9 4.3 %collective-permute-done.22 = f32[8,4096]{1,0:T(8,128)S(1)} collective-permute-done((f32[8,4096]{1,0:T(8,128)}, f32[8,4096]{1,0:T(8,128)S(1)}, u32[]{:S(2)}, u32[]{:S(2)}) %collective-permute-start.22) | collective-permute-done | bytes 131104 | tf_op jit(solution)/shard_map/ppermute | solution.py:37
  176.1 10.4 %work.5 = (f32[128,4096]{1,0:T(8,128)}, f32[1024,128]{1,0:T(8,128)S(1)}) custom-call(f32[32,128,128]{2,1,0:T(8,128)} %all-to-all-done.refs_0_, f32[128,512]{1,0:T(8,128)S(1)} %solve.3.refs_1_, f32[64,4096]{1,0:T(8,128)S(1)} %bitcast.147, f32[64,4096]{1,0:T(8,128)S(1)} %bitcast.150, f32[64,4096]{1,0:T(8,128)S(1)} %copy-done.1, ...), custom_call_target="tpu_custom_call" | custom-call | flops 3221225472 | bytes 20971520 | tf_op jit(solution)/shard_map/work/pallas_call | solution.py:202
  187.3 6.3 %all-to-all-start.3 = ((f32[8,128,128]{2,1,0:T(8,128)}), f32[8,128,128]{2,1,0:T(8,128)S(1)}, u32[]{:S(2)}, u32[]{:S(2)}) async-start(f32[8,128,128]{2,1,0:T(8,128)} %bitcast.153), calls=%async_computation.3 | async-start | bytes 1048576 | tf_op jit(solution)/shard_map/all_to_all | solution.py:92
  194.7 1.9 collective-permute-start.25
  196.6 1.6 collective-permute-start.26
  198.2 5.1 %all-to-all-done.3 = f32[8,128,128]{2,1,0:T(8,128)S(1)} async-done(((f32[8,128,128]{2,1,0:T(8,128)}), f32[8,128,128]{2,1,0:T(8,128)S(1)}, u32[]{:S(2)}, u32[]{:S(2)}) %all-to-all-start.3) | async-done | bytes 524320 | tf_op jit(solution)/shard_map/all_to_all | solution.py:92
  204.1 4.5 %all-to-all-start.4 = ((f32[8,128,128]{2,1,0:T(8,128)}), f32[8,128,128]{2,1,0:T(8,128)}, u32[]{:S(2)}, u32[]{:S(2)}) async-start(f32[8,128,128]{2,1,0:T(8,128)} %broadcast_in_dim.5), calls=%async_computation.4 | async-start | bytes 1048576 | tf_op jit(solution)/shard_map/all_to_all | solution.py:99
  209.1 1.9 collective-permute-done.26.refs_14_.refs_6_
  211.0 1.4 fusion.4
  213.7 4.6 %all-to-all-done.4 = f32[8,128,128]{2,1,0:T(8,128)} async-done(((f32[8,128,128]{2,1,0:T(8,128)}), f32[8,128,128]{2,1,0:T(8,128)}, u32[]{:S(2)}, u32[]{:S(2)}) %all-to-all-start.4) | async-done | bytes 524320 | tf_op jit(solution)/shard_map/all_to_all | solution.py:99
  219.4 2.5 %solve.4.refs_1_ = f32[128,512]{1,0:T(8,128)S(1)} custom-call(f32[2,256,256]{2,1,0:T(8,128)S(1)} %copy-done.2, f32[1024,128]{1,0:T(8,128)} %bitcast.79.w_ref), custom_call_target="tpu_custom_call" | custom-call | flops 201326592 | bytes 1048576 | tf_op jit(solution)/shard_map/solve/pallas_call | solution.py:231
  221.9 7.8 %work.6 = (f32[128,4096]{1,0:T(8,128)}, f32[256,128]{1,0:T(8,128)S(1)}) custom-call(f32[128,4096]{1,0:T(8,128)} %get-tuple-element.30.refs_0_, f32[128,512]{1,0:T(8,128)S(1)} %solve.4.refs_1_, f32[64,4096]{1,0:T(8,128)} %bitcast.66.refs_10_.refs_2_, f32[64,4096]{1,0:T(8,128)} %bitcast.77.refs_11_.refs_3_, ...), custom_call_target="tpu_custom_call" | custom-call | flops 2415919104 | bytes 16777216 | tf_op jit(solution)/shard_map/work/pallas_call | solution.py:202
  230.2 4.7 %collective-permute-done.30 = f32[256,128]{1,0:T(8,128)S(1)} collective-permute-done((f32[256,128]{1,0:T(8,128)S(1)}, f32[256,128]{1,0:T(8,128)S(1)}, u32[]{:S(2)}, u32[]{:S(2)}) %collective-permute-start.30) | collective-permute-done | bytes 131104 | tf_op jit(solution)/shard_map/ppermute | solution.py:29
  234.9 1.8 collective-permute-start.33
  236.7 1.5 collective-permute-start.32
  239.9 1.8 collective-permute-done.33
  241.7 2.3 collective-permute-done.32
  245.8 4.9 %work.7 = f32[4096,128]{1,0:T(8,128)} custom-call(f32[128,4096]{1,0:T(8,128)} %get-tuple-element.37.refs_0_, f32[128,256]{1,0:T(8,128)S(1)} %solve.5.refs_1_, f32[32,4096]{1,0:T(8,128)S(1)} %maximum_bitcast_fusion.refs_10_.refs_2_, f32[32,4096]{1,0:T(8,128)S(1)} %maximum_bitcast_fusion.1.refs_11_.refs_3_, ...), custom_call_target="tpu_custom_call" | custom-call | flops 805306368 | bytes 8388608 | tf_op jit(solution)/shard_map/work/pallas_call | solution.py:202
  (116 shorter events, 31.3 us)
Async XLA Ops:
  1.9 24.9 %copy-start.10 = (f32[128,4096]{1,0:T(8,128)S(1)}, f32[128,4096]{1,0:T(8,128)}, u32[]{:S(2)}) copy-start(f32[128,4096]{1,0:T(8,128)} %param.3) | copy-start | bytes 6291460
  2.0 1.6 collective-permute-start
  4.3 18.3 %collective-permute-start.1 = (f32[32,4096]{1,0:T(8,128)S(1)}, f32[32,4096]{1,0:T(8,128)S(1)}, u32[]{:S(2)}, u32[]{:S(2)}) collective-permute-start(f32[32,4096]{1,0:T(8,128)S(1)} %pad_maximum_fusion.6), channel_id=1, source_target_pairs={{0,8},{1,25},{8,16},{9,1},{16,24},{17,9},{24,0},{25,17},{2,10},{3,... | collective-permute-start | bytes 1572872 | tf_op jit(solution)/shard_map/ppermute | solution.py:37
  23.6 11.9 %collective-permute-start.2 = (f32[16,4096]{1,0:T(8,128)}, f32[16,4096]{1,0:T(8,128)}, u32[]{:S(2)}, u32[]{:S(2)}) collective-permute-start(f32[16,4096]{1,0:T(8,128)} %get-tuple-element.60), channel_id=1, source_target_pairs={{0,8},{1,25},{8,16},{9,1},{16,24},{17,9},{24,0},{25,17},{2,10},{3,... | collective-permute-start | bytes 786440 | tf_op jit(solution)/shard_map/ppermute | solution.py:37
  24.7 12.1 %collective-permute-start.9 = (f32[16,4096]{1,0:T(8,128)}, f32[16,4096]{1,0:T(8,128)}, u32[]{:S(2)}, u32[]{:S(2)}) collective-permute-start(f32[16,4096]{1,0:T(8,128)} %get-tuple-element.68), channel_id=1, source_target_pairs={{0,1},{1,0},{2,3},{3,2},{4,5},{5,4},{6,7},{7,6},{8,9},{9,8},{10,11... | collective-permute-start | bytes 786440 | tf_op jit(solution)/shard_map/ppermute | solution.py:29
  28.6 54.6 %all-to-all-start = ((f32[32,128,128]{2,1,0:T(8,128)}), f32[32,128,128]{2,1,0:T(8,128)}, u32[]{:S(2)}, u32[]{:S(2)}) async-start(f32[32,128,128]{2,1,0:T(8,128)} %bitcast.4), calls=%async_computation | async-start | bytes 4194304 | tf_op jit(solution)/shard_map/all_to_all | solution.py:87
  35.4 3.2 %copy-start.15 = (f32[2,1,8,4096]{3,2,1,0:T(8,128)S(1)}, f32[2,1,8,4096]{3,2,1,0:T(8,128)}, u32[]{:S(2)}) copy-start(f32[2,1,8,4096]{3,2,1,0:T(8,128)} %get-tuple-element.58) | copy-start | bytes 786436
  36.5 4.9 %collective-permute-start.3 = (f32[48,4096]{1,0:T(8,128)S(1)}, f32[48,4096]{1,0:T(8,128)S(1)}, u32[]{:S(2)}, u32[]{:S(2)}) collective-permute-start(f32[48,4096]{1,0:T(8,128)S(1)} %pad_maximum_fusion.4), channel_id=1, source_target_pairs={{0,1},{1,0},{2,3},{3,2},{4,5},{5,4},{6,7},{7,6},{8,9},{9,8},{10,11... | collective-permute-start | bytes 2359304 | tf_op jit(solution)/shard_map/ppermute | solution.py:29
  39.6 32.7 %collective-permute-start.4 = (f32[64,4096]{1,0:T(8,128)S(1)}, f32[64,4096]{1,0:T(8,128)S(1)}, u32[]{:S(2)}, u32[]{:S(2)}) collective-permute-start(f32[64,4096]{1,0:T(8,128)S(1)} %bitcast.145), channel_id=1, source_target_pairs={{0,2},{1,7},{2,4},{3,1},{4,6},{5,3},{6,0},{7,5},{8,10},{9,15},{10,... | collective-permute-start | bytes 3145736 | tf_op jit(solution)/shard_map/ppermute | solution.py:37
  41.5 39.7 %collective-permute-start.10 = (f32[32,4096]{1,0:T(8,128)}, f32[32,4096]{1,0:T(8,128)}, u32[]{:S(2)}, u32[]{:S(2)}) collective-permute-start(f32[32,4096]{1,0:T(8,128)} %pad_maximum_fusion.7), channel_id=1, source_target_pairs={{0,8},{1,25},{8,16},{9,1},{16,24},{17,9},{24,0},{25,17},{2,10},{3,... | collective-permute-start | bytes 1572872 | tf_op jit(solution)/shard_map/ppermute | solution.py:37
  44.0 70.2 %collective-permute-start.20 = (f32[8,4096]{1,0:T(8,128)}, f32[8,4096]{1,0:T(8,128)S(1)}, u32[]{:S(2)}, u32[]{:S(2)}) collective-permute-start(f32[8,4096]{1,0:T(8,128)} %get-tuple-element.50), channel_id=1, source_target_pairs={{0,1},{1,0},{2,3},{3,2},{4,5},{5,4},{6,7},{7,6},{8,9},{9,8},{10,11... | collective-permute-start | bytes 393224 | tf_op jit(solution)/shard_map/ppermute | solution.py:29
  46.4 39.3 %collective-permute-start.5 = (f32[64,4096]{1,0:T(8,128)S(1)}, f32[64,4096]{1,0:T(8,128)}, u32[]{:S(2)}, u32[]{:S(2)}) collective-permute-start(f32[64,4096]{1,0:T(8,128)S(1)} %bitcast.148), channel_id=1, source_target_pairs={{0,2},{1,7},{2,4},{3,1},{4,6},{5,3},{6,0},{7,5},{8,10},{9,15},{10,... | collective-permute-start | bytes 3145736 | tf_op jit(solution)/shard_map/ppermute | solution.py:37
  72.3 43.6 %copy-start = (f32[64,4096]{1,0:T(8,128)}, f32[64,4096]{1,0:T(8,128)S(1)}, u32[]{:S(2)}) copy-start(f32[64,4096]{1,0:T(8,128)S(1)} %collective-permute-done.4.refs_3_.refs_4_) | copy-start | bytes 3145732
  72.4 38.2 %collective-permute-start.6 = (f32[64,4096]{1,0:T(8,128)S(1)}, f32[64,4096]{1,0:T(8,128)}, u32[]{:S(2)}, u32[]{:S(2)}) collective-permute-start(f32[64,4096]{1,0:T(8,128)S(1)} %collective-permute-done.4.refs_3_.refs_4_), channel_id=1, source_target_pairs={{0,2},{1,7},{2,4},{3,1},{4,6},{5,3},{6,0},{7,5},{8,10},{9,15},{10,... | collective-permute-start | bytes 3145736 | tf_op jit(solution)/shard_map/ppermute | solution.py:37
  83.2 25.2 %collective-permute-start.11 = (f32[16,4096]{1,0:T(8,128)}, f32[16,4096]{1,0:T(8,128)}, u32[]{:S(2)}, u32[]{:S(2)}) collective-permute-start(f32[16,4096]{1,0:T(8,128)} %get-tuple-element.24), channel_id=1, source_target_pairs={{0,8},{1,25},{8,16},{9,1},{16,24},{17,9},{24,0},{25,17},{2,10},{3,... | collective-permute-start | bytes 786440 | tf_op jit(solution)/shard_map/ppermute | solution.py:37
  84.0 29.2 %copy-start.11 = (f32[5,256,256]{2,1,0:T(8,128)S(1)}, f32[5,256,256]{2,1,0:T(8,128)}, u32[]{:S(2)}) copy-start(f32[5,256,256]{2,1,0:T(8,128)} %param.5) | copy-start | bytes 3932164
  84.0 31.8 %collective-permute-start.7 = (f32[64,4096]{1,0:T(8,128)S(1)}, f32[64,4096]{1,0:T(8,128)S(1)}, u32[]{:S(2)}, u32[]{:S(2)}) collective-permute-start(f32[64,4096]{1,0:T(8,128)S(1)} %collective-permute-done.4.refs_3_.refs_4_), channel_id=1, source_target_pairs={{0,1},{1,0},{2,3},{3,2},{4,5},{5,4},{6,7},{7,6},{8,9},{9,8},{10,11... | collective-permute-start | bytes 3145736 | tf_op jit(solution)/shard_map/ppermute | solution.py:29
  85.7 30.2 %collective-permute-start.8 = (f32[64,4096]{1,0:T(8,128)}, f32[64,4096]{1,0:T(8,128)S(1)}, u32[]{:S(2)}, u32[]{:S(2)}) collective-permute-start(f32[64,4096]{1,0:T(8,128)} %collective-permute-done.5.refs_4_.refs_5_), channel_id=1, source_target_pairs={{0,1},{1,0},{2,3},{3,2},{4,5},{5,4},{6,7},{7,6},{8,9},{9,8},{10,11... | collective-permute-start | bytes 3145736 | tf_op jit(solution)/shard_map/ppermute | solution.py:29
  110.6 5.3 %collective-permute-start.12 = (f32[64,4096]{1,0:T(8,128)}, f32[64,4096]{1,0:T(8,128)S(1)}, u32[]{:S(2)}, u32[]{:S(2)}) collective-permute-start(f32[64,4096]{1,0:T(8,128)} %collective-permute-done.6.refs_5_.refs_6_), channel_id=1, source_target_pairs={{0,1},{1,0},{2,3},{3,2},{4,5},{5,4},{6,7},{7,6},{8,9},{9,8},{10,11... | collective-permute-start | bytes 3145736 | tf_op jit(solution)/shard_map/ppermute | solution.py:29
  112.7 20.6 %collective-permute-start.13 = (f32[48,4096]{1,0:T(8,128)}, f32[48,4096]{1,0:T(8,128)}, u32[]{:S(2)}, u32[]{:S(2)}) collective-permute-start(f32[48,4096]{1,0:T(8,128)} %pad_maximum_fusion.5), channel_id=1, source_target_pairs={{0,1},{1,0},{2,3},{3,2},{4,5},{5,4},{6,7},{7,6},{8,9},{9,8},{10,11... | collective-permute-start | bytes 2359304 | tf_op jit(solution)/shard_map/ppermute | solution.py:29
  115.8 35.1 %collective-permute-start.21 = (f32[16,4096]{1,0:T(8,128)}, f32[16,4096]{1,0:T(8,128)S(1)}, u32[]{:S(2)}, u32[]{:S(2)}) collective-permute-start(f32[16,4096]{1,0:T(8,128)} %pad_maximum_fusion.11), channel_id=1, source_target_pairs={{0,8},{1,25},{8,16},{9,1},{16,24},{17,9},{24,0},{25,17},{2,10},{3,... | collective-permute-start | bytes 786440 | tf_op jit(solution)/shard_map/ppermute | solution.py:37
  115.8 21.6 %collective-permute-start.14 = (f32[64,4096]{1,0:T(8,128)}, f32[64,4096]{1,0:T(8,128)}, u32[]{:S(2)}, u32[]{:S(2)}) collective-permute-start(f32[64,4096]{1,0:T(8,128)} %bitcast.66.refs_10_.refs_2_), channel_id=1, source_target_pairs={{0,2},{1,7},{2,4},{3,1},{4,6},{5,3},{6,0},{7,5},{8,10},{9,15},{10,... | collective-permute-start | bytes 3145736 | tf_op jit(solution)/shard_map/ppermute | solution.py:37
  125.5 17.6 %all-to-all-start.1 = ((f32[8,128,128]{2,1,0:T(8,128)}), f32[8,128,128]{2,1,0:T(8,128)S(1)}, u32[]{:S(2)}, u32[]{:S(2)}) async-start(f32[8,128,128]{2,1,0:T(8,128)} %bitcast.152), calls=%async_computation.1 | async-start | bytes 1048576 | tf_op jit(solution)/shard_map/all_to_all | solution.py:92
  134.4 15.3 %copy-start.13 = (f32[1,256,256]{2,1,0:T(8,128)S(1)}, f32[1,256,256]{2,1,0:T(8,128)}, u32[]{:S(2)}) copy-start(f32[1,256,256]{2,1,0:T(8,128)} %get-tuple-element.40) | copy-start | bytes 786436
  134.4 15.3 %copy-start.14 = (f32[1,256,256]{2,1,0:T(8,128)S(1)}, f32[1,256,256]{2,1,0:T(8,128)}, u32[]{:S(2)}) copy-start(f32[1,256,256]{2,1,0:T(8,128)} %get-tuple-element.41) | copy-start | bytes 786436
  134.4 15.3 %copy-start.19 = (s32[256]{0:T(256)S(1)}, s32[256]{0:T(256)}, u32[]{:S(2)}) copy-start(s32[256]{0:T(256)} %add.629) | copy-start | bytes 3076
  136.5 16.3 %collective-permute-start.15 = (f32[64,4096]{1,0:T(8,128)}, f32[64,4096]{1,0:T(8,128)}, u32[]{:S(2)}, u32[]{:S(2)}) collective-permute-start(f32[64,4096]{1,0:T(8,128)} %bitcast.77.refs_11_.refs_3_), channel_id=1, source_target_pairs={{0,2},{1,7},{2,4},{3,1},{4,6},{5,3},{6,0},{7,5},{8,10},{9,15},{10,... | collective-permute-start | bytes 3145736 | tf_op jit(solution)/shard_map/ppermute | solution.py:37
  137.4 26.6 %collective-permute-start.16 = (f32[64,4096]{1,0:T(8,128)}, f32[64,4096]{1,0:T(8,128)}, u32[]{:S(2)}, u32[]{:S(2)}) collective-permute-start(f32[64,4096]{1,0:T(8,128)} %collective-permute-done.14.refs_12_.refs_4_), channel_id=1, source_target_pairs={{0,2},{1,7},{2,4},{3,1},{4,6},{5,3},{6,0},{7,5},{8,10},{9,15},{10,... | collective-permute-start | bytes 3145736 | tf_op jit(solution)/shard_map/ppermute | solution.py:37
  145.4 13.1 %all-to-all-start.2 = ((f32[8,128,128]{2,1,0:T(8,128)}), f32[8,128,128]{2,1,0:T(8,128)S(1)}, u32[]{:S(2)}, u32[]{:S(2)}) async-start(f32[8,128,128]{2,1,0:T(8,128)} %broadcast_in_dim.4), calls=%async_computation.2 | async-start | bytes 1048576 | tf_op jit(solution)/shard_map/all_to_all | solution.py:99
  151.6 22.5 %collective-permute-start.17 = (f32[64,4096]{1,0:T(8,128)}, f32[64,4096]{1,0:T(8,128)}, u32[]{:S(2)}, u32[]{:S(2)}) collective-permute-start(f32[64,4096]{1,0:T(8,128)} %collective-permute-done.14.refs_12_.refs_4_), channel_id=1, source_target_pairs={{0,1},{1,0},{2,3},{3,2},{4,5},{5,4},{6,7},{7,6},{8,9},{9,8},{10,11... | collective-permute-start | bytes 3145736 | tf_op jit(solution)/shard_map/ppermute | solution.py:29
  158.5 15.5 %collective-permute-start.18 = (f32[64,4096]{1,0:T(8,128)}, f32[64,4096]{1,0:T(8,128)S(1)}, u32[]{:S(2)}, u32[]{:S(2)}) collective-permute-start(f32[64,4096]{1,0:T(8,128)} %collective-permute-done.15.refs_13_.refs_5_), channel_id=1, source_target_pairs={{0,1},{1,0},{2,3},{3,2},{4,5},{5,4},{6,7},{7,6},{8,9},{9,8},{10,11... | collective-permute-start | bytes 3145736 | tf_op jit(solution)/shard_map/ppermute | solution.py:29
  164.1 10.0 %collective-permute-start.19 = (f32[64,4096]{1,0:T(8,128)}, f32[64,4096]{1,0:T(8,128)S(1)}, u32[]{:S(2)}, u32[]{:S(2)}) collective-permute-start(f32[64,4096]{1,0:T(8,128)} %collective-permute-done.16.refs_14_.refs_6_), channel_id=1, source_target_pairs={{0,1},{1,0},{2,3},{3,2},{4,5},{5,4},{6,7},{7,6},{8,9},{9,8},{10,11... | collective-permute-start | bytes 3145736 | tf_op jit(solution)/shard_map/ppermute | solution.py:29
  164.1 12.0 %copy-start.1 = (f32[64,4096]{1,0:T(8,128)S(1)}, f32[64,4096]{1,0:T(8,128)}, u32[]{:S(2)}) copy-start(f32[64,4096]{1,0:T(8,128)} %copy-done) | copy-start | bytes 3145732
  164.1 8.1 %collective-permute-start.22 = (f32[8,4096]{1,0:T(8,128)}, f32[8,4096]{1,0:T(8,128)S(1)}, u32[]{:S(2)}, u32[]{:S(2)}) collective-permute-start(f32[8,4096]{1,0:T(8,128)} %get-tuple-element.33), channel_id=1, source_target_pairs={{0,8},{1,25},{8,16},{9,1},{16,24},{17,9},{24,0},{25,17},{2,10},{3,... | collective-permute-start | bytes 393224 | tf_op jit(solution)/shard_map/ppermute | solution.py:37
  173.0 20.5 %collective-permute-start.23 = (f32[24,4096]{1,0:T(8,128)}, f32[24,4096]{1,0:T(8,128)}, u32[]{:S(2)}, u32[]{:S(2)}) collective-permute-start(f32[24,4096]{1,0:T(8,128)} %pad_maximum_fusion.8), channel_id=1, source_target_pairs={{0,1},{1,0},{2,3},{3,2},{4,5},{5,4},{6,7},{7,6},{8,9},{9,8},{10,11... | collective-permute-start | bytes 1179656 | tf_op jit(solution)/shard_map/ppermute | solution.py:29
  174.0 22.7 %collective-permute-start.24 = (f32[32,4096]{1,0:T(8,128)S(1)}, f32[32,4096]{1,0:T(8,128)S(1)}, u32[]{:S(2)}, u32[]{:S(2)}) collective-permute-start(f32[32,4096]{1,0:T(8,128)S(1)} %maximum_bitcast_fusion.refs_10_.refs_2_), channel_id=1, source_target_pairs={{0,2},{1,7},{2,4},{3,1},{4,6},{5,3},{6,0},{7,5},{8,10},{9,15},{10,... | collective-permute-start | bytes 1572872 | tf_op jit(solution)/shard_map/ppermute | solution.py:37
  187.3 15.9 %all-to-all-start.3 = ((f32[8,128,128]{2,1,0:T(8,128)}), f32[8,128,128]{2,1,0:T(8,128)S(1)}, u32[]{:S(2)}, u32[]{:S(2)}) async-start(f32[8,128,128]{2,1,0:T(8,128)} %bitcast.153), calls=%async_computation.3 | async-start | bytes 1048576 | tf_op jit(solution)/shard_map/all_to_all | solution.py:92
  193.6 17.5 %copy-start.12 = (f32[1,256,256]{2,1,0:T(8,128)S(1)}, f32[1,256,256]{2,1,0:T(8,128)}, u32[]{:S(2)}) copy-start(f32[1,256,256]{2,1,0:T(8,128)} %get-tuple-element.39) | copy-start | bytes 786436
  194.7 14.1 %collective-permute-start.25 = (f32[32,4096]{1,0:T(8,128)S(1)}, f32[32,4096]{1,0:T(8,128)S(1)}, u32[]{:S(2)}, u32[]{:S(2)}) collective-permute-start(f32[32,4096]{1,0:T(8,128)S(1)} %maximum_bitcast_fusion.1.refs_11_.refs_3_), channel_id=1, source_target_pairs={{0,2},{1,7},{2,4},{3,1},{4,6},{5,3},{6,0},{7,5},{8,10},{9,15},{10,... | collective-permute-start | bytes 1572872 | tf_op jit(solution)/shard_map/ppermute | solution.py:37
  196.6 14.4 %collective-permute-start.26 = (f32[32,4096]{1,0:T(8,128)S(1)}, f32[32,4096]{1,0:T(8,128)S(1)}, u32[]{:S(2)}, u32[]{:S(2)}) collective-permute-start(f32[32,4096]{1,0:T(8,128)S(1)} %collective-permute-done.24.refs_12_.refs_4_), channel_id=1, source_target_pairs={{0,2},{1,7},{2,4},{3,1},{4,6},{5,3},{6,0},{7,5},{8,10},{9,15},{10,... | collective-permute-start | bytes 1572872 | tf_op jit(solution)/shard_map/ppermute | solution.py:37
  204.1 14.2 %all-to-all-start.4 = ((f32[8,128,128]{2,1,0:T(8,128)}), f32[8,128,128]{2,1,0:T(8,128)}, u32[]{:S(2)}, u32[]{:S(2)}) async-start(f32[8,128,128]{2,1,0:T(8,128)} %broadcast_in_dim.5), calls=%async_computation.4 | async-start | bytes 1048576 | tf_op jit(solution)/shard_map/all_to_all | solution.py:99
  208.6 13.3 %collective-permute-start.27 = (f32[32,4096]{1,0:T(8,128)S(1)}, f32[32,4096]{1,0:T(8,128)S(1)}, u32[]{:S(2)}, u32[]{:S(2)}) collective-permute-start(f32[32,4096]{1,0:T(8,128)S(1)} %collective-permute-done.24.refs_12_.refs_4_), channel_id=1, source_target_pairs={{0,1},{1,0},{2,3},{3,2},{4,5},{5,4},{6,7},{7,6},{8,9},{9,8},{10,11... | collective-permute-start | bytes 1572872 | tf_op jit(solution)/shard_map/ppermute | solution.py:29
  208.8 13.1 %collective-permute-start.28 = (f32[32,4096]{1,0:T(8,128)S(1)}, f32[32,4096]{1,0:T(8,128)}, u32[]{:S(2)}, u32[]{:S(2)}) collective-permute-start(f32[32,4096]{1,0:T(8,128)S(1)} %collective-permute-done.25.refs_13_.refs_5_), channel_id=1, source_target_pairs={{0,1},{1,0},{2,3},{3,2},{4,5},{5,4},{6,7},{7,6},{8,9},{9,8},{10,11... | collective-permute-start | bytes 1572872 | tf_op jit(solution)/shard_map/ppermute | solution.py:29
  211.0 10.9 %collective-permute-start.29 = (f32[32,4096]{1,0:T(8,128)S(1)}, f32[32,4096]{1,0:T(8,128)}, u32[]{:S(2)}, u32[]{:S(2)}) collective-permute-start(f32[32,4096]{1,0:T(8,128)S(1)} %collective-permute-done.26.refs_14_.refs_6_), channel_id=1, source_target_pairs={{0,1},{1,0},{2,3},{3,2},{4,5},{5,4},{6,7},{7,6},{8,9},{9,8},{10,11... | collective-permute-start | bytes 1572872 | tf_op jit(solution)/shard_map/ppermute | solution.py:29
  229.7 5.2 %collective-permute-start.30 = (f32[256,128]{1,0:T(8,128)S(1)}, f32[256,128]{1,0:T(8,128)S(1)}, u32[]{:S(2)}, u32[]{:S(2)}) collective-permute-start(f32[256,128]{1,0:T(8,128)S(1)} %get-tuple-element.38), channel_id=1, source_target_pairs={{0,128},{128,0},{1,129},{129,1},{2,130},{130,2},{3,131},{131,3},{4... | collective-permute-start | bytes 393224 | tf_op jit(solution)/shard_map/ppermute | solution.py:29
  234.9 6.8 %collective-permute-start.33 = (f32[256,128]{1,0:T(8,128)S(1)}, f32[256,128]{1,0:T(8,128)S(1)}, u32[]{:S(2)}, u32[]{:S(2)}) collective-permute-start(f32[256,128]{1,0:T(8,128)S(1)} %add.630), channel_id=1, source_target_pairs={{0,96},{32,0},{64,32},{96,64},{1,97},{33,1},{65,33},{97,65},{2,98}... | collective-permute-start | bytes 393224 | tf_op jit(solution)/shard_map/ppermute | solution.py:29
  236.7 7.3 %collective-permute-start.32 = (f32[256,128]{1,0:T(8,128)S(1)}, f32[256,128]{1,0:T(8,128)S(1)}, u32[]{:S(2)}, u32[]{:S(2)}) collective-permute-start(f32[256,128]{1,0:T(8,128)S(1)} %add.630), channel_id=1, source_target_pairs={{0,64},{32,96},{64,0},{96,32},{1,65},{33,97},{65,1},{97,33},{2,66}... | collective-permute-start | bytes 393224 | tf_op jit(solution)/shard_map/ppermute | solution.py:29
  238.2 7.2 %collective-permute-start.31 = (f32[256,128]{1,0:T(8,128)S(1)}, f32[256,128]{1,0:T(8,128)S(1)}, u32[]{:S(2)}, u32[]{:S(2)}) collective-permute-start(f32[256,128]{1,0:T(8,128)S(1)} %add.630), channel_id=1, source_target_pairs={{0,32},{32,64},{64,96},{96,0},{1,33},{33,65},{65,97},{97,1},{2,34}... | collective-permute-start | bytes 393224 | tf_op jit(solution)/shard_map/ppermute | solution.py:29
  (11 other events, 14.6 us)
